TPU v7x, 32 devices: a whole 2x2x4 slice. The times are simulated.
32 devices in a mesh: cell: 8 (over y, x, core), blk: 4 (over z).
Axes of the slice: x: 2, y: 2, z: 4, core: 2. Of those that a mesh axis runs over, the one named last changes fastest.
Arguments:
- snapshots: float32 [128, 16384], P('blk', 'cell'), may hold values from -100 to 100
- plan: int32 [31, 32], replicated, may hold values from 0 to 31, as said below
Outputs:
- energy_field: float32 [128, 16384], P('blk', 'cell')
- mode_energy: float32 [128], P('blk')
Inputs may be any that keep to these rules, and one draw needn't show every extreme that they name: `plan`: each row pairs every index 0 .. 31 with exactly one other index (the partner's partner is the index itself, never the index), and over all rows every two indices are paired exactly once.
All inputs are finite; a program needn't handle non-finite values.
Results may differ from a plain program's by a relative error of at most 0.0055.
Values sent between devices are 32-bit elements; how exact they have to be, the bound alone decides.
No kernel may reach another device: no remote copies, remote signals or barrier semaphores. Data moves between devices by JAX's collectives and lax.ppermute only.
A program may use at most 64 MiB of HBM per device.

v0:
```python
import jax
import jax.numpy as jnp
from jax import lax
from jax.sharding import PartitionSpec as P

ROUNDS = 7


def passed_along(value, axis, steps):
    count = lax.axis_size(axis)
    first, last = (max(0, -steps), min(count, count - steps))
    return lax.ppermute(value, axis, [(source, source + steps) for source in range(first, last)])


def inner_sweep(gram_whole, plan):
    pair_width = gram_whole.shape[0]
    positions = jnp.arange(pair_width, dtype=jnp.int32)

    def one_step(step_index, loop_state):
        gram_now, accumulated = loop_state
        partner = lax.dynamic_index_in_dim(plan, step_index, 0, keepdims=False)
        onehot = (partner[:, None] == positions[None, :]).astype(jnp.float32)
        symmetric = 0.5 * (gram_now + gram_now.T)
        own_diag = jnp.diagonal(symmetric)
        cross_term = jnp.sum(onehot * symmetric, axis=1)
        other_diag = jnp.sum(onehot * own_diag[None, :], axis=1)
        is_lower = positions < partner
        spread = jnp.where(is_lower, own_diag - other_diag, other_diag - own_diag)
        angles = 0.5 * jnp.arctan2(2.0 * cross_term, spread)
        cosine = jnp.cos(angles)
        sine_part = jnp.where(is_lower, jnp.sin(angles), -jnp.sin(angles))
        rotation_step = jnp.diag(cosine) + (onehot * sine_part[:, None]).T
        gram_now = jnp.dot(
            jnp.dot(rotation_step.T, gram_now, precision=lax.Precision.HIGHEST),
            rotation_step,
            precision=lax.Precision.HIGHEST,
        )
        accumulated = jnp.dot(accumulated, rotation_step, precision=lax.Precision.HIGHEST)
        return (gram_now, accumulated)

    initial = (gram_whole, jnp.eye(pair_width, dtype=jnp.float32))
    return lax.fori_loop(0, pair_width - 1, one_step, initial)[1]


def self_gram(block):
    return jnp.dot(block, block.T, precision=lax.Precision.HIGHEST)


def on_device(snapshots, plan):
    pair_width = snapshots.shape[0]
    half_width = pair_width // 2
    local_rows = snapshots.shape[1]
    block_devices = lax.axis_size("blk")
    position = lax.axis_index("blk")

    def round_step(round_index, loop_state):
        current, gram_local = loop_state
        gram_whole = lax.psum(gram_local, "cell")
        turning = inner_sweep(gram_whole, plan)
        rotated = jnp.dot(turning.T, current, precision=lax.Precision.HIGHEST)
        upper_part = rotated[:half_width]
        lower_part = rotated[half_width:]
        rightward = jnp.where(position == 0, lower_part, upper_part)
        from_left = passed_along(rightward, "blk", 1)
        from_right = passed_along(lower_part, "blk", -1)
        new_upper = jnp.where(position == 0, upper_part, from_left)
        new_lower = jnp.where(position == block_devices - 1, upper_part, from_right)
        current = jnp.concatenate([new_upper, new_lower], axis=0)
        gram_local = self_gram(current)
        return (current, gram_local)

    gram_first = self_gram(snapshots)
    current, gram_local = lax.fori_loop(0, ROUNDS, round_step, (snapshots, gram_first))
    squared = current * current
    energy_local = jnp.sum(squared, axis=1)
    total_rows = local_rows * lax.axis_size("cell")
    mode_energy = lax.psum(energy_local, "cell") / total_rows
    return (squared, mode_energy)


def solution(mesh):
    return jax.shard_map(
        on_device,
        mesh=mesh,
        in_specs=(P("blk", "cell"), P()),
        out_specs=(P("blk", "cell"), P("blk")),
        check_vma=False,
    )
```

profile of v0, /device:TPU:0, one launch (start us, length us, event | category | flops | bytes accessed | tf_op | source)
XLA Modules:
  0.0 1115.6 jit_solution(7370657845704556550)
XLA Ops:
  0.6 1.0 copy.29
  1.9 1100.5 %while.37 = (s32[]{:T(128)}, f32[32,2048]{1,0:T(8,128)S(1)}, f32[32,32]{1,0:T(8,128)S(1)}, pred[]{:T(512)}, s32[31,32]{1,0:T(8,128)}, /*index=5*/pred[]{:T(512)}, s32[]{:T(128)}, s32[]{:T(128)}, s32[]{:T(128)}) while((s32[]{:T(128)}, f32[32,2048]{1,0:T(8,128)S(1)}, f32[32,32]{1,0:T(8,128)S(1)}, pred[]{:T(512)}, s32[31,32]{1,0:T(8,128)}, ...), condition=%wide.region_6.7_spmd, body=%wide.region_0.6_spmd.sunk | while | flops 51701092 | bytes 3620785 | solution.py:73
  2.0 25.5 %psum.18 = f32[32,32]{1,0:T(8,128)S(1)} all-reduce(f32[32,32]{1,0:T(8,128)S(1)} %get-tuple-element.345), channel_id=1, replica_groups=mesh['cell'=8,'blk'=4] {'cell'}, use_global_device_ids=true, to_apply=%region_1.0 | all-reduce | flops 1024 | bytes 8192 | tf_op jit(solution)/shard_map/while/body/eval_jaxpr/psum | solution.py:58
  27.5 124.2 %while.38 = (s32[]{:T(128)}, f32[32,32]{1,0:T(8,128)S(1)}, f32[32,32]{0,1:T(8,128)S(1)}, s32[31,32]{1,0:T(8,128)}, s32[]{:T(128)}) while((s32[]{:T(128)}, f32[32,32]{1,0:T(8,128)S(1)}, f32[32,32]{0,1:T(8,128)S(1)}, s32[31,32]{1,0:T(8,128)}, s32[]{:T(128)}) %tuple.77), condition=%wide.region_5.5_spmd.clone.clone, body=%wide.region_2.4_spmd.clone.clone.sunk | while | flops 1202530 | bytes 61137 | solution.py:42
  33.2 0.8 fusion.70
  41.2 0.8 fusion.70
  152.0 3.5 collective-permute-start
  155.5 1.3 collective-permute-start.1
  156.8 1.2 collective-permute-done
  158.0 4.4 collective-permute-done.1
  162.8 22.3 %psum.18 = f32[32,32]{1,0:T(8,128)S(1)} all-reduce(f32[32,32]{1,0:T(8,128)S(1)} %get-tuple-element.345), channel_id=1, replica_groups=mesh['cell'=8,'blk'=4] {'cell'}, use_global_device_ids=true, to_apply=%region_1.0 | all-reduce | flops 1024 | bytes 8192 | tf_op jit(solution)/shard_map/while/body/eval_jaxpr/psum | solution.py:58
  185.1 124.2 %while.38 = (s32[]{:T(128)}, f32[32,32]{1,0:T(8,128)S(1)}, f32[32,32]{0,1:T(8,128)S(1)}, s32[31,32]{1,0:T(8,128)}, s32[]{:T(128)}) while((s32[]{:T(128)}, f32[32,32]{1,0:T(8,128)S(1)}, f32[32,32]{0,1:T(8,128)S(1)}, s32[31,32]{1,0:T(8,128)}, s32[]{:T(128)}) %tuple.77), condition=%wide.region_5.5_spmd.clone.clone, body=%wide.region_2.4_spmd.clone.clone.sunk | while | flops 1202530 | bytes 61137 | solution.py:42
  309.7 3.5 collective-permute-start
  313.2 1.3 collective-permute-start.1
  314.5 1.2 collective-permute-done
  315.7 4.4 collective-permute-done.1
  320.5 22.3 %psum.18 = f32[32,32]{1,0:T(8,128)S(1)} all-reduce(f32[32,32]{1,0:T(8,128)S(1)} %get-tuple-element.345), channel_id=1, replica_groups=mesh['cell'=8,'blk'=4] {'cell'}, use_global_device_ids=true, to_apply=%region_1.0 | all-reduce | flops 1024 | bytes 8192 | tf_op jit(solution)/shard_map/while/body/eval_jaxpr/psum | solution.py:58
  342.8 124.2 %while.38 = (s32[]{:T(128)}, f32[32,32]{1,0:T(8,128)S(1)}, f32[32,32]{0,1:T(8,128)S(1)}, s32[31,32]{1,0:T(8,128)}, s32[]{:T(128)}) while((s32[]{:T(128)}, f32[32,32]{1,0:T(8,128)S(1)}, f32[32,32]{0,1:T(8,128)S(1)}, s32[31,32]{1,0:T(8,128)}, s32[]{:T(128)}) %tuple.77), condition=%wide.region_5.5_spmd.clone.clone, body=%wide.region_2.4_spmd.clone.clone.sunk | while | flops 1202530 | bytes 61137 | solution.py:42
  467.3 3.5 collective-permute-start
  470.8 1.3 collective-permute-start.1
  472.1 1.2 collective-permute-done
  473.3 4.4 collective-permute-done.1
  478.1 22.3 %psum.18 = f32[32,32]{1,0:T(8,128)S(1)} all-reduce(f32[32,32]{1,0:T(8,128)S(1)} %get-tuple-element.345), channel_id=1, replica_groups=mesh['cell'=8,'blk'=4] {'cell'}, use_global_device_ids=true, to_apply=%region_1.0 | all-reduce | flops 1024 | bytes 8192 | tf_op jit(solution)/shard_map/while/body/eval_jaxpr/psum | solution.py:58
  500.5 124.2 %while.38 = (s32[]{:T(128)}, f32[32,32]{1,0:T(8,128)S(1)}, f32[32,32]{0,1:T(8,128)S(1)}, s32[31,32]{1,0:T(8,128)}, s32[]{:T(128)}) while((s32[]{:T(128)}, f32[32,32]{1,0:T(8,128)S(1)}, f32[32,32]{0,1:T(8,128)S(1)}, s32[31,32]{1,0:T(8,128)}, s32[]{:T(128)}) %tuple.77), condition=%wide.region_5.5_spmd.clone.clone, body=%wide.region_2.4_spmd.clone.clone.sunk | while | flops 1202530 | bytes 61137 | solution.py:42
  625.0 1.9 collective-permute-start
  626.9 1.3 collective-permute-start.1
  628.2 1.2 collective-permute-done
  629.4 4.4 collective-permute-done.1
  634.2 22.3 %psum.18 = f32[32,32]{1,0:T(8,128)S(1)} all-reduce(f32[32,32]{1,0:T(8,128)S(1)} %get-tuple-element.345), channel_id=1, replica_groups=mesh['cell'=8,'blk'=4] {'cell'}, use_global_device_ids=true, to_apply=%region_1.0 | all-reduce | flops 1024 | bytes 8192 | tf_op jit(solution)/shard_map/while/body/eval_jaxpr/psum | solution.py:58
  656.5 124.2 %while.38 = (s32[]{:T(128)}, f32[32,32]{1,0:T(8,128)S(1)}, f32[32,32]{0,1:T(8,128)S(1)}, s32[31,32]{1,0:T(8,128)}, s32[]{:T(128)}) while((s32[]{:T(128)}, f32[32,32]{1,0:T(8,128)S(1)}, f32[32,32]{0,1:T(8,128)S(1)}, s32[31,32]{1,0:T(8,128)}, s32[]{:T(128)}) %tuple.77), condition=%wide.region_5.5_spmd.clone.clone, body=%wide.region_2.4_spmd.clone.clone.sunk | while | flops 1202530 | bytes 61137 | solution.py:42
  781.1 1.9 collective-permute-start
  783.0 1.3 collective-permute-start.1
  784.3 1.2 collective-permute-done
  785.5 4.4 collective-permute-done.1
  790.3 22.3 %psum.18 = f32[32,32]{1,0:T(8,128)S(1)} all-reduce(f32[32,32]{1,0:T(8,128)S(1)} %get-tuple-element.345), channel_id=1, replica_groups=mesh['cell'=8,'blk'=4] {'cell'}, use_global_device_ids=true, to_apply=%region_1.0 | all-reduce | flops 1024 | bytes 8192 | tf_op jit(solution)/shard_map/while/body/eval_jaxpr/psum | solution.py:58
  812.6 124.2 %while.38 = (s32[]{:T(128)}, f32[32,32]{1,0:T(8,128)S(1)}, f32[32,32]{0,1:T(8,128)S(1)}, s32[31,32]{1,0:T(8,128)}, s32[]{:T(128)}) while((s32[]{:T(128)}, f32[32,32]{1,0:T(8,128)S(1)}, f32[32,32]{0,1:T(8,128)S(1)}, s32[31,32]{1,0:T(8,128)}, s32[]{:T(128)}) %tuple.77), condition=%wide.region_5.5_spmd.clone.clone, body=%wide.region_2.4_spmd.clone.clone.sunk | while | flops 1202530 | bytes 61137 | solution.py:42
  937.2 1.9 collective-permute-start
  939.1 1.3 collective-permute-start.1
  940.4 1.2 collective-permute-done
  941.6 4.4 collective-permute-done.1
  946.4 22.3 %psum.18 = f32[32,32]{1,0:T(8,128)S(1)} all-reduce(f32[32,32]{1,0:T(8,128)S(1)} %get-tuple-element.345), channel_id=1, replica_groups=mesh['cell'=8,'blk'=4] {'cell'}, use_global_device_ids=true, to_apply=%region_1.0 | all-reduce | flops 1024 | bytes 8192 | tf_op jit(solution)/shard_map/while/body/eval_jaxpr/psum | solution.py:58
  968.7 124.2 %while.38 = (s32[]{:T(128)}, f32[32,32]{1,0:T(8,128)S(1)}, f32[32,32]{0,1:T(8,128)S(1)}, s32[31,32]{1,0:T(8,128)}, s32[]{:T(128)}) while((s32[]{:T(128)}, f32[32,32]{1,0:T(8,128)S(1)}, f32[32,32]{0,1:T(8,128)S(1)}, s32[31,32]{1,0:T(8,128)}, s32[]{:T(128)}) %tuple.77), condition=%wide.region_5.5_spmd.clone.clone, body=%wide.region_2.4_spmd.clone.clone.sunk | while | flops 1202530 | bytes 61137 | solution.py:42
  1093.3 1.9 collective-permute-start
  1095.2 1.3 collective-permute-start.1
  1096.5 1.2 collective-permute-done
  1097.7 4.4 collective-permute-done.1
  1102.5 0.8 fusion.30
  1103.3 11.8 %psum.16 = f32[32]{0:T(128)S(1)} all-reduce(f32[32]{0:T(128)S(1)} %get-tuple-element.224), channel_id=1, replica_groups=mesh['cell'=8,'blk'=4] {'cell'}, use_global_device_ids=true, to_apply=%region_8.9 | all-reduce | flops 32 | bytes 256 | tf_op jit(solution)/shard_map/psum | solution.py:77
  (2646 shorter events, 862.0 us)
Async XLA Ops:
  152.0 6.0 collective-permute-start
  155.5 6.9 collective-permute-start.1
  309.7 6.0 collective-permute-start
  313.2 6.9 collective-permute-start.1
  467.3 6.0 collective-permute-start
  470.8 6.9 collective-permute-start.1
  625.0 4.4 collective-permute-start
  626.9 6.9 collective-permute-start.1
  781.1 4.4 collective-permute-start
  783.0 6.9 collective-permute-start.1
  937.2 4.4 collective-permute-start
  939.1 6.9 collective-permute-start.1
  1093.3 4.4 collective-permute-start
  1095.2 6.9 collective-permute-start.1
where the time goes:
time: 1140 us; the launch traced here: 1120 us
  other arithmetic  370 us (32%)
  local copies, waits for them, and re-layouts  324 us (28%)
  matrix products  171 us (15%)
  blocking collectives  171 us (15%)
  waiting for transfers between devices  38.9 us (3%)
  starting transfers between devices  27.2 us (2%)
  loops' own time  12.4 us (1%)
    cos x217, other arithmetic, one_step(): cosine = jnp.cos(angles)  167 us
    psum x7, blocking collectives, round_step(): gram_whole = lax.psum(gram_local, 'cell')  159 us
    select_n x217, other arithmetic, one_step(): sine_part = jnp.where(is_lower, jnp.sin(angles), -jnp.sin(angles))  159 us
    gather x217, local copies, waits for them, and re-layouts, one_step(): own_diag = jnp.diagonal(symmetric)  156 us
    eq x217, local copies, waits for them, and re-layouts, one_step(): onehot = (partner[:, None] == positions[None, :]).astype(jnp.float32)  151 us
    dot_general x217, matrix products, one_step(): jnp.dot(accumulated, rotation_step, precision=lax.Precision.HIGHEST)  60.8 us
    dot_general x217, matrix products, one_step(): jnp.dot(rotation_step.T, gram_now, precision=lax.Precision.HIGHEST)  60.1 us
    dot_general x217, matrix products, one_step(): jnp.dot(jnp.dot(rotation_step.T, gram_now, precision=lax.Precision.HIGHES...  44.7 us
  transfers between devices with their start and end apart: 14, of which 14 were waited for; matrix products, arithmetic and copies ran while one was open for 0% of the time, Pallas kernels for 0%

commit v1 on v0

v1 whole, which is shorter than its diff:
```python
import functools

import jax
import jax.numpy as jnp
from jax import lax
from jax.experimental import pallas as pl
from jax.experimental.pallas import tpu as pltpu
from jax.sharding import PartitionSpec as P

ROUNDS = 7
TINY_SQUARE = 2.0**-78
UP = 2.0**80
FLOOR = 2.0**-124
FLOOR_ROOT = 2.0**-62
LANES = 128


def split3(x):
    high = x.astype(jnp.bfloat16)
    rest = x - high.astype(jnp.float32)
    middle = rest.astype(jnp.bfloat16)
    low = (rest - middle.astype(jnp.float32)).astype(jnp.bfloat16)
    return high, middle, low


def dot_full(a, b, contract_a=1, contract_b=0):
    a0, a1, a2 = split3(a)
    b0, b1, b2 = split3(b)

    def one(x, y):
        return lax.dot_general(
            x, y, (((contract_a,), (contract_b,)), ((), ())), preferred_element_type=jnp.float32
        )

    small = one(a0, b2) + one(a2, b0) + one(a1, b1)
    return one(a0, b0) + ((one(a0, b1) + one(a1, b0)) + small)


def half_angle(twice_cross, spread, sign):
    up_cross, up_spread = twice_cross * UP, spread * UP
    square = spread * spread + twice_cross * twice_cross
    up_square = up_spread * up_spread + up_cross * up_cross
    is_small = square < TINY_SQUARE
    norm_square = jnp.maximum(jnp.where(is_small, up_square, square), FLOOR)
    size = jnp.maximum(jnp.abs(jnp.where(is_small, up_spread, spread)), FLOOR_ROOT)
    half_cross = jnp.where(is_small, up_cross, twice_cross) * (0.5 * sign)
    cross_sign = jnp.where(twice_cross < 0, -sign, sign)
    inverse = lax.rsqrt(norm_square)
    large_square = 0.5 * (size * inverse) + 0.5
    root = lax.rsqrt(large_square)
    large = large_square * root
    small = (half_cross * inverse) * root
    in_order = spread >= 0
    cosine = jnp.where(in_order, large, jnp.abs(small))
    sine = jnp.where(in_order, small, cross_sign * large)
    return cosine, sine


def gather(x, index):
    return jnp.take_along_axis(x, jnp.broadcast_to(index, x.shape), axis=1)


def tall(x, like):
    return jnp.concatenate([x] * (like.shape[0] // x.shape[0]), axis=0)


def turned_by(c, s, x, y):
    return tall(c, x) * x + tall(s, x) * y


def both(wx, tx, wy, ty):
    return jnp.sum(wx * ty + wy * tx, axis=0, keepdims=True)


def new_diagonal(cosine, sine, twice_cross, own, other):
    return (cosine * cosine) * own + (cosine * sine) * twice_cross + (sine * sine) * other


def single_step(state, index, signs):
    w, t, d = state
    p = index[0:1]
    wp, tp, dp = gather(w, p), gather(t, p), gather(d, p)
    sign = signs[0:1]
    cross = both(w, t, wp, tp)
    c, s = half_angle(cross, (d - dp) * sign, sign)
    return turned_by(c, s, w, wp), turned_by(c, s, t, tp), new_diagonal(c, s, cross, d, dp)


def double_step(state, index, signs):
    w, t, d = state
    p, q, pq = index[0:1], index[1:2], index[2:3]
    sign, sign_q, sign_next = signs[0:1], signs[1:2], signs[2:3]
    wp, tp, dp = gather(w, p), gather(t, p), gather(d, p)
    wq, tq, dq = gather(w, q), gather(t, q), gather(d, q)
    wpq, tpq, dpq = gather(w, pq), gather(t, pq), gather(d, pq)
    cross = both(w, t, wp, tp)
    cross_q = both(wq, tq, wpq, tpq)
    e00, e01 = both(w, t, wq, tq), both(w, t, wpq, tpq)
    e10, e11 = both(wp, tp, wq, tq), both(wp, tp, wpq, tpq)
    c, s = half_angle(cross, (d - dp) * sign, sign)
    cq, sq = half_angle(cross_q, (dq - dpq) * sign_q, sign_q)
    cross_next = ((c * cq) * e00 + (s * sq) * e11) + ((c * sq) * e01 + (s * cq) * e10)
    d1 = new_diagonal(c, s, cross, d, dp)
    d1q = new_diagonal(cq, sq, cross_q, dq, dpq)
    c1, s1 = half_angle(cross_next, (d1 - d1q) * sign_next, sign_next)
    w1, t1 = turned_by(c, s, w, wp), turned_by(c, s, t, tp)
    w1q, t1q = turned_by(cq, sq, wq, wpq), turned_by(cq, sq, tq, tpq)
    return (
        turned_by(c1, s1, w1, w1q),
        turned_by(c1, s1, t1, t1q),
        new_diagonal(c1, s1, cross_next, d1, d1q),
    )


def turn_kernel(n_steps, gram_ref, index_ref, sign_ref, modes_ref, energy_ref, c_ref):
    cols = gram_ref.shape[0]
    pair = 32
    half = pair // 2
    tiles = cols // LANES
    lane = lax.broadcasted_iota(jnp.int32, (pair, cols), 1)
    row = lax.broadcasted_iota(jnp.int32, (pair, cols), 0)
    is_diag = row == lane % pair
    start = is_diag.astype(jnp.float32)
    own_pair = lax.broadcasted_iota(jnp.int32, (cols, cols), 0) // pair == (
        lax.broadcasted_iota(jnp.int32, (cols, cols), 1) // pair
    )
    c_ref[...] = gram_ref[...]
    modes_ref[...] = (
        lax.broadcasted_iota(jnp.int32, (cols, cols), 0) == lax.broadcasted_iota(jnp.int32, (cols, cols), 1)
    ).astype(jnp.float32)

    def moved(x):
        place = lax.broadcasted_iota(jnp.int32, x.shape, 1)
        is_upper = place % pair < half
        from_own = (place < half) & is_upper
        shifted = ((place // pair == 1) & is_upper) | (place >= cols - half)
        right, left, by_half = pltpu.roll(x, pair, 1), pltpu.roll(x, cols - pair, 1), pltpu.roll(x, half, 1)
        return jnp.where(from_own, x, jnp.where(shifted, by_half, jnp.where(is_upper, right, left)))

    def one_round(round_index, carry):
        kept = jnp.where(own_pair, c_ref[...], 0.0)
        w = kept[0:pair]
        for p in range(1, cols // pair):
            w = w + kept[p * pair : (p + 1) * pair]
        d = jnp.broadcast_to(jnp.sum(jnp.where(is_diag, w, 0.0), axis=0, keepdims=True), (8, cols))
        turned, energies = [], []
        for tile in range(tiles):
            at = slice(tile * LANES, (tile + 1) * LANES)
            state = (w[:, at], start[:, at], d[:, at])

            def steps(k, state):
                return double_step(state, index_ref[k], sign_ref[k])

            state = lax.fori_loop(0, n_steps // 2, steps, state)
            if n_steps % 2:
                state = single_step(state, index_ref[n_steps // 2], sign_ref[n_steps // 2])
            turned.append(state[1])
            energies.append(state[2])
        t = moved(jnp.concatenate(turned, axis=1) if tiles > 1 else turned[0])
        d = jnp.concatenate(energies, axis=1) if tiles > 1 else energies[0]
        energy_ref[...] = moved(d)
        lanes_from = moved(lax.broadcasted_iota(jnp.int32, (8, cols), 1))[0:1] // pair
        rows_pair = lax.broadcasted_iota(jnp.int32, (cols, cols), 0) // pair
        whole = jnp.where(rows_pair == lanes_from, jnp.concatenate([t] * (cols // pair), axis=0), 0.0)
        half_way = dot_full(c_ref[...], whole)
        c_ref[...] = dot_full(whole, half_way, 0, 0)
        modes_ref[...] = dot_full(modes_ref[...], whole)
        return carry

    lax.fori_loop(0, ROUNDS, one_round, 0)


def turn_all(gram, plan):
    cols = gram.shape[0]
    n_steps, pair = plan.shape
    pairs = (n_steps + 1) // 2
    here = jnp.arange(pair, dtype=jnp.int32)
    first = plan[0::2]
    second = jnp.concatenate([plan[1::2], here[None]], axis=0)[:pairs]
    first_of_second = jnp.take_along_axis(first, second, axis=1)
    index = jnp.stack([first, second, first_of_second], axis=1)
    index = jnp.concatenate([index + 32 * g for g in range(LANES // 32)], axis=2)

    def sign_of(own, other):
        return jnp.where(own < other, 1.0, -1.0).astype(jnp.float32)

    signs = jnp.stack(
        [sign_of(here[None], first), sign_of(second, first_of_second), sign_of(here[None], second)], axis=1
    )
    signs = jnp.concatenate([signs] * (LANES // 32), axis=2)
    return pl.pallas_call(
        functools.partial(turn_kernel, n_steps),
        out_shape=(
            jax.ShapeDtypeStruct((cols, cols), jnp.float32),
            jax.ShapeDtypeStruct((8, cols), jnp.float32),
        ),
        in_specs=[pl.BlockSpec(memory_space=pltpu.VMEM)] * 3,
        out_specs=[pl.BlockSpec(memory_space=pltpu.VMEM)] * 2,
        scratch_shapes=[pltpu.VMEM((cols, cols), jnp.float32)],
        compiler_params=pltpu.CompilerParams(vmem_limit_bytes=48 * 1024 * 1024),
    )(gram, index, signs)


def summed_over_all(x):
    n = lax.axis_size("cell") * lax.axis_size("blk")
    rows, cols = x.shape
    pieces = lax.all_to_all(x.reshape(n, rows // n, cols), ("cell", "blk"), 0, 0)
    total = jnp.sum(pieces, axis=0)
    return lax.all_to_all(
        jnp.broadcast_to(total[None], (n,) + total.shape), ("cell", "blk"), 0, 0
    ).reshape(rows, cols)


def on_device(snapshots, plan):
    pair, cells = snapshots.shape
    n_blk = lax.axis_size("blk")
    cols = pair * n_blk
    part = lax.all_to_all(snapshots.reshape(pair, n_blk, cells // n_blk), "blk", 1, 0)
    part = part.reshape(cols, cells // n_blk)
    gathered = lax.all_gather(snapshots, "blk", axis=0, tiled=True)
    gram = summed_over_all(
        lax.dot_general(part, part, (((1,), (1,)), ((), ())), precision=lax.Precision.HIGHEST)
    )
    modes, energy = turn_all(gram, plan)
    place = lax.axis_index("blk") * pair
    own = lax.dynamic_slice_in_dim(modes, place, pair, 1)
    rotated = lax.dot_general(own, gathered, (((0,), (0,)), ((), ())), precision=lax.Precision.HIGHEST)
    mode_energy = lax.dynamic_slice_in_dim(energy[0], place, pair, 0) / (cells * lax.axis_size("cell"))
    return rotated * rotated, mode_energy


def solution(mesh):
    return jax.shard_map(
        on_device,
        mesh=mesh,
        in_specs=(P("blk", "cell"), P()),
        out_specs=(P("blk", "cell"), P("blk")),
        check_vma=False,
    )
```

time: 1140 us -> 87.7 us (0.08); the launches traced: 1120 us -> 87.3 us
  other arithmetic: 370 us -> 1.1 us
  local copies, waits for them, and re-layouts: 324 us -> 6.52 us
  blocking collectives: 171 us -> 0 us
  matrix products: 171 us -> 3 us
  Pallas kernels: 0 us -> 24.1 us
  waiting for transfers between devices: 38.9 us -> 23.1 us
  between operations: 0.65 us -> 14.2 us
  loops' own time: 12.4 us -> 0 us
  starting transfers between devices: 27.2 us -> 15.3 us
    psum x8 -> x0, blocking collectives: 171 us -> none  [the longest x7 159 us: round_step(): gram_whole = lax.psum(gram_local, 'cell')]
    dot_general x666 -> x2, matrix products: 171 us -> 3 us  [the longest x1 2.59 us: on_device(): lax.dot_general(own, gathered, (((0,), (0,)), ((), ())), precision=lax.Pr...]
    cos x217 -> x0, other arithmetic: 167 us -> none  [one_step(): cosine = jnp.cos(angles)]
    select_n x231 -> x3, other arithmetic: 160 us -> 0.04 us  [sign_of(): return jnp.where(own < other, 1.0, -1.0).astype(jnp.float32)]
    gather x217 -> x3, local copies, waits for them, and re-layouts: 156 us -> 3.92 us  [turn_all(): first_of_second = jnp.take_along_axis(first, second, axis=1)]
    eq x217 -> x0, local copies, waits for them, and re-layouts: 151 us -> none  [one_step(): onehot = (partner[:, None] == positions[None, :]).astype(jnp.float32)]
    reduce_sum x218 -> x1, other arithmetic: 39.8 us -> 0.04 us  [summed_over_all(): total = jnp.sum(pieces, axis=0)]
    ppermute x14 -> x0, waiting for transfers between devices: 38.9 us -> none  [passed_along(): lax.ppermute(value, axis, [(source, source + steps) for source in range(f...]
  transfers between devices with their start and end apart: 14 -> 4, of which waited for: 14 -> 3; matrix products, arithmetic and copies ran while one was open for 0% -> 9% of each run, Pallas kernels for 0% -> 28%
where the time goes in v1:
time: 87.7 us; the launch traced here: 87.3 us
  Pallas kernels  24.1 us (27%)
  waiting for transfers between devices  23.1 us (26%)
  starting transfers between devices  15.3 us (17%)
  between operations  14.2 us (16%)
  local copies, waits for them, and re-layouts  6.52 us (7%)
  matrix products  3 us (3%)
  other arithmetic  1.1 us (1%)
    pallas_call x1, Pallas kernels, turn_all(): pl.pallas_call(functools.partial(turn_kernel, n_steps), out_shape=(jax.Sh...  24.1 us
    all_to_all x1, waiting for transfers between devices, summed_over_all(): lax.all_to_all(x.reshape(n, rows // n, cols), ('cell', 'blk'), 0, 0)  8.52 us
    all_to_all x1, waiting for transfers between devices, summed_over_all(): lax.all_to_all(jnp.broadcast_to(total[None], (n,) + total.shape), ('cell'...  7.14 us
    all_to_all x1, waiting for transfers between devices, on_device(): lax.all_to_all(snapshots.reshape(pair, n_blk, cells // n_blk), 'blk', 1, 0)  6.74 us
    all_to_all x1, starting transfers between devices, on_device(): lax.all_to_all(snapshots.reshape(pair, n_blk, cells // n_blk), 'blk', 1, 0)  6.45 us
    all_to_all x1, starting transfers between devices, summed_over_all(): lax.all_to_all(x.reshape(n, rows // n, cols), ('cell', 'blk'), 0, 0)  6.23 us
    gather x3, local copies, waits for them, and re-layouts, turn_all(): first_of_second = jnp.take_along_axis(first, second, axis=1)  3.92 us
    dot_general x1, matrix products, on_device(): lax.dot_general(own, gathered, (((0,), (0,)), ((), ())), precision=lax.Pr...  2.59 us
  transfers between devices with their start and end apart: 4, of which 3 were waited for; matrix products, arithmetic and copies ran while one was open for 9% of the time, Pallas kernels for 28%

profile of v1, /device:TPU:0, one launch (start us, length us, event | category | flops | bytes accessed | tf_op | source)
XLA Modules:
  0.0 87.3 jit_solution(14733869981349614584)
XLA Ops:
  7.2 0.0 copy-start
  7.2 0.0 all-gather.2.cloned.1.call-start
  7.2 0.7 all-gather.2.cloned.1.call-update
  7.9 0.2 copy-done
  8.1 0.2 broadcast_in_dim_reshape.3
  8.3 0.8 copy.21
  9.1 0.0 copy-start.1
  9.1 6.4 %all-to-all-start = ((f32[1,32,4,512]{3,1,0,2:T(8,128)}), f32[1,32,4,512]{3,1,0,2:T(8,128)S(1)}, u32[]{:S(2)}, u32[]{:S(2)}) async-start(f32[1,32,4,512]{3,1,0,2:T(8,128)} %copy.21), calls=%async_computation | async-start | bytes 524288 | tf_op jit(solution)/shard_map/all_to_all | solution.py:218
  15.5 0.0 copy-done.1
  15.6 0.1 reshape.256
  15.7 3.8 %gather_fusion = s32[512]{0:T(512)S(1)} fusion(s32[16,32]{1,0:T(8,128)S(1)} %slice.9, s32[512]{0:T(512)S(1)} %reshape.256), kind=kCustom, calls=%fused_computation | custom fusion | bytes 8192 | tf_op jit(solution)/shard_map/jit(take_along_axis)/gather | solution.py:180
  19.4 0.1 gather.7
  19.6 6.7 %all-to-all-done = f32[1,32,4,512]{3,1,0,2:T(8,128)S(1)} async-done(((f32[1,32,4,512]{3,1,0,2:T(8,128)}), f32[1,32,4,512]{3,1,0,2:T(8,128)S(1)}, u32[]{:S(2)}, u32[]{:S(2)}) %all-to-all-start) | async-done | bytes 262176 | tf_op jit(solution)/shard_map/all_to_all | solution.py:218
  26.3 0.1 dot_general.8
  26.4 0.4 fusion
  26.8 0.7 copy.23
  27.5 6.2 %all-to-all-start.1 = ((f32[32,4,128]{2,1,0:T(4,128)}), f32[32,4,128]{2,1,0:T(4,128)S(1)}, u32[]{:S(2)}, u32[]{:S(2)}) async-start(f32[32,4,128]{2,1,0:T(4,128)} %copy.23), calls=%async_computation.1 | async-start | bytes 131072 | tf_op jit(solution)/shard_map/all_to_all | solution.py:207
  33.8 8.5 %all-to-all-done.1 = f32[32,4,128]{2,1,0:T(4,128)S(1)} async-done(((f32[32,4,128]{2,1,0:T(4,128)}), f32[32,4,128]{2,1,0:T(4,128)S(1)}, u32[]{:S(2)}, u32[]{:S(2)}) %all-to-all-start.1) | async-done | bytes 65568 | tf_op jit(solution)/shard_map/all_to_all | solution.py:207
  42.4 0.6 broadcast_in_dim.29
  43.0 2.6 %all-to-all-start.2 = ((f32[32,4,128]{2,1,0:T(4,128)}), f32[32,4,128]{2,1,0:T(4,128)S(1)}, u32[]{:S(2)}, u32[]{:S(2)}) async-start(f32[32,4,128]{2,1,0:T(4,128)} %broadcast_in_dim.29), calls=%async_computation.2 | async-start | bytes 131072 | tf_op jit(solution)/shard_map/all_to_all | solution.py:209
  45.6 0.1 pad_add_fusion.1.index_ref
  45.8 0.2 maximum_maximum_fusion.sign_ref
  46.0 7.1 %all-to-all-done.2 = f32[32,4,128]{2,1,0:T(4,128)S(1)} async-done(((f32[32,4,128]{2,1,0:T(4,128)}), f32[32,4,128]{2,1,0:T(4,128)S(1)}, u32[]{:S(2)}, u32[]{:S(2)}) %all-to-all-start.2) | async-done | bytes 65568 | tf_op jit(solution)/shard_map/all_to_all | solution.py:209
  53.1 24.1 %shard_map.41 = (f32[128,128]{1,0:T(8,128)S(1)}, f32[8,128]{1,0:T(8,128)S(1)}) custom-call(f32[128,128]{1,0:T(8,128)S(1)} %bitcast.26, s32[16,3,128]{2,1,0:T(4,128)S(1)} %pad_add_fusion.1.index_ref, f32[16,3,128]{2,1,0:T(4,128)S(1)} %maximum_maximum_fusion.sign_ref), custom_call_target="tpu_custom_call" | custom-call | tf_op jit(solution)/shard_map/pallas_call | solution.py:191
  77.3 0.6 multiply_bitcast_fusion
  77.8 0.0 all-gather.2.cloned.1.call-done
  77.8 2.6 %convolution_multiply_fusion = f32[32,2048]{1,0:T(8,128)} fusion(f32[128,2048]{1,0:T(8,128)} %all-gather.2.cloned.1.call-done, f32[128,128]{1,0:T(8,128)S(1)} %get-tuple-element.4, s32[]{:T(128)S(6)} %select_n.75), kind=kOutput, calls=%fused_computation.1 | convolution fusion | flops 100728832 | bytes 1376260 | tf_op jit(solution)/shard_map/dot_general | solution.py:227
  (15 shorter events, 0.2 us)
Async XLA Ops:
  7.2 1.0 %copy-start = (f32[32,2048]{1,0:T(8,128)S(1)}, f32[32,2048]{1,0:T(8,128)}, u32[]{:S(2)}) copy-start(f32[32,2048]{1,0:T(8,128)} %param.2) | copy-start | bytes 786436
  7.2 70.7 %all-gather.2.cloned.1.call-start = ((), (), s32[]{:S(2)}) async-start(), calls=%async_computation.3 | async-start | bytes 1310720 | tf_op jit(solution)/shard_map/all_gather | solution.py:220
  9.1 6.5 %copy-start.1 = (s32[31,32]{1,0:T(8,128)S(1)}, s32[31,32]{1,0:T(8,128)}, u32[]{:S(2)}) copy-start(s32[31,32]{1,0:T(8,128)} %param.3) | copy-start | bytes 11908
  9.1 17.3 %all-to-all-start = ((f32[1,32,4,512]{3,1,0,2:T(8,128)}), f32[1,32,4,512]{3,1,0,2:T(8,128)S(1)}, u32[]{:S(2)}, u32[]{:S(2)}) async-start(f32[1,32,4,512]{3,1,0,2:T(8,128)} %copy.21), calls=%async_computation | async-start | bytes 524288 | tf_op jit(solution)/shard_map/all_to_all | solution.py:218
  27.5 14.8 %all-to-all-start.1 = ((f32[32,4,128]{2,1,0:T(4,128)}), f32[32,4,128]{2,1,0:T(4,128)S(1)}, u32[]{:S(2)}, u32[]{:S(2)}) async-start(f32[32,4,128]{2,1,0:T(4,128)} %copy.23), calls=%async_computation.1 | async-start | bytes 131072 | tf_op jit(solution)/shard_map/all_to_all | solution.py:207
  43.0 10.1 %all-to-all-start.2 = ((f32[32,4,128]{2,1,0:T(4,128)}), f32[32,4,128]{2,1,0:T(4,128)S(1)}, u32[]{:S(2)}, u32[]{:S(2)}) async-start(f32[32,4,128]{2,1,0:T(4,128)} %broadcast_in_dim.29), calls=%async_computation.2 | async-start | bytes 131072 | tf_op jit(solution)/shard_map/all_to_all | solution.py:209
Sparse Core Ops, SparseCore 0:
  9.6 33.4 all-gather.1

commit v2 on v1

--- a/solution.py
+++ b/solution.py
@@ -78,9 +78,9 @@
 
 def single_step(state, index, signs):
     w, t, d = state
-    p = index[0:1]
+    (p,) = index
     wp, tp, dp = gather(w, p), gather(t, p), gather(d, p)
-    sign = signs[0:1]
+    (sign,) = signs
     cross = both(w, t, wp, tp)
     c, s = half_angle(cross, (d - dp) * sign, sign)
     return turned_by(c, s, w, wp), turned_by(c, s, t, tp), new_diagonal(c, s, cross, d, dp)
@@ -88,8 +88,8 @@
 
 def double_step(state, index, signs):
     w, t, d = state
-    p, q, pq = index[0:1], index[1:2], index[2:3]
-    sign, sign_q, sign_next = signs[0:1], signs[1:2], signs[2:3]
+    p, q, pq = index
+    sign, sign_q, sign_next = signs
     wp, tp, dp = gather(w, p), gather(t, p), gather(d, p)
     wq, tq, dq = gather(w, q), gather(t, q), gather(d, q)
     wpq, tpq, dpq = gather(w, pq), gather(t, pq), gather(d, pq)
@@ -112,22 +112,34 @@
     )
 
 
-def turn_kernel(n_steps, gram_ref, index_ref, sign_ref, modes_ref, energy_ref, c_ref):
+def turn_kernel(n_steps, gram_ref, plan_ref, place_ref, modes_ref, energy_ref, c_ref, q_ref, index_ref, sign_ref):
     cols = gram_ref.shape[0]
-    pair = 32
+    pair = plan_ref.shape[1]
     half = pair // 2
     tiles = cols // LANES
     lane = lax.broadcasted_iota(jnp.int32, (pair, cols), 1)
     row = lax.broadcasted_iota(jnp.int32, (pair, cols), 0)
     is_diag = row == lane % pair
     start = is_diag.astype(jnp.float32)
-    own_pair = lax.broadcasted_iota(jnp.int32, (cols, cols), 0) // pair == (
-        lax.broadcasted_iota(jnp.int32, (cols, cols), 1) // pair
-    )
+    square_row = lax.broadcasted_iota(jnp.int32, (cols, cols), 0)
+    square_lane = lax.broadcasted_iota(jnp.int32, (cols, cols), 1)
+    own_pair = square_row // pair == square_lane // pair
     c_ref[...] = gram_ref[...]
-    modes_ref[...] = (
-        lax.broadcasted_iota(jnp.int32, (cols, cols), 0) == lax.broadcasted_iota(jnp.int32, (cols, cols), 1)
-    ).astype(jnp.float32)
+    q_ref[...] = (square_row == square_lane).astype(jnp.float32)
+
+    own_lane = lax.broadcasted_iota(jnp.int32, (pair, LANES), 1)
+    table = plan_ref[...]
+    table = jnp.concatenate([table + pair * g for g in range(LANES // pair)], axis=1)
+    following = pltpu.roll(table, pair - 1, 0)
+    partner_of_following = jnp.take_along_axis(table, following, axis=1)
+
+    def sign_of(own, other):
+        return jnp.where(own < other, 1.0, -1.0).astype(jnp.float32)
+
+    index_ref[0:pair] = table
+    index_ref[pair : 2 * pair] = partner_of_following
+    sign_ref[0:pair] = sign_of(own_lane, table)
+    sign_ref[pair : 2 * pair] = sign_of(following, partner_of_following)
 
     def moved(x):
         place = lax.broadcasted_iota(jnp.int32, x.shape, 1)
@@ -136,6 +148,9 @@
         shifted = ((place // pair == 1) & is_upper) | (place >= cols - half)
         right, left, by_half = pltpu.roll(x, pair, 1), pltpu.roll(x, cols - pair, 1), pltpu.roll(x, half, 1)
         return jnp.where(from_own, x, jnp.where(shifted, by_half, jnp.where(is_upper, right, left)))
+
+    def rows_of(ref, *places):
+        return [ref[pl.ds(p, 1), :] for p in places]
 
     def one_round(round_index, carry):
         kept = jnp.where(own_pair, c_ref[...], 0.0)
@@ -149,83 +164,121 @@
             state = (w[:, at], start[:, at], d[:, at])
 
             def steps(k, state):
-                return double_step(state, index_ref[k], sign_ref[k])
+                first = 2 * k
+                index = rows_of(index_ref, first, first + 1, first + pair)
+                signs = rows_of(sign_ref, first, first + pair, first + 1)
+                return double_step(state, index, signs)
 
             state = lax.fori_loop(0, n_steps // 2, steps, state)
             if n_steps % 2:
-                state = single_step(state, index_ref[n_steps // 2], sign_ref[n_steps // 2])
+                state = single_step(state, rows_of(index_ref, n_steps - 1), rows_of(sign_ref, n_steps - 1))
             turned.append(state[1])
             energies.append(state[2])
         t = moved(jnp.concatenate(turned, axis=1) if tiles > 1 else turned[0])
         d = jnp.concatenate(energies, axis=1) if tiles > 1 else energies[0]
         energy_ref[...] = moved(d)
         lanes_from = moved(lax.broadcasted_iota(jnp.int32, (8, cols), 1))[0:1] // pair
-        rows_pair = lax.broadcasted_iota(jnp.int32, (cols, cols), 0) // pair
-        whole = jnp.where(rows_pair == lanes_from, jnp.concatenate([t] * (cols // pair), axis=0), 0.0)
+        whole = jnp.where(square_row // pair == lanes_from, jnp.concatenate([t] * (cols // pair), axis=0), 0.0)
         half_way = dot_full(c_ref[...], whole)
         c_ref[...] = dot_full(whole, half_way, 0, 0)
-        modes_ref[...] = dot_full(modes_ref[...], whole)
+        q_ref[...] = dot_full(q_ref[...], whole)
         return carry
 
     lax.fori_loop(0, ROUNDS, one_round, 0)
-
-
-def turn_all(gram, plan):
+    place = place_ref[0]
+    to_front = lax.rem(cols - place * pair, cols)
+    energy_ref[...] = pltpu.roll(energy_ref[...], to_front, 1)
+    for d in range(cols // pair):
+        rows = q_ref[pl.ds(pl.multiple_of((place ^ d) * pair, pair), pair), :]
+        modes_ref[d * pair : (d + 1) * pair] = pltpu.roll(rows, to_front, 1)
+
+
+def in_vmem(n):
+    return [pl.BlockSpec(memory_space=pltpu.VMEM)] * n
+
+
+def turn_all(gram, plan, place):
     cols = gram.shape[0]
     n_steps, pair = plan.shape
-    pairs = (n_steps + 1) // 2
-    here = jnp.arange(pair, dtype=jnp.int32)
-    first = plan[0::2]
-    second = jnp.concatenate([plan[1::2], here[None]], axis=0)[:pairs]
-    first_of_second = jnp.take_along_axis(first, second, axis=1)
-    index = jnp.stack([first, second, first_of_second], axis=1)
-    index = jnp.concatenate([index + 32 * g for g in range(LANES // 32)], axis=2)
-
-    def sign_of(own, other):
-        return jnp.where(own < other, 1.0, -1.0).astype(jnp.float32)
-
-    signs = jnp.stack(
-        [sign_of(here[None], first), sign_of(second, first_of_second), sign_of(here[None], second)], axis=1
-    )
-    signs = jnp.concatenate([signs] * (LANES // 32), axis=2)
+    plan = jnp.concatenate([plan, jnp.arange(pair, dtype=jnp.int32)[None]], axis=0)
     return pl.pallas_call(
         functools.partial(turn_kernel, n_steps),
         out_shape=(
             jax.ShapeDtypeStruct((cols, cols), jnp.float32),
             jax.ShapeDtypeStruct((8, cols), jnp.float32),
         ),
-        in_specs=[pl.BlockSpec(memory_space=pltpu.VMEM)] * 3,
-        out_specs=[pl.BlockSpec(memory_space=pltpu.VMEM)] * 2,
-        scratch_shapes=[pltpu.VMEM((cols, cols), jnp.float32)],
+        in_specs=in_vmem(2) + [pl.BlockSpec(memory_space=pltpu.SMEM)],
+        out_specs=in_vmem(2),
+        scratch_shapes=[
+            pltpu.VMEM((cols, cols), jnp.float32),
+            pltpu.VMEM((cols, cols), jnp.float32),
+            pltpu.VMEM((2 * pair, LANES), jnp.int32),
+            pltpu.VMEM((2 * pair, LANES), jnp.float32),
+        ],
         compiler_params=pltpu.CompilerParams(vmem_limit_bytes=48 * 1024 * 1024),
-    )(gram, index, signs)
+        name="all_rounds",
+    )(gram, plan, place)
+
+
+def gram_kernel(place_ref, *refs):
+    blocks, gram_ref, whole_ref = refs[:-2], refs[-2], refs[-1]
+    pair = blocks[0].shape[0]
+    for d, block in enumerate(blocks):
+        whole_ref[pl.ds(pl.multiple_of((place_ref[0] ^ d) * pair, pair), pair), :] = block[...]
+    whole = whole_ref[...]
+    gram_ref[...] = dot_full(whole, whole, 1, 1)
+
+
+def gram_of(blocks, place):
+    pair, cells = blocks[0].shape
+    cols = pair * len(blocks)
+    return pl.pallas_call(
+        gram_kernel,
+        out_shape=jax.ShapeDtypeStruct((cols, cols), jnp.float32),
+        in_specs=[pl.BlockSpec(memory_space=pltpu.SMEM)] + in_vmem(len(blocks)),
+        out_specs=pl.BlockSpec(memory_space=pltpu.VMEM),
+        scratch_shapes=[pltpu.VMEM((cols, cells), jnp.float32)],
+        name="gram_of_part",
+    )(place, *blocks)
+
+
+def sent(value, axis, toggle):
+    return lax.ppermute(value, axis, [(i, i ^ toggle) for i in range(lax.axis_size(axis))])
+
+
+def tree_sum(values):
+    while len(values) > 1:
+        values = [a + b for a, b in zip(values[::2], values[1::2])]
+    return values[0]
 
 
 def summed_over_all(x):
-    n = lax.axis_size("cell") * lax.axis_size("blk")
-    rows, cols = x.shape
-    pieces = lax.all_to_all(x.reshape(n, rows // n, cols), ("cell", "blk"), 0, 0)
-    total = jnp.sum(pieces, axis=0)
-    return lax.all_to_all(
-        jnp.broadcast_to(total[None], (n,) + total.shape), ("cell", "blk"), 0, 0
-    ).reshape(rows, cols)
+    x = x + sent(x, "cell", 1)
+    x = tree_sum([x] + [sent(x, "cell", d) for d in range(2, lax.axis_size("cell"), 2)])
+    return tree_sum([x] + [sent(x, "blk", d) for d in range(1, lax.axis_size("blk"))])
 
 
 def on_device(snapshots, plan):
     pair, cells = snapshots.shape
     n_blk = lax.axis_size("blk")
-    cols = pair * n_blk
-    part = lax.all_to_all(snapshots.reshape(pair, n_blk, cells // n_blk), "blk", 1, 0)
-    part = part.reshape(cols, cells // n_blk)
-    gathered = lax.all_gather(snapshots, "blk", axis=0, tiled=True)
-    gram = summed_over_all(
-        lax.dot_general(part, part, (((1,), (1,)), ((), ())), precision=lax.Precision.HIGHEST)
+    here = lax.axis_index("blk")
+    place = here.astype(jnp.int32)[None]
+    part = cells // n_blk
+
+    def part_for(d):
+        return lax.dynamic_slice_in_dim(snapshots, (here ^ d) * part, part, 1)
+
+    parts = [part_for(0)] + [sent(part_for(d), "blk", d) for d in range(1, n_blk)]
+    blocks = [snapshots] + [sent(snapshots, "blk", d) for d in range(1, n_blk)]
+    gram = summed_over_all(gram_of(parts, place))
+    modes, energy = turn_all(gram, plan, place)
+    rotated = lax.dot_general(
+        modes[:, :pair],
+        jnp.concatenate(blocks, axis=0),
+        (((0,), (0,)), ((), ())),
+        precision=lax.Precision.HIGHEST,
     )
-    modes, energy = turn_all(gram, plan)
-    place = lax.axis_index("blk") * pair
-    own = lax.dynamic_slice_in_dim(modes, place, pair, 1)
-    rotated = lax.dot_general(own, gathered, (((0,), (0,)), ((), ())), precision=lax.Precision.HIGHEST)
-    mode_energy = lax.dynamic_slice_in_dim(energy[0], place, pair, 0) / (cells * lax.axis_size("cell"))
+    mode_energy = energy[0, :pair] / (cells * lax.axis_size("cell"))
     return rotated * rotated, mode_energy
 
 

time: 87.7 us -> 73.9 us (0.84)
  between operations: 14.2 us -> 0.7 us
  local copies, waits for them, and re-layouts: 6.52 us -> 2.26 us
  starting transfers between devices: 15.3 us -> 18.8 us
  Pallas kernels: 24.1 us -> 26.3 us
  matrix products: 3 us -> 1.36 us
    ppermute x0 -> x13, waiting for transfers between devices: none -> 22.8 us  [sent(): lax.ppermute(value, axis, [(i, i ^ toggle) for i in range(lax.axis_size(a...]
    all_to_all x3 -> x0, waiting for transfers between devices: 22.4 us -> none  [the longest x1 8.52 us: summed_over_all(): lax.all_to_all(x.reshape(n, rows // n, cols), ('cell', 'blk'), 0, 0)]
    ppermute x0 -> x13, starting transfers between devices: none -> 18.8 us  [sent(): lax.ppermute(value, axis, [(i, i ^ toggle) for i in range(lax.axis_size(a...]
    all_to_all x3 -> x0, starting transfers between devices: 15.3 us -> none  [the longest x1 6.45 us: on_device(): lax.all_to_all(snapshots.reshape(pair, n_blk, cells // n_blk), 'blk', 1, 0)]
    gather x3 -> x0, local copies, waits for them, and re-layouts: 3.92 us -> none  [turn_all(): first_of_second = jnp.take_along_axis(first, second, axis=1)]
    pallas_call x0 -> x1, Pallas kernels: none -> 1.99 us  [gram_of(): pl.pallas_call(gram_kernel, out_shape=jax.ShapeDtypeStruct((cols, cols),...]
    dot_general x2 -> x1, matrix products: 3 us -> 1.36 us  [on_device(): lax.dot_general(modes[:, :pair], jnp.concatenate(blocks, axis=0), (((0,),...]
    dynamic_slice x0 -> x1, local copies, waits for them, and re-layouts: none -> 1.59 us  [part_for(): return lax.dynamic_slice_in_dim(snapshots, (here ^ d) * part, part, 1)]
  transfers between devices with their start and end apart: 4 -> 13, of which waited for: 3 -> 6; matrix products, arithmetic and copies ran while one was open for 9% -> 1% of each run, Pallas kernels for 28% -> 33%
where the time goes in v2:
time: 73.9 us; the launch traced here: 73.7 us
  Pallas kernels  26.3 us (36%)
  waiting for transfers between devices  22.8 us (31%)
  starting transfers between devices  18.8 us (25%)
  local copies, waits for them, and re-layouts  2.26 us (3%)
  other arithmetic  1.42 us (2%)
  matrix products  1.36 us (2%)
    pallas_call x1, Pallas kernels, turn_all(): pl.pallas_call(functools.partial(turn_kernel, n_steps), out_shape=(jax.Sh...  24.3 us
    ppermute x13, waiting for transfers between devices, sent(): lax.ppermute(value, axis, [(i, i ^ toggle) for i in range(lax.axis_size(a...  22.8 us
    ppermute x13, starting transfers between devices, sent(): lax.ppermute(value, axis, [(i, i ^ toggle) for i in range(lax.axis_size(a...  18.8 us
    pallas_call x1, Pallas kernels, gram_of(): pl.pallas_call(gram_kernel, out_shape=jax.ShapeDtypeStruct((cols, cols),...  1.99 us
    dynamic_slice x1, local copies, waits for them, and re-layouts, part_for(): return lax.dynamic_slice_in_dim(snapshots, (here ^ d) * part, part, 1)  1.59 us
  transfers between devices with their start and end apart: 13, of which 6 were waited for; matrix products, arithmetic and copies ran while one was open for 1% of the time, Pallas kernels for 33%

profile of v2, /device:TPU:0, one launch (start us, length us, event | category | flops | bytes accessed | tf_op | source)
XLA Modules:
  0.0 73.7 jit_solution(4220656478185394614)
XLA Ops:
  0.6 1.6 %constant_dynamic-slice_fusion = (f32[32,512]{1,0:T(8,128)S(1)}, f32[32,512]{1,0:T(8,128)S(1)}, f32[32,512]{1,0:T(8,128)S(1)}, f32[32,512]{1,0:T(8,128)}) fusion(f32[32,2048]{1,0:T(8,128)} %param.2, s32[]{:T(128)S(6)} %select_n.15, s32[]{:T(128)S(6)} %select_n.14, s32[]{:T(128)S(6)} %select_n.13, s32[]{:T(128)S(6)} %select_n.12), kind=kLoop, calls=%fused_computation.12 | loop fusion | bytes 524304 | tf_op jit(solution)/shard_map/dynamic_slice | solution.py:269
  2.2 5.0 %collective-permute-start.2 = (f32[32,512]{1,0:T(8,128)S(1)}, f32[32,512]{1,0:T(8,128)S(1)}, u32[]{:S(2)}, u32[]{:S(2)}) collective-permute-start(f32[32,512]{1,0:T(8,128)S(1)} %get-tuple-element.6), channel_id=1, source_target_pairs={{0,3},{1,2},{2,1},{3,0},{4,7},{5,6},{6,5},{7,4},{8,11},{9,10},{10,... | collective-permute-start | bytes 196616 | tf_op jit(solution)/shard_map/ppermute | solution.py:246
  7.3 0.0 collective-permute-start.1
  7.3 0.6 collective-permute-start
  7.9 2.0 %collective-permute-done.2.refs_3_ = f32[32,512]{1,0:T(8,128)S(1)} collective-permute-done((f32[32,512]{1,0:T(8,128)S(1)}, f32[32,512]{1,0:T(8,128)S(1)}, u32[]{:S(2)}, u32[]{:S(2)}) %collective-permute-start.2) | collective-permute-done | bytes 65568 | tf_op jit(solution)/shard_map/ppermute | solution.py:246
  9.9 0.0 copy-start.1
  9.9 3.0 %collective-permute-done.1.refs_2_ = f32[32,512]{1,0:T(8,128)S(1)} collective-permute-done((f32[32,512]{1,0:T(8,128)S(1)}, f32[32,512]{1,0:T(8,128)S(1)}, u32[]{:S(2)}, u32[]{:S(2)}) %collective-permute-start.1) | collective-permute-done | bytes 65568 | tf_op jit(solution)/shard_map/ppermute | solution.py:246
  12.9 0.0 copy-start.2
  12.9 0.0 collective-permute-done.refs_1_
  12.9 0.0 copy-start.3
  12.9 0.0 copy-done.1
  12.9 0.6 copy-done.2
  13.5 0.0 copy-done.3
  13.6 0.0 copy-start
  13.6 2.0 %gram_of_part.1 = f32[128,128]{1,0:T(8,128)} custom-call(s32[1]{0:T(128)} %bitcast.place_ref, f32[32,512]{1,0:T(8,128)} %get-tuple-element.9.refs_0_, f32[32,512]{1,0:T(8,128)} %copy-done.3, f32[32,512]{1,0:T(8,128)} %copy-done.2, f32[32,512]{1,0:T(8,128)} %copy-done.1), custom_call_target="tpu_custom_call" | custom-call | tf_op jit(solution)/shard_map/gram_of_part/pallas_call | solution.py:235
  15.5 0.0 collective-permute-start.3
  15.6 1.5 %collective-permute-done.3 = f32[128,128]{1,0:T(8,128)S(1)} collective-permute-done((f32[128,128]{1,0:T(8,128)}, f32[128,128]{1,0:T(8,128)S(1)}, u32[]{:S(2)}, u32[]{:S(2)}) %collective-permute-start.3) | collective-permute-done | bytes 65568 | tf_op jit(solution)/shard_map/ppermute | solution.py:246
  17.0 0.9 %add.37 = f32[128,128]{1,0:T(8,128)S(1)} add(f32[128,128]{1,0:T(8,128)} %gram_of_part.1, f32[128,128]{1,0:T(8,128)S(1)} %collective-permute-done.3) | non-fusion elementwise | flops 16384 | bytes 196608 | tf_op jit(solution)/shard_map/add | solution.py:256
  17.9 0.0 copy-start.4
  17.9 2.5 %collective-permute-start.6 = (f32[128,128]{1,0:T(8,128)S(1)}, f32[128,128]{1,0:T(8,128)S(1)}, u32[]{:S(2)}, u32[]{:S(2)}) collective-permute-start(f32[128,128]{1,0:T(8,128)S(1)} %add.37), channel_id=1, source_target_pairs={{0,24},{4,28},{8,16},{12,20},{16,8},{20,12},{24,0},{28,4},{1,25},{... | collective-permute-start | bytes 196616 | tf_op jit(solution)/shard_map/ppermute | solution.py:246
  20.4 0.5 collective-permute-start.5
  20.9 0.5 collective-permute-start.4
  21.4 0.0 copy-done
  21.4 1.6 %collective-permute-start.11 = (f32[32,2048]{1,0:T(8,128)S(1)}, f32[32,2048]{1,0:T(8,128)S(1)}, u32[]{:S(2)}, u32[]{:S(2)}) collective-permute-start(f32[32,2048]{1,0:T(8,128)S(1)} %copy-done), channel_id=1, source_target_pairs={{0,2},{1,3},{2,0},{3,1},{4,6},{5,7},{6,4},{7,5},{8,10},{9,11},{10,... | collective-permute-start | bytes 786440 | tf_op jit(solution)/shard_map/ppermute | solution.py:246
  23.0 1.7 %collective-permute-start.10 = (f32[32,2048]{1,0:T(8,128)S(1)}, f32[32,2048]{1,0:T(8,128)S(1)}, u32[]{:S(2)}, u32[]{:S(2)}) collective-permute-start(f32[32,2048]{1,0:T(8,128)S(1)} %copy-done), channel_id=1, source_target_pairs={{0,1},{1,0},{2,3},{3,2},{4,5},{5,4},{6,7},{7,6},{8,9},{9,8},{10,11... | collective-permute-start | bytes 786440 | tf_op jit(solution)/shard_map/ppermute | solution.py:246
  24.6 0.0 collective-permute-done.6
  24.6 0.0 collective-permute-done.5
  24.6 0.5 collective-permute-done.4
  25.2 2.7 %collective-permute-start.9 = (f32[128,128]{1,0:T(8,128)S(1)}, f32[128,128]{1,0:T(8,128)S(1)}, u32[]{:S(2)}, u32[]{:S(2)}) collective-permute-start(f32[128,128]{1,0:T(8,128)S(1)} %add_add_fusion.1), channel_id=1, source_target_pairs={{0,3},{1,2},{2,1},{3,0},{4,7},{5,6},{6,5},{7,4},{8,11},{9,10},{10,... | collective-permute-start | bytes 196616 | tf_op jit(solution)/shard_map/ppermute | solution.py:246
  27.9 0.0 collective-permute-start.8
  27.9 1.7 %collective-permute-start.7 = (f32[128,128]{1,0:T(8,128)S(1)}, f32[128,128]{1,0:T(8,128)S(1)}, u32[]{:S(2)}, u32[]{:S(2)}) collective-permute-start(f32[128,128]{1,0:T(8,128)S(1)} %add_add_fusion.1), channel_id=1, source_target_pairs={{0,1},{1,0},{2,3},{3,2},{4,5},{5,4},{6,7},{7,6},{8,9},{9,8},{10,11... | collective-permute-start | bytes 196616 | tf_op jit(solution)/shard_map/ppermute | solution.py:246
  29.6 0.0 copy-done.4
  29.7 9.3 %collective-permute-done.9 = f32[128,128]{1,0:T(8,128)S(1)} collective-permute-done((f32[128,128]{1,0:T(8,128)S(1)}, f32[128,128]{1,0:T(8,128)S(1)}, u32[]{:S(2)}, u32[]{:S(2)}) %collective-permute-start.9) | collective-permute-done | bytes 65568 | tf_op jit(solution)/shard_map/ppermute | solution.py:246
  38.9 2.0 %collective-permute-start.12 = (f32[32,2048]{1,0:T(8,128)S(1)}, f32[32,2048]{1,0:T(8,128)S(1)}, u32[]{:S(2)}, u32[]{:S(2)}) collective-permute-start(f32[32,2048]{1,0:T(8,128)S(1)} %copy-done), channel_id=1, source_target_pairs={{0,3},{1,2},{2,1},{3,0},{4,7},{5,6},{6,5},{7,4},{8,11},{9,10},{10,... | collective-permute-start | bytes 786440 | tf_op jit(solution)/shard_map/ppermute | solution.py:246
  40.9 6.5 %collective-permute-done.8 = f32[128,128]{1,0:T(8,128)S(1)} collective-permute-done((f32[128,128]{1,0:T(8,128)S(1)}, f32[128,128]{1,0:T(8,128)S(1)}, u32[]{:S(2)}, u32[]{:S(2)}) %collective-permute-start.8) | collective-permute-done | bytes 65568 | tf_op jit(solution)/shard_map/ppermute | solution.py:246
  47.4 0.0 collective-permute-done.7
  47.4 24.3 %all_rounds.1 = (f32[128,128]{1,0:T(8,128)S(1)}, f32[8,128]{1,0:T(8,128)S(1)}) custom-call(f32[128,128]{1,0:T(8,128)S(1)} %add_add_fusion.gram_ref, s32[32,32]{1,0:T(8,128)S(1)} %pad_add_fusion.plan_ref, s32[1]{0:T(128)} %bitcast.place_ref), custom_call_target="tpu_custom_call" | custom-call | tf_op jit(solution)/shard_map/all_rounds/pallas_call | solution.py:204
  71.8 0.5 multiply_bitcast_fusion
  72.3 0.0 collective-permute-done.11
  72.3 0.0 collective-permute-done.10
  72.3 0.0 collective-permute-done.12
  72.3 1.4 %convolution_multiply_fusion = f32[32,2048]{1,0:T(8,128)} fusion(f32[32,2048]{1,0:T(8,128)S(1)} %collective-permute-done.12, f32[32,2048]{1,0:T(8,128)S(1)} %collective-permute-done.11, f32[32,2048]{1,0:T(8,128)S(1)} %collective-permute-done.10, f32[32,2048]{1,0:T(8,128)S(1)} %copy-done, f32[128,128]{1,0:T(8,128)S(1)} %get-tuple-element.4), kind=kOutput, calls=%fused_computation | convolution fusion | flops 101515264 | bytes 1376256 | tf_op jit(solution)/shard_map/dot_general | solution.py:275
  (4 shorter events, 0.0 us)
Async XLA Ops:
  2.2 7.6 %collective-permute-start.2 = (f32[32,512]{1,0:T(8,128)S(1)}, f32[32,512]{1,0:T(8,128)S(1)}, u32[]{:S(2)}, u32[]{:S(2)}) collective-permute-start(f32[32,512]{1,0:T(8,128)S(1)} %get-tuple-element.6), channel_id=1, source_target_pairs={{0,3},{1,2},{2,1},{3,0},{4,7},{5,6},{6,5},{7,4},{8,11},{9,10},{10,... | collective-permute-start | bytes 196616 | tf_op jit(solution)/shard_map/ppermute | solution.py:246
  7.3 5.6 %collective-permute-start.1 = (f32[32,512]{1,0:T(8,128)S(1)}, f32[32,512]{1,0:T(8,128)S(1)}, u32[]{:S(2)}, u32[]{:S(2)}) collective-permute-start(f32[32,512]{1,0:T(8,128)S(1)} %get-tuple-element.7), channel_id=1, source_target_pairs={{0,2},{1,3},{2,0},{3,1},{4,6},{5,7},{6,4},{7,5},{8,10},{9,11},{10,... | collective-permute-start | bytes 196616 | tf_op jit(solution)/shard_map/ppermute | solution.py:246
  7.3 5.6 %collective-permute-start = (f32[32,512]{1,0:T(8,128)S(1)}, f32[32,512]{1,0:T(8,128)S(1)}, u32[]{:S(2)}, u32[]{:S(2)}) collective-permute-start(f32[32,512]{1,0:T(8,128)S(1)} %get-tuple-element.8), channel_id=1, source_target_pairs={{0,1},{1,0},{2,3},{3,2},{4,5},{5,4},{6,7},{7,6},{8,9},{9,8},{10,11... | collective-permute-start | bytes 196616 | tf_op jit(solution)/shard_map/ppermute | solution.py:246
  9.9 3.0 %copy-start.1 = (f32[32,512]{1,0:T(8,128)}, f32[32,512]{1,0:T(8,128)S(1)}, u32[]{:S(2)}) copy-start(f32[32,512]{1,0:T(8,128)S(1)} %collective-permute-done.2.refs_3_) | copy-start | bytes 196612
  12.9 0.6 copy-start.2
  12.9 0.7 copy-start.3
  13.6 7.9 %copy-start = (f32[32,2048]{1,0:T(8,128)S(1)}, f32[32,2048]{1,0:T(8,128)}, u32[]{:S(2)}) copy-start(f32[32,2048]{1,0:T(8,128)} %param.2) | copy-start | bytes 786436
  15.5 1.5 %collective-permute-start.3 = (f32[128,128]{1,0:T(8,128)}, f32[128,128]{1,0:T(8,128)S(1)}, u32[]{:S(2)}, u32[]{:S(2)}) collective-permute-start(f32[128,128]{1,0:T(8,128)} %gram_of_part.1), channel_id=1, source_target_pairs={{0,4},{4,0},{8,12},{12,8},{16,20},{20,16},{24,28},{28,24},{1,5},{5... | collective-permute-start | bytes 196616 | tf_op jit(solution)/shard_map/ppermute | solution.py:246
  17.9 11.8 %copy-start.4 = (s32[31,32]{1,0:T(8,128)S(1)}, s32[31,32]{1,0:T(8,128)}, u32[]{:S(2)}) copy-start(s32[31,32]{1,0:T(8,128)} %param.3) | copy-start | bytes 11908
  17.9 6.8 %collective-permute-start.6 = (f32[128,128]{1,0:T(8,128)S(1)}, f32[128,128]{1,0:T(8,128)S(1)}, u32[]{:S(2)}, u32[]{:S(2)}) collective-permute-start(f32[128,128]{1,0:T(8,128)S(1)} %add.37), channel_id=1, source_target_pairs={{0,24},{4,28},{8,16},{12,20},{16,8},{20,12},{24,0},{28,4},{1,25},{... | collective-permute-start | bytes 196616 | tf_op jit(solution)/shard_map/ppermute | solution.py:246
  20.4 4.3 %collective-permute-start.5 = (f32[128,128]{1,0:T(8,128)S(1)}, f32[128,128]{1,0:T(8,128)S(1)}, u32[]{:S(2)}, u32[]{:S(2)}) collective-permute-start(f32[128,128]{1,0:T(8,128)S(1)} %add.37), channel_id=1, source_target_pairs={{0,16},{4,20},{8,24},{12,28},{16,0},{20,4},{24,8},{28,12},{1,17},{... | collective-permute-start | bytes 196616 | tf_op jit(solution)/shard_map/ppermute | solution.py:246
  20.9 4.3 %collective-permute-start.4 = (f32[128,128]{1,0:T(8,128)S(1)}, f32[128,128]{1,0:T(8,128)S(1)}, u32[]{:S(2)}, u32[]{:S(2)}) collective-permute-start(f32[128,128]{1,0:T(8,128)S(1)} %add.37), channel_id=1, source_target_pairs={{0,8},{4,12},{8,0},{12,4},{16,24},{20,28},{24,16},{28,20},{1,9},{5... | collective-permute-start | bytes 196616 | tf_op jit(solution)/shard_map/ppermute | solution.py:246
  21.4 50.9 %collective-permute-start.11 = (f32[32,2048]{1,0:T(8,128)S(1)}, f32[32,2048]{1,0:T(8,128)S(1)}, u32[]{:S(2)}, u32[]{:S(2)}) collective-permute-start(f32[32,2048]{1,0:T(8,128)S(1)} %copy-done), channel_id=1, source_target_pairs={{0,2},{1,3},{2,0},{3,1},{4,6},{5,7},{6,4},{7,5},{8,10},{9,11},{10,... | collective-permute-start | bytes 786440 | tf_op jit(solution)/shard_map/ppermute | solution.py:246
  23.0 49.3 %collective-permute-start.10 = (f32[32,2048]{1,0:T(8,128)S(1)}, f32[32,2048]{1,0:T(8,128)S(1)}, u32[]{:S(2)}, u32[]{:S(2)}) collective-permute-start(f32[32,2048]{1,0:T(8,128)S(1)} %copy-done), channel_id=1, source_target_pairs={{0,1},{1,0},{2,3},{3,2},{4,5},{5,4},{6,7},{7,6},{8,9},{9,8},{10,11... | collective-permute-start | bytes 786440 | tf_op jit(solution)/shard_map/ppermute | solution.py:246
  25.2 13.7 %collective-permute-start.9 = (f32[128,128]{1,0:T(8,128)S(1)}, f32[128,128]{1,0:T(8,128)S(1)}, u32[]{:S(2)}, u32[]{:S(2)}) collective-permute-start(f32[128,128]{1,0:T(8,128)S(1)} %add_add_fusion.1), channel_id=1, source_target_pairs={{0,3},{1,2},{2,1},{3,0},{4,7},{5,6},{6,5},{7,4},{8,11},{9,10},{10,... | collective-permute-start | bytes 196616 | tf_op jit(solution)/shard_map/ppermute | solution.py:246
  27.9 19.5 %collective-permute-start.8 = (f32[128,128]{1,0:T(8,128)S(1)}, f32[128,128]{1,0:T(8,128)S(1)}, u32[]{:S(2)}, u32[]{:S(2)}) collective-permute-start(f32[128,128]{1,0:T(8,128)S(1)} %add_add_fusion.1), channel_id=1, source_target_pairs={{0,2},{1,3},{2,0},{3,1},{4,6},{5,7},{6,4},{7,5},{8,10},{9,11},{10,... | collective-permute-start | bytes 196616 | tf_op jit(solution)/shard_map/ppermute | solution.py:246
  27.9 19.5 %collective-permute-start.7 = (f32[128,128]{1,0:T(8,128)S(1)}, f32[128,128]{1,0:T(8,128)S(1)}, u32[]{:S(2)}, u32[]{:S(2)}) collective-permute-start(f32[128,128]{1,0:T(8,128)S(1)} %add_add_fusion.1), channel_id=1, source_target_pairs={{0,1},{1,0},{2,3},{3,2},{4,5},{5,4},{6,7},{7,6},{8,9},{9,8},{10,11... | collective-permute-start | bytes 196616 | tf_op jit(solution)/shard_map/ppermute | solution.py:246
  38.9 33.4 %collective-permute-start.12 = (f32[32,2048]{1,0:T(8,128)S(1)}, f32[32,2048]{1,0:T(8,128)S(1)}, u32[]{:S(2)}, u32[]{:S(2)}) collective-permute-start(f32[32,2048]{1,0:T(8,128)S(1)} %copy-done), channel_id=1, source_target_pairs={{0,3},{1,2},{2,1},{3,0},{4,7},{5,6},{6,5},{7,4},{8,11},{9,10},{10,... | collective-permute-start | bytes 786440 | tf_op jit(solution)/shard_map/ppermute | solution.py:246

commit v3 on v2

--- a/solution.py
+++ b/solution.py
@@ -112,7 +112,7 @@
     )
 
 
-def turn_kernel(n_steps, gram_ref, plan_ref, place_ref, modes_ref, energy_ref, c_ref, q_ref, index_ref, sign_ref):
+def turn_kernel(n_steps, n_cells, gram_ref, plan_ref, place_ref, modes_ref, mean_ref, energy_ref, c_ref, q_ref, index_ref, sign_ref):
     cols = gram_ref.shape[0]
     pair = plan_ref.shape[1]
     half = pair // 2
@@ -187,29 +187,30 @@
     lax.fori_loop(0, ROUNDS, one_round, 0)
     place = place_ref[0]
     to_front = lax.rem(cols - place * pair, cols)
-    energy_ref[...] = pltpu.roll(energy_ref[...], to_front, 1)
+    mean_ref[...] = pltpu.roll(energy_ref[...], to_front, 1)[0:1, 0:pair] / n_cells
     for d in range(cols // pair):
         rows = q_ref[pl.ds(pl.multiple_of((place ^ d) * pair, pair), pair), :]
-        modes_ref[d * pair : (d + 1) * pair] = pltpu.roll(rows, to_front, 1)
+        modes_ref[d * pair : (d + 1) * pair] = pltpu.roll(rows, to_front, 1)[:, 0:pair]
 
 
 def in_vmem(n):
     return [pl.BlockSpec(memory_space=pltpu.VMEM)] * n
 
 
-def turn_all(gram, plan, place):
+def turn_all(gram, plan, place, n_cells):
     cols = gram.shape[0]
     n_steps, pair = plan.shape
     plan = jnp.concatenate([plan, jnp.arange(pair, dtype=jnp.int32)[None]], axis=0)
     return pl.pallas_call(
-        functools.partial(turn_kernel, n_steps),
+        functools.partial(turn_kernel, n_steps, n_cells),
         out_shape=(
-            jax.ShapeDtypeStruct((cols, cols), jnp.float32),
-            jax.ShapeDtypeStruct((8, cols), jnp.float32),
+            jax.ShapeDtypeStruct((cols, pair), jnp.float32),
+            jax.ShapeDtypeStruct((1, pair), jnp.float32),
         ),
         in_specs=in_vmem(2) + [pl.BlockSpec(memory_space=pltpu.SMEM)],
         out_specs=in_vmem(2),
         scratch_shapes=[
+            pltpu.VMEM((8, cols), jnp.float32),
             pltpu.VMEM((cols, cols), jnp.float32),
             pltpu.VMEM((cols, cols), jnp.float32),
             pltpu.VMEM((2 * pair, LANES), jnp.int32),
@@ -220,28 +221,6 @@
     )(gram, plan, place)
 
 
-def gram_kernel(place_ref, *refs):
-    blocks, gram_ref, whole_ref = refs[:-2], refs[-2], refs[-1]
-    pair = blocks[0].shape[0]
-    for d, block in enumerate(blocks):
-        whole_ref[pl.ds(pl.multiple_of((place_ref[0] ^ d) * pair, pair), pair), :] = block[...]
-    whole = whole_ref[...]
-    gram_ref[...] = dot_full(whole, whole, 1, 1)
-
-
-def gram_of(blocks, place):
-    pair, cells = blocks[0].shape
-    cols = pair * len(blocks)
-    return pl.pallas_call(
-        gram_kernel,
-        out_shape=jax.ShapeDtypeStruct((cols, cols), jnp.float32),
-        in_specs=[pl.BlockSpec(memory_space=pltpu.SMEM)] + in_vmem(len(blocks)),
-        out_specs=pl.BlockSpec(memory_space=pltpu.VMEM),
-        scratch_shapes=[pltpu.VMEM((cols, cells), jnp.float32)],
-        name="gram_of_part",
-    )(place, *blocks)
-
-
 def sent(value, axis, toggle):
     return lax.ppermute(value, axis, [(i, i ^ toggle) for i in range(lax.axis_size(axis))])
 
@@ -252,15 +231,9 @@
     return values[0]
 
 
-def summed_over_all(x):
-    x = x + sent(x, "cell", 1)
-    x = tree_sum([x] + [sent(x, "cell", d) for d in range(2, lax.axis_size("cell"), 2)])
-    return tree_sum([x] + [sent(x, "blk", d) for d in range(1, lax.axis_size("blk"))])
-
-
 def on_device(snapshots, plan):
     pair, cells = snapshots.shape
-    n_blk = lax.axis_size("blk")
+    n_blk, n_cell = lax.axis_size("blk"), lax.axis_size("cell")
     here = lax.axis_index("blk")
     place = here.astype(jnp.int32)[None]
     part = cells // n_blk
@@ -268,18 +241,20 @@
     def part_for(d):
         return lax.dynamic_slice_in_dim(snapshots, (here ^ d) * part, part, 1)
 
-    parts = [part_for(0)] + [sent(part_for(d), "blk", d) for d in range(1, n_blk)]
-    blocks = [snapshots] + [sent(snapshots, "blk", d) for d in range(1, n_blk)]
-    gram = summed_over_all(gram_of(parts, place))
-    modes, energy = turn_all(gram, plan, place)
+    parts = jnp.stack([part_for(0)] + [sent(part_for(d), "blk", d) for d in range(1, n_blk)])
+    parts = [lax.dynamic_index_in_dim(parts, here ^ q, 0, keepdims=False) for q in range(n_blk)]
+    whole = jnp.concatenate(parts, axis=0)
+    gram = lax.dot_general(whole, whole, (((1,), (1,)), ((), ())), precision=lax.Precision.HIGHEST)
+    gram = gram + sent(gram, "cell", 1)
+    gram = tree_sum([gram] + [sent(gram, "blk", d) for d in range(1, n_blk)])
+    gram, held = lax.optimization_barrier((gram, snapshots))
+    blocks = [snapshots] + [sent(held, "blk", d) for d in range(1, n_blk)]
+    gram = tree_sum([gram] + [sent(gram, "cell", d) for d in range(2, n_cell, 2)])
+    modes, energy = turn_all(gram, plan, place, cells * n_cell)
     rotated = lax.dot_general(
-        modes[:, :pair],
-        jnp.concatenate(blocks, axis=0),
-        (((0,), (0,)), ((), ())),
-        precision=lax.Precision.HIGHEST,
+        modes, jnp.concatenate(blocks, axis=0), (((0,), (0,)), ((), ())), precision=lax.Precision.HIGHEST
     )
-    mode_energy = energy[0, :pair] / (cells * lax.axis_size("cell"))
-    return rotated * rotated, mode_energy
+    return rotated * rotated, energy.reshape(pair)
 
 
 def solution(mesh):

time: 73.9 us -> 57.6 us (0.78)
  waiting for transfers between devices: 22.8 us -> 10.8 us
  Pallas kernels: 26.3 us -> 24.8 us
  other arithmetic: 1.42 us -> 0.07 us
  local copies, waits for them, and re-layouts: 2.26 us -> 1.01 us
    ppermute x13, waiting for transfers between devices: 22.8 us -> 10.8 us  [sent(): lax.ppermute(value, axis, [(i, i ^ toggle) for i in range(lax.axis_size(a...]
    dynamic_slice x1 -> x0, local copies, waits for them, and re-layouts: 1.59 us -> none  [part_for(): return lax.dynamic_slice_in_dim(snapshots, (here ^ d) * part, part, 1)]
    pallas_call x2 -> x1, Pallas kernels: 26.3 us -> 24.8 us  [turn_all(): pl.pallas_call(functools.partial(turn_kernel, n_steps, n_cells), out_shap...]
    another operation x0 -> x1, local copies, waits for them, and re-layouts: none -> 0.97 us  [on_device(): jnp.stack([part_for(0)] + [sent(part_for(d), 'blk', d) for d in range(1,...]
    add x1, other arithmetic: 0.85 us -> 0.01 us  [on_device(): gram = gram + sent(gram, 'cell', 1)]
    dot_general x1 -> x2, matrix products: 1.36 us -> 1.73 us  [the longest x1 1.35 us: on_device(): lax.dot_general(modes, jnp.concatenate(blocks, axis=0), (((0,), (0,)), ((...]
  transfers between devices with their start and end apart: 13 -> 13, of which waited for: 6 -> 5; matrix products, arithmetic and copies ran while one was open for 1% -> 0% of each run, Pallas kernels for 33% -> 43%
where the time goes in v3:
time: 57.6 us; the launch traced here: 57.5 us
  Pallas kernels  24.8 us (43%)
  starting transfers between devices  18.2 us (32%)
  waiting for transfers between devices  10.8 us (19%)
  matrix products  1.73 us (3%)
  local copies, waits for them, and re-layouts  1.01 us (2%)
  between operations  0.75 us (1%)
    pallas_call x1, Pallas kernels, turn_all(): pl.pallas_call(functools.partial(turn_kernel, n_steps, n_cells), out_shap...  24.8 us
    ppermute x13, starting transfers between devices, sent(): lax.ppermute(value, axis, [(i, i ^ toggle) for i in range(lax.axis_size(a...  18.2 us
    ppermute x13, waiting for transfers between devices, sent(): lax.ppermute(value, axis, [(i, i ^ toggle) for i in range(lax.axis_size(a...  10.8 us
    dot_general x1, matrix products, on_device(): lax.dot_general(modes, jnp.concatenate(blocks, axis=0), (((0,), (0,)), ((...  1.35 us
  transfers between devices with their start and end apart: 13, of which 5 were waited for; matrix products, arithmetic and copies ran while one was open for 0% of the time, Pallas kernels for 43%

profile of v3, /device:TPU:0, one launch (start us, length us, event | category | flops | bytes accessed | tf_op | source)
XLA Modules:
  0.0 57.5 jit_solution(12009960653759781268)
XLA Ops:
  0.7 1.0 %dynamic-slice_bitcast_fusion.4 = (f32[1,32,512]{2,1,0:T(8,128)S(1)}, f32[32,512]{1,0:T(8,128)S(1)}, f32[32,512]{1,0:T(8,128)S(1)}, f32[32,512]{1,0:T(8,128)S(1)}) fusion(f32[32,2048]{1,0:T(8,128)} %param.2, s32[]{:T(128)S(6)} %select_n.25, s32[]{:T(128)S(6)} %select_n.28, s32[]{:T(128)S(6)} %select_n.27, s32[]{:T(128)S(6)} %select_n.26), kind=kLoop, calls=%fused_computation.23 | loop fusion | bytes 524304 | tf_op jit(solution)/shard_map/stack | solution.py:244
  1.6 5.1 %collective-permute-start.2 = (f32[32,512]{1,0:T(8,128)S(1)}, f32[32,512]{1,0:T(8,128)S(1)}, u32[]{:S(2)}, u32[]{:S(2)}) collective-permute-start(f32[32,512]{1,0:T(8,128)S(1)} %get-tuple-element.15), channel_id=1, source_target_pairs={{0,3},{1,2},{2,1},{3,0},{4,7},{5,6},{6,5},{7,4},{8,11},{9,10},{10,... | collective-permute-start | bytes 196616 | tf_op jit(solution)/shard_map/ppermute | solution.py:225
  6.7 0.0 collective-permute-start.1
  6.7 0.6 %collective-permute-start = (f32[32,512]{1,0:T(8,128)S(1)}, f32[32,512]{1,0:T(8,128)S(1)}, u32[]{:S(2)}, u32[]{:S(2)}) collective-permute-start(f32[32,512]{1,0:T(8,128)S(1)} %get-tuple-element.17), channel_id=1, source_target_pairs={{0,1},{1,0},{2,3},{3,2},{4,5},{5,4},{6,7},{7,6},{8,9},{9,8},{10,11... | collective-permute-start | bytes 196616 | tf_op jit(solution)/shard_map/ppermute | solution.py:225
  7.4 1.9 %collective-permute-done.2 = f32[32,512]{1,0:T(8,128)S(1)} collective-permute-done((f32[32,512]{1,0:T(8,128)S(1)}, f32[32,512]{1,0:T(8,128)S(1)}, u32[]{:S(2)}, u32[]{:S(2)}) %collective-permute-start.2) | collective-permute-done | bytes 65568 | tf_op jit(solution)/shard_map/ppermute | solution.py:225
  9.3 3.0 %collective-permute-done.1 = f32[32,512]{1,0:T(8,128)S(1)} collective-permute-done((f32[32,512]{1,0:T(8,128)S(1)}, f32[32,512]{1,0:T(8,128)S(1)}, u32[]{:S(2)}, u32[]{:S(2)}) %collective-permute-start.1) | collective-permute-done | bytes 65568 | tf_op jit(solution)/shard_map/ppermute | solution.py:225
  12.3 0.0 collective-permute-done
  12.4 0.4 fusion.7
  12.8 0.0 copy-start
  12.8 0.1 collective-permute-start.3
  12.9 1.2 %collective-permute-done.3 = f32[128,128]{1,0:T(8,128)S(1)} collective-permute-done((f32[128,128]{1,0:T(8,128)S(1)}, f32[128,128]{1,0:T(8,128)S(1)}, u32[]{:S(2)}, u32[]{:S(2)}) %collective-permute-start.3) | collective-permute-done | bytes 65568 | tf_op jit(solution)/shard_map/ppermute | solution.py:225
  14.1 0.0 copy-start.1
  14.2 2.8 %collective-permute-start.6 = (f32[128,128]{1,0:T(8,128)S(1)}, f32[128,128]{1,0:T(8,128)S(1)}, u32[]{:S(2)}, u32[]{:S(2)}) collective-permute-start(f32[128,128]{1,0:T(8,128)S(1)} %add.54), channel_id=1, source_target_pairs={{0,3},{1,2},{2,1},{3,0},{4,7},{5,6},{6,5},{7,4},{8,11},{9,10},{10,... | collective-permute-start | bytes 196616 | tf_op jit(solution)/shard_map/ppermute | solution.py:225
  16.9 0.0 collective-permute-start.5
  16.9 1.7 %collective-permute-start.4 = (f32[128,128]{1,0:T(8,128)S(1)}, f32[128,128]{1,0:T(8,128)S(1)}, u32[]{:S(2)}, u32[]{:S(2)}) collective-permute-start(f32[128,128]{1,0:T(8,128)S(1)} %add.54), channel_id=1, source_target_pairs={{0,1},{1,0},{2,3},{3,2},{4,5},{5,4},{6,7},{7,6},{8,9},{9,8},{10,11... | collective-permute-start | bytes 196616 | tf_op jit(solution)/shard_map/ppermute | solution.py:225
  18.6 2.4 %collective-permute-done.6 = f32[128,128]{1,0:T(8,128)S(1)} collective-permute-done((f32[128,128]{1,0:T(8,128)S(1)}, f32[128,128]{1,0:T(8,128)S(1)}, u32[]{:S(2)}, u32[]{:S(2)}) %collective-permute-start.6) | collective-permute-done | bytes 65568 | tf_op jit(solution)/shard_map/ppermute | solution.py:225
  21.0 2.2 %collective-permute-done.5 = f32[128,128]{1,0:T(8,128)S(1)} collective-permute-done((f32[128,128]{1,0:T(8,128)S(1)}, f32[128,128]{1,0:T(8,128)S(1)}, u32[]{:S(2)}, u32[]{:S(2)}) %collective-permute-start.5) | collective-permute-done | bytes 65568 | tf_op jit(solution)/shard_map/ppermute | solution.py:225
  23.2 0.0 collective-permute-done.4
  23.2 2.5 %collective-permute-start.9 = (f32[128,128]{1,0:T(8,128)S(1)}, f32[128,128]{1,0:T(8,128)S(1)}, u32[]{:S(2)}, u32[]{:S(2)}) collective-permute-start(f32[128,128]{1,0:T(8,128)S(1)} %add_add_fusion.1), channel_id=1, source_target_pairs={{0,24},{4,28},{8,16},{12,20},{16,8},{20,12},{24,0},{28,4},{1,25},{... | collective-permute-start | bytes 196616 | tf_op jit(solution)/shard_map/ppermute | solution.py:225
  25.7 0.5 collective-permute-start.8
  26.3 0.5 collective-permute-start.7
  26.8 0.0 copy-done
  26.8 2.4 %collective-permute-start.12 = (f32[32,2048]{1,0:T(8,128)S(1)}, f32[32,2048]{1,0:T(8,128)S(1)}, u32[]{:S(2)}, u32[]{:S(2)}) collective-permute-start(f32[32,2048]{1,0:T(8,128)S(1)} %copy-done), channel_id=1, source_target_pairs={{0,3},{1,2},{2,1},{3,0},{4,7},{5,6},{6,5},{7,4},{8,11},{9,10},{10,... | collective-permute-start | bytes 786440 | tf_op jit(solution)/shard_map/ppermute | solution.py:225
  29.2 0.0 collective-permute-start.11
  29.2 0.0 collective-permute-done.9
  29.2 2.0 %collective-permute-start.10 = (f32[32,2048]{1,0:T(8,128)S(1)}, f32[32,2048]{1,0:T(8,128)S(1)}, u32[]{:S(2)}, u32[]{:S(2)}) collective-permute-start(f32[32,2048]{1,0:T(8,128)S(1)} %copy-done), channel_id=1, source_target_pairs={{0,1},{1,0},{2,3},{3,2},{4,5},{5,4},{6,7},{7,6},{8,9},{9,8},{10,11... | collective-permute-start | bytes 786440 | tf_op jit(solution)/shard_map/ppermute | solution.py:225
  31.2 0.0 copy-done.1
  31.2 0.0 collective-permute-done.8
  31.2 0.0 collective-permute-done.7
  31.2 24.8 %all_rounds.1 = (f32[128,32]{1,0:T(8,128)S(1)}, f32[1,32]{1,0:T(1,128)}) custom-call(f32[128,128]{1,0:T(8,128)S(1)} %add_add_fusion.gram_ref, s32[32,32]{1,0:T(8,128)S(1)} %pad_add_fusion.plan_ref, s32[1]{0:T(128)} %bitcast.8.place_ref), custom_call_target="tpu_custom_call" | custom-call | tf_op jit(solution)/shard_map/all_rounds/pallas_call | solution.py:204
  56.1 0.0 collective-permute-done.12
  56.1 0.0 collective-permute-done.11
  56.1 0.0 collective-permute-done.10
  56.1 1.4 %convolution_multiply_fusion = f32[32,2048]{1,0:T(8,128)} fusion(f32[128,32]{1,0:T(8,128)S(1)} %get-tuple-element.7, f32[32,2048]{1,0:T(8,128)S(1)} %collective-permute-done.12, f32[32,2048]{1,0:T(8,128)S(1)} %collective-permute-done.11, f32[32,2048]{1,0:T(8,128)S(1)} %collective-permute-done.10, f32[32,2048]{1,0:T(8,128)S(1)} %copy-done), kind=kOutput, calls=%fused_computation | convolution fusion | flops 101515264 | bytes 1327104 | tf_op jit(solution)/shard_map/dot_general | solution.py:254
  (7 shorter events, 0.1 us)
Async XLA Ops:
  1.6 7.7 %collective-permute-start.2 = (f32[32,512]{1,0:T(8,128)S(1)}, f32[32,512]{1,0:T(8,128)S(1)}, u32[]{:S(2)}, u32[]{:S(2)}) collective-permute-start(f32[32,512]{1,0:T(8,128)S(1)} %get-tuple-element.15), channel_id=1, source_target_pairs={{0,3},{1,2},{2,1},{3,0},{4,7},{5,6},{6,5},{7,4},{8,11},{9,10},{10,... | collective-permute-start | bytes 196616 | tf_op jit(solution)/shard_map/ppermute | solution.py:225
  6.7 5.6 %collective-permute-start.1 = (f32[32,512]{1,0:T(8,128)S(1)}, f32[32,512]{1,0:T(8,128)S(1)}, u32[]{:S(2)}, u32[]{:S(2)}) collective-permute-start(f32[32,512]{1,0:T(8,128)S(1)} %get-tuple-element.16), channel_id=1, source_target_pairs={{0,2},{1,3},{2,0},{3,1},{4,6},{5,7},{6,4},{7,5},{8,10},{9,11},{10,... | collective-permute-start | bytes 196616 | tf_op jit(solution)/shard_map/ppermute | solution.py:225
  6.7 5.6 %collective-permute-start = (f32[32,512]{1,0:T(8,128)S(1)}, f32[32,512]{1,0:T(8,128)S(1)}, u32[]{:S(2)}, u32[]{:S(2)}) collective-permute-start(f32[32,512]{1,0:T(8,128)S(1)} %get-tuple-element.17), channel_id=1, source_target_pairs={{0,1},{1,0},{2,3},{3,2},{4,5},{5,4},{6,7},{7,6},{8,9},{9,8},{10,11... | collective-permute-start | bytes 196616 | tf_op jit(solution)/shard_map/ppermute | solution.py:225
  12.8 14.0 %copy-start = (f32[32,2048]{1,0:T(8,128)S(1)}, f32[32,2048]{1,0:T(8,128)}, u32[]{:S(2)}) copy-start(f32[32,2048]{1,0:T(8,128)} %param.2) | copy-start | bytes 786436
  12.8 1.3 %collective-permute-start.3 = (f32[128,128]{1,0:T(8,128)S(1)}, f32[128,128]{1,0:T(8,128)S(1)}, u32[]{:S(2)}, u32[]{:S(2)}) collective-permute-start(f32[128,128]{1,0:T(8,128)S(1)} %fusion.7), channel_id=1, source_target_pairs={{0,4},{4,0},{8,12},{12,8},{16,20},{20,16},{24,28},{28,24},{1,5},{5... | collective-permute-start | bytes 196616 | tf_op jit(solution)/shard_map/ppermute | solution.py:225
  14.1 17.1 %copy-start.1 = (s32[31,32]{1,0:T(8,128)S(1)}, s32[31,32]{1,0:T(8,128)}, u32[]{:S(2)}) copy-start(s32[31,32]{1,0:T(8,128)} %param.3) | copy-start | bytes 11908
  14.2 6.8 %collective-permute-start.6 = (f32[128,128]{1,0:T(8,128)S(1)}, f32[128,128]{1,0:T(8,128)S(1)}, u32[]{:S(2)}, u32[]{:S(2)}) collective-permute-start(f32[128,128]{1,0:T(8,128)S(1)} %add.54), channel_id=1, source_target_pairs={{0,3},{1,2},{2,1},{3,0},{4,7},{5,6},{6,5},{7,4},{8,11},{9,10},{10,... | collective-permute-start | bytes 196616 | tf_op jit(solution)/shard_map/ppermute | solution.py:225
  16.9 6.3 %collective-permute-start.5 = (f32[128,128]{1,0:T(8,128)S(1)}, f32[128,128]{1,0:T(8,128)S(1)}, u32[]{:S(2)}, u32[]{:S(2)}) collective-permute-start(f32[128,128]{1,0:T(8,128)S(1)} %add.54), channel_id=1, source_target_pairs={{0,2},{1,3},{2,0},{3,1},{4,6},{5,7},{6,4},{7,5},{8,10},{9,11},{10,... | collective-permute-start | bytes 196616 | tf_op jit(solution)/shard_map/ppermute | solution.py:225
  16.9 6.3 %collective-permute-start.4 = (f32[128,128]{1,0:T(8,128)S(1)}, f32[128,128]{1,0:T(8,128)S(1)}, u32[]{:S(2)}, u32[]{:S(2)}) collective-permute-start(f32[128,128]{1,0:T(8,128)S(1)} %add.54), channel_id=1, source_target_pairs={{0,1},{1,0},{2,3},{3,2},{4,5},{5,4},{6,7},{7,6},{8,9},{9,8},{10,11... | collective-permute-start | bytes 196616 | tf_op jit(solution)/shard_map/ppermute | solution.py:225
  23.2 6.0 %collective-permute-start.9 = (f32[128,128]{1,0:T(8,128)S(1)}, f32[128,128]{1,0:T(8,128)S(1)}, u32[]{:S(2)}, u32[]{:S(2)}) collective-permute-start(f32[128,128]{1,0:T(8,128)S(1)} %add_add_fusion.1), channel_id=1, source_target_pairs={{0,24},{4,28},{8,16},{12,20},{16,8},{20,12},{24,0},{28,4},{1,25},{... | collective-permute-start | bytes 196616 | tf_op jit(solution)/shard_map/ppermute | solution.py:225
  25.7 5.5 %collective-permute-start.8 = (f32[128,128]{1,0:T(8,128)S(1)}, f32[128,128]{1,0:T(8,128)S(1)}, u32[]{:S(2)}, u32[]{:S(2)}) collective-permute-start(f32[128,128]{1,0:T(8,128)S(1)} %add_add_fusion.1), channel_id=1, source_target_pairs={{0,16},{4,20},{8,24},{12,28},{16,0},{20,4},{24,8},{28,12},{1,17},{... | collective-permute-start | bytes 196616 | tf_op jit(solution)/shard_map/ppermute | solution.py:225
  26.3 5.0 %collective-permute-start.7 = (f32[128,128]{1,0:T(8,128)S(1)}, f32[128,128]{1,0:T(8,128)S(1)}, u32[]{:S(2)}, u32[]{:S(2)}) collective-permute-start(f32[128,128]{1,0:T(8,128)S(1)} %add_add_fusion.1), channel_id=1, source_target_pairs={{0,8},{4,12},{8,0},{12,4},{16,24},{20,28},{24,16},{28,20},{1,9},{5... | collective-permute-start | bytes 196616 | tf_op jit(solution)/shard_map/ppermute | solution.py:225
  26.8 29.3 %collective-permute-start.12 = (f32[32,2048]{1,0:T(8,128)S(1)}, f32[32,2048]{1,0:T(8,128)S(1)}, u32[]{:S(2)}, u32[]{:S(2)}) collective-permute-start(f32[32,2048]{1,0:T(8,128)S(1)} %copy-done), channel_id=1, source_target_pairs={{0,3},{1,2},{2,1},{3,0},{4,7},{5,6},{6,5},{7,4},{8,11},{9,10},{10,... | collective-permute-start | bytes 786440 | tf_op jit(solution)/shard_map/ppermute | solution.py:225
  29.2 26.9 %collective-permute-start.11 = (f32[32,2048]{1,0:T(8,128)S(1)}, f32[32,2048]{1,0:T(8,128)S(1)}, u32[]{:S(2)}, u32[]{:S(2)}) collective-permute-start(f32[32,2048]{1,0:T(8,128)S(1)} %copy-done), channel_id=1, source_target_pairs={{0,2},{1,3},{2,0},{3,1},{4,6},{5,7},{6,4},{7,5},{8,10},{9,11},{10,... | collective-permute-start | bytes 786440 | tf_op jit(solution)/shard_map/ppermute | solution.py:225
  29.2 26.9 %collective-permute-start.10 = (f32[32,2048]{1,0:T(8,128)S(1)}, f32[32,2048]{1,0:T(8,128)S(1)}, u32[]{:S(2)}, u32[]{:S(2)}) collective-permute-start(f32[32,2048]{1,0:T(8,128)S(1)} %copy-done), channel_id=1, source_target_pairs={{0,1},{1,0},{2,3},{3,2},{4,5},{5,4},{6,7},{7,6},{8,9},{9,8},{10,11... | collective-permute-start | bytes 786440 | tf_op jit(solution)/shard_map/ppermute | solution.py:225

commit v4 on v3

--- a/solution.py
+++ b/solution.py
@@ -36,24 +36,24 @@
     return one(a0, b0) + ((one(a0, b1) + one(a1, b0)) + small)
 
 
-def half_angle(twice_cross, spread, sign):
+def turning(twice_cross, own, other, sign):
+    spread = (own - other) * sign
     up_cross, up_spread = twice_cross * UP, spread * UP
     square = spread * spread + twice_cross * twice_cross
-    up_square = up_spread * up_spread + up_cross * up_cross
+    up_square = (up_spread * up_spread + FLOOR) + up_cross * up_cross
     is_small = square < TINY_SQUARE
-    norm_square = jnp.maximum(jnp.where(is_small, up_square, square), FLOOR)
+    norm_square = jnp.where(is_small, up_square, square)
     size = jnp.maximum(jnp.abs(jnp.where(is_small, up_spread, spread)), FLOOR_ROOT)
-    half_cross = jnp.where(is_small, up_cross, twice_cross) * (0.5 * sign)
+    cross = jnp.where(is_small, up_cross, twice_cross) * sign
+    half_norm = norm_square * jnp.where(is_small, (0.5 / UP) * sign, 0.5 * sign)
     cross_sign = jnp.where(twice_cross < 0, -sign, sign)
+    in_order = spread >= 0
     inverse = lax.rsqrt(norm_square)
-    large_square = 0.5 * (size * inverse) + 0.5
-    root = lax.rsqrt(large_square)
-    large = large_square * root
-    small = (half_cross * inverse) * root
-    in_order = spread >= 0
-    cosine = jnp.where(in_order, large, jnp.abs(small))
-    sine = jnp.where(in_order, small, cross_sign * large)
-    return cosine, sine
+    large = size * inverse + 1.0
+    small = cross * inverse
+    u = jnp.where(in_order, large, jnp.abs(small))
+    v = jnp.where(in_order, small, cross_sign * large)
+    return u, v, lax.rsqrt(large + large), 0.5 * (own + other) + half_norm * inverse
 
 
 def gather(x, index):
@@ -72,44 +72,31 @@
     return jnp.sum(wx * ty + wy * tx, axis=0, keepdims=True)
 
 
-def new_diagonal(cosine, sine, twice_cross, own, other):
-    return (cosine * cosine) * own + (cosine * sine) * twice_cross + (sine * sine) * other
-
-
-def single_step(state, index, signs):
+def last_step(state, places, sign):
     w, t, d = state
-    (p,) = index
-    wp, tp, dp = gather(w, p), gather(t, p), gather(d, p)
-    (sign,) = signs
-    cross = both(w, t, wp, tp)
-    c, s = half_angle(cross, (d - dp) * sign, sign)
-    return turned_by(c, s, w, wp), turned_by(c, s, t, tp), new_diagonal(c, s, cross, d, dp)
+    (wi, ti, di), (wp, tp, dp) = [[gather(x, place) for x in (w, t, d)] for place in places]
+    u, v, f, d = turning(both(wi, ti, wp, tp), di, dp, sign)
+    return turned_by(u * f, v * f, ti, tp), d
 
 
 def double_step(state, index, signs):
     w, t, d = state
     p, q, pq = index
     sign, sign_q, sign_next = signs
-    wp, tp, dp = gather(w, p), gather(t, p), gather(d, p)
     wq, tq, dq = gather(w, q), gather(t, q), gather(d, q)
     wpq, tpq, dpq = gather(w, pq), gather(t, pq), gather(d, pq)
-    cross = both(w, t, wp, tp)
-    cross_q = both(wq, tq, wpq, tpq)
+    wp, tp, dp = gather(w, p), gather(t, p), gather(d, p)
+    u, v, f, d1 = turning(both(w, t, wp, tp), d, dp, sign)
+    uq, vq, fq, d1q = turning(both(wq, tq, wpq, tpq), dq, dpq, sign_q)
     e00, e01 = both(w, t, wq, tq), both(w, t, wpq, tpq)
     e10, e11 = both(wp, tp, wq, tq), both(wp, tp, wpq, tpq)
-    c, s = half_angle(cross, (d - dp) * sign, sign)
-    cq, sq = half_angle(cross_q, (dq - dpq) * sign_q, sign_q)
-    cross_next = ((c * cq) * e00 + (s * sq) * e11) + ((c * sq) * e01 + (s * cq) * e10)
-    d1 = new_diagonal(c, s, cross, d, dp)
-    d1q = new_diagonal(cq, sq, cross_q, dq, dpq)
-    c1, s1 = half_angle(cross_next, (d1 - d1q) * sign_next, sign_next)
+    cross = (f * fq) * (((u * uq) * e00 + (v * vq) * e11) + ((u * vq) * e01 + (v * uq) * e10))
+    u1, v1, f1, d2 = turning(cross, d1, d1q, sign_next)
+    c, s, cq, sq = u * f, v * f, uq * fq, vq * fq
+    c1, s1 = u1 * f1, v1 * f1
     w1, t1 = turned_by(c, s, w, wp), turned_by(c, s, t, tp)
     w1q, t1q = turned_by(cq, sq, wq, wpq), turned_by(cq, sq, tq, tpq)
-    return (
-        turned_by(c1, s1, w1, w1q),
-        turned_by(c1, s1, t1, t1q),
-        new_diagonal(c1, s1, cross_next, d1, d1q),
-    )
+    return turned_by(c1, s1, w1, w1q), turned_by(c1, s1, t1, t1q), d2
 
 
 def turn_kernel(n_steps, n_cells, gram_ref, plan_ref, place_ref, modes_ref, mean_ref, energy_ref, c_ref, q_ref, index_ref, sign_ref):
@@ -152,7 +139,14 @@
     def rows_of(ref, *places):
         return [ref[pl.ds(p, 1), :] for p in places]
 
-    def one_round(round_index, carry):
+    arrivals = moved(lax.broadcasted_iota(jnp.int32, (8, cols), 1))
+    last = jnp.broadcast_to(table[n_steps - 1 : n_steps], (8, LANES))
+    last_places = [arrivals, gather(last, arrivals)] if tiles == 1 else [own_lane[0:8], last]
+    last_places = [x[0:1] for x in last_places]
+    last_sign = sign_of(*last_places)
+    arrivals = arrivals[0:1]
+
+    def sweep():
         kept = jnp.where(own_pair, c_ref[...], 0.0)
         w = kept[0:pair]
         for p in range(1, cols // pair):
@@ -161,7 +155,6 @@
         turned, energies = [], []
         for tile in range(tiles):
             at = slice(tile * LANES, (tile + 1) * LANES)
-            state = (w[:, at], start[:, at], d[:, at])
 
             def steps(k, state):
                 first = 2 * k
@@ -169,22 +162,27 @@
                 signs = rows_of(sign_ref, first, first + pair, first + 1)
                 return double_step(state, index, signs)
 
-            state = lax.fori_loop(0, n_steps // 2, steps, state)
-            if n_steps % 2:
-                state = single_step(state, rows_of(index_ref, n_steps - 1), rows_of(sign_ref, n_steps - 1))
-            turned.append(state[1])
-            energies.append(state[2])
-        t = moved(jnp.concatenate(turned, axis=1) if tiles > 1 else turned[0])
-        d = jnp.concatenate(energies, axis=1) if tiles > 1 else energies[0]
-        energy_ref[...] = moved(d)
-        lanes_from = moved(lax.broadcasted_iota(jnp.int32, (8, cols), 1))[0:1] // pair
-        whole = jnp.where(square_row // pair == lanes_from, jnp.concatenate([t] * (cols // pair), axis=0), 0.0)
+            begin = (w[:, at], start[:, at], d[:, at])
+            state = lax.fori_loop(0, n_steps // 2, steps, begin, unroll=5)
+            t, d_tile = last_step(state, last_places, last_sign)
+            turned.append(t)
+            energies.append(d_tile)
+        if tiles == 1:
+            t, energy_ref[...] = turned[0], energies[0]
+        else:
+            t, energy_ref[...] = moved(jnp.concatenate(turned, axis=1)), moved(jnp.concatenate(energies, axis=1))
+        whole = jnp.concatenate([t] * (cols // pair), axis=0)
+        return jnp.where(square_row // pair == arrivals // pair, whole, 0.0)
+
+    def one_round(round_index, carry):
+        whole = sweep()
         half_way = dot_full(c_ref[...], whole)
         c_ref[...] = dot_full(whole, half_way, 0, 0)
         q_ref[...] = dot_full(q_ref[...], whole)
         return carry
 
-    lax.fori_loop(0, ROUNDS, one_round, 0)
+    lax.fori_loop(0, ROUNDS - 1, one_round, 0)
+    q_ref[...] = dot_full(q_ref[...], sweep())
     place = place_ref[0]
     to_front = lax.rem(cols - place * pair, cols)
     mean_ref[...] = pltpu.roll(energy_ref[...], to_front, 1)[0:1, 0:pair] / n_cells

time: 57.6 us -> 54.9 us (0.953)
  Pallas kernels: 24.8 us -> 22.2 us
    pallas_call x1, Pallas kernels: 24.8 us -> 22.2 us  [turn_all(): pl.pallas_call(functools.partial(turn_kernel, n_steps, n_cells), out_shap...]
  transfers between devices with their start and end apart: 13 -> 13, of which waited for: 5 -> 5; matrix products, arithmetic and copies ran while one was open for 0% -> 0% of each run, Pallas kernels for 43% -> 40%
where the time goes in v4:
time: 54.9 us; the launch traced here: 54.8 us
  Pallas kernels  22.2 us (40%)
  starting transfers between devices  18.2 us (33%)
  waiting for transfers between devices  10.8 us (20%)
  matrix products  1.73 us (3%)
  local copies, waits for them, and re-layouts  1.01 us (2%)
  between operations  0.75 us (1%)
    pallas_call x1, Pallas kernels, turn_all(): pl.pallas_call(functools.partial(turn_kernel, n_steps, n_cells), out_shap...  22.2 us
    ppermute x13, starting transfers between devices, sent(): lax.ppermute(value, axis, [(i, i ^ toggle) for i in range(lax.axis_size(a...  18.2 us
    ppermute x13, waiting for transfers between devices, sent(): lax.ppermute(value, axis, [(i, i ^ toggle) for i in range(lax.axis_size(a...  10.8 us
    dot_general x1, matrix products, on_device(): lax.dot_general(modes, jnp.concatenate(blocks, axis=0), (((0,), (0,)), ((...  1.35 us
  transfers between devices with their start and end apart: 13, of which 5 were waited for; matrix products, arithmetic and copies ran while one was open for 0% of the time, Pallas kernels for 40%

profile of v4, /device:TPU:0, one launch (start us, length us, event | category | flops | bytes accessed | tf_op | source)
XLA Modules:
  0.0 54.8 jit_solution(12952165427529250775)
XLA Ops:
  0.7 1.0 %dynamic-slice_bitcast_fusion.4 = (f32[1,32,512]{2,1,0:T(8,128)S(1)}, f32[32,512]{1,0:T(8,128)S(1)}, f32[32,512]{1,0:T(8,128)S(1)}, f32[32,512]{1,0:T(8,128)S(1)}) fusion(f32[32,2048]{1,0:T(8,128)} %param.2, s32[]{:T(128)S(6)} %select_n.25, s32[]{:T(128)S(6)} %select_n.28, s32[]{:T(128)S(6)} %select_n.27, s32[]{:T(128)S(6)} %select_n.26), kind=kLoop, calls=%fused_computation.23 | loop fusion | bytes 524304 | tf_op jit(solution)/shard_map/stack | solution.py:242
  1.6 5.1 %collective-permute-start.2 = (f32[32,512]{1,0:T(8,128)S(1)}, f32[32,512]{1,0:T(8,128)S(1)}, u32[]{:S(2)}, u32[]{:S(2)}) collective-permute-start(f32[32,512]{1,0:T(8,128)S(1)} %get-tuple-element.15), channel_id=1, source_target_pairs={{0,3},{1,2},{2,1},{3,0},{4,7},{5,6},{6,5},{7,4},{8,11},{9,10},{10,... | collective-permute-start | bytes 196616 | tf_op jit(solution)/shard_map/ppermute | solution.py:223
  6.7 0.0 collective-permute-start.1
  6.7 0.6 %collective-permute-start = (f32[32,512]{1,0:T(8,128)S(1)}, f32[32,512]{1,0:T(8,128)S(1)}, u32[]{:S(2)}, u32[]{:S(2)}) collective-permute-start(f32[32,512]{1,0:T(8,128)S(1)} %get-tuple-element.17), channel_id=1, source_target_pairs={{0,1},{1,0},{2,3},{3,2},{4,5},{5,4},{6,7},{7,6},{8,9},{9,8},{10,11... | collective-permute-start | bytes 196616 | tf_op jit(solution)/shard_map/ppermute | solution.py:223
  7.4 1.9 %collective-permute-done.2 = f32[32,512]{1,0:T(8,128)S(1)} collective-permute-done((f32[32,512]{1,0:T(8,128)S(1)}, f32[32,512]{1,0:T(8,128)S(1)}, u32[]{:S(2)}, u32[]{:S(2)}) %collective-permute-start.2) | collective-permute-done | bytes 65568 | tf_op jit(solution)/shard_map/ppermute | solution.py:223
  9.3 3.0 %collective-permute-done.1 = f32[32,512]{1,0:T(8,128)S(1)} collective-permute-done((f32[32,512]{1,0:T(8,128)S(1)}, f32[32,512]{1,0:T(8,128)S(1)}, u32[]{:S(2)}, u32[]{:S(2)}) %collective-permute-start.1) | collective-permute-done | bytes 65568 | tf_op jit(solution)/shard_map/ppermute | solution.py:223
  12.3 0.0 collective-permute-done
  12.4 0.4 fusion.7
  12.8 0.0 copy-start
  12.8 0.1 collective-permute-start.3
  12.9 1.2 %collective-permute-done.3 = f32[128,128]{1,0:T(8,128)S(1)} collective-permute-done((f32[128,128]{1,0:T(8,128)S(1)}, f32[128,128]{1,0:T(8,128)S(1)}, u32[]{:S(2)}, u32[]{:S(2)}) %collective-permute-start.3) | collective-permute-done | bytes 65568 | tf_op jit(solution)/shard_map/ppermute | solution.py:223
  14.1 0.0 copy-start.1
  14.2 2.8 %collective-permute-start.6 = (f32[128,128]{1,0:T(8,128)S(1)}, f32[128,128]{1,0:T(8,128)S(1)}, u32[]{:S(2)}, u32[]{:S(2)}) collective-permute-start(f32[128,128]{1,0:T(8,128)S(1)} %add.54), channel_id=1, source_target_pairs={{0,3},{1,2},{2,1},{3,0},{4,7},{5,6},{6,5},{7,4},{8,11},{9,10},{10,... | collective-permute-start | bytes 196616 | tf_op jit(solution)/shard_map/ppermute | solution.py:223
  16.9 0.0 collective-permute-start.5
  16.9 1.7 %collective-permute-start.4 = (f32[128,128]{1,0:T(8,128)S(1)}, f32[128,128]{1,0:T(8,128)S(1)}, u32[]{:S(2)}, u32[]{:S(2)}) collective-permute-start(f32[128,128]{1,0:T(8,128)S(1)} %add.54), channel_id=1, source_target_pairs={{0,1},{1,0},{2,3},{3,2},{4,5},{5,4},{6,7},{7,6},{8,9},{9,8},{10,11... | collective-permute-start | bytes 196616 | tf_op jit(solution)/shard_map/ppermute | solution.py:223
  18.6 2.4 %collective-permute-done.6 = f32[128,128]{1,0:T(8,128)S(1)} collective-permute-done((f32[128,128]{1,0:T(8,128)S(1)}, f32[128,128]{1,0:T(8,128)S(1)}, u32[]{:S(2)}, u32[]{:S(2)}) %collective-permute-start.6) | collective-permute-done | bytes 65568 | tf_op jit(solution)/shard_map/ppermute | solution.py:223
  21.0 2.2 %collective-permute-done.5 = f32[128,128]{1,0:T(8,128)S(1)} collective-permute-done((f32[128,128]{1,0:T(8,128)S(1)}, f32[128,128]{1,0:T(8,128)S(1)}, u32[]{:S(2)}, u32[]{:S(2)}) %collective-permute-start.5) | collective-permute-done | bytes 65568 | tf_op jit(solution)/shard_map/ppermute | solution.py:223
  23.2 0.0 collective-permute-done.4
  23.2 2.5 %collective-permute-start.9 = (f32[128,128]{1,0:T(8,128)S(1)}, f32[128,128]{1,0:T(8,128)S(1)}, u32[]{:S(2)}, u32[]{:S(2)}) collective-permute-start(f32[128,128]{1,0:T(8,128)S(1)} %add_add_fusion.1), channel_id=1, source_target_pairs={{0,24},{4,28},{8,16},{12,20},{16,8},{20,12},{24,0},{28,4},{1,25},{... | collective-permute-start | bytes 196616 | tf_op jit(solution)/shard_map/ppermute | solution.py:223
  25.7 0.5 collective-permute-start.8
  26.3 0.5 collective-permute-start.7
  26.8 0.0 copy-done
  26.8 2.4 %collective-permute-start.12 = (f32[32,2048]{1,0:T(8,128)S(1)}, f32[32,2048]{1,0:T(8,128)S(1)}, u32[]{:S(2)}, u32[]{:S(2)}) collective-permute-start(f32[32,2048]{1,0:T(8,128)S(1)} %copy-done), channel_id=1, source_target_pairs={{0,3},{1,2},{2,1},{3,0},{4,7},{5,6},{6,5},{7,4},{8,11},{9,10},{10,... | collective-permute-start | bytes 786440 | tf_op jit(solution)/shard_map/ppermute | solution.py:223
  29.2 0.0 collective-permute-start.11
  29.2 0.0 collective-permute-done.9
  29.2 2.0 %collective-permute-start.10 = (f32[32,2048]{1,0:T(8,128)S(1)}, f32[32,2048]{1,0:T(8,128)S(1)}, u32[]{:S(2)}, u32[]{:S(2)}) collective-permute-start(f32[32,2048]{1,0:T(8,128)S(1)} %copy-done), channel_id=1, source_target_pairs={{0,1},{1,0},{2,3},{3,2},{4,5},{5,4},{6,7},{7,6},{8,9},{9,8},{10,11... | collective-permute-start | bytes 786440 | tf_op jit(solution)/shard_map/ppermute | solution.py:223
  31.2 0.0 copy-done.1
  31.2 0.0 collective-permute-done.8
  31.2 0.0 collective-permute-done.7
  31.2 22.2 %all_rounds.1 = (f32[128,32]{1,0:T(8,128)S(1)}, f32[1,32]{1,0:T(1,128)}) custom-call(f32[128,128]{1,0:T(8,128)S(1)} %add_add_fusion.gram_ref, s32[32,32]{1,0:T(8,128)S(1)} %pad_add_fusion.plan_ref, s32[1]{0:T(128)} %bitcast.8.place_ref), custom_call_target="tpu_custom_call" | custom-call | tf_op jit(solution)/shard_map/all_rounds/pallas_call | solution.py:202
  53.4 0.0 collective-permute-done.12
  53.4 0.0 collective-permute-done.11
  53.4 0.0 collective-permute-done.10
  53.4 1.4 %convolution_multiply_fusion = f32[32,2048]{1,0:T(8,128)} fusion(f32[128,32]{1,0:T(8,128)S(1)} %get-tuple-element.7, f32[32,2048]{1,0:T(8,128)S(1)} %collective-permute-done.12, f32[32,2048]{1,0:T(8,128)S(1)} %collective-permute-done.11, f32[32,2048]{1,0:T(8,128)S(1)} %collective-permute-done.10, f32[32,2048]{1,0:T(8,128)S(1)} %copy-done), kind=kOutput, calls=%fused_computation | convolution fusion | flops 101515264 | bytes 1327104 | tf_op jit(solution)/shard_map/dot_general | solution.py:252
  (7 shorter events, 0.1 us)
Async XLA Ops:
  1.6 7.7 %collective-permute-start.2 = (f32[32,512]{1,0:T(8,128)S(1)}, f32[32,512]{1,0:T(8,128)S(1)}, u32[]{:S(2)}, u32[]{:S(2)}) collective-permute-start(f32[32,512]{1,0:T(8,128)S(1)} %get-tuple-element.15), channel_id=1, source_target_pairs={{0,3},{1,2},{2,1},{3,0},{4,7},{5,6},{6,5},{7,4},{8,11},{9,10},{10,... | collective-permute-start | bytes 196616 | tf_op jit(solution)/shard_map/ppermute | solution.py:223
  6.7 5.6 %collective-permute-start.1 = (f32[32,512]{1,0:T(8,128)S(1)}, f32[32,512]{1,0:T(8,128)S(1)}, u32[]{:S(2)}, u32[]{:S(2)}) collective-permute-start(f32[32,512]{1,0:T(8,128)S(1)} %get-tuple-element.16), channel_id=1, source_target_pairs={{0,2},{1,3},{2,0},{3,1},{4,6},{5,7},{6,4},{7,5},{8,10},{9,11},{10,... | collective-permute-start | bytes 196616 | tf_op jit(solution)/shard_map/ppermute | solution.py:223
  6.7 5.6 %collective-permute-start = (f32[32,512]{1,0:T(8,128)S(1)}, f32[32,512]{1,0:T(8,128)S(1)}, u32[]{:S(2)}, u32[]{:S(2)}) collective-permute-start(f32[32,512]{1,0:T(8,128)S(1)} %get-tuple-element.17), channel_id=1, source_target_pairs={{0,1},{1,0},{2,3},{3,2},{4,5},{5,4},{6,7},{7,6},{8,9},{9,8},{10,11... | collective-permute-start | bytes 196616 | tf_op jit(solution)/shard_map/ppermute | solution.py:223
  12.8 14.0 %copy-start = (f32[32,2048]{1,0:T(8,128)S(1)}, f32[32,2048]{1,0:T(8,128)}, u32[]{:S(2)}) copy-start(f32[32,2048]{1,0:T(8,128)} %param.2) | copy-start | bytes 786436
  12.8 1.3 %collective-permute-start.3 = (f32[128,128]{1,0:T(8,128)S(1)}, f32[128,128]{1,0:T(8,128)S(1)}, u32[]{:S(2)}, u32[]{:S(2)}) collective-permute-start(f32[128,128]{1,0:T(8,128)S(1)} %fusion.7), channel_id=1, source_target_pairs={{0,4},{4,0},{8,12},{12,8},{16,20},{20,16},{24,28},{28,24},{1,5},{5... | collective-permute-start | bytes 196616 | tf_op jit(solution)/shard_map/ppermute | solution.py:223
  14.1 17.1 %copy-start.1 = (s32[31,32]{1,0:T(8,128)S(1)}, s32[31,32]{1,0:T(8,128)}, u32[]{:S(2)}) copy-start(s32[31,32]{1,0:T(8,128)} %param.3) | copy-start | bytes 11908
  14.2 6.8 %collective-permute-start.6 = (f32[128,128]{1,0:T(8,128)S(1)}, f32[128,128]{1,0:T(8,128)S(1)}, u32[]{:S(2)}, u32[]{:S(2)}) collective-permute-start(f32[128,128]{1,0:T(8,128)S(1)} %add.54), channel_id=1, source_target_pairs={{0,3},{1,2},{2,1},{3,0},{4,7},{5,6},{6,5},{7,4},{8,11},{9,10},{10,... | collective-permute-start | bytes 196616 | tf_op jit(solution)/shard_map/ppermute | solution.py:223
  16.9 6.3 %collective-permute-start.5 = (f32[128,128]{1,0:T(8,128)S(1)}, f32[128,128]{1,0:T(8,128)S(1)}, u32[]{:S(2)}, u32[]{:S(2)}) collective-permute-start(f32[128,128]{1,0:T(8,128)S(1)} %add.54), channel_id=1, source_target_pairs={{0,2},{1,3},{2,0},{3,1},{4,6},{5,7},{6,4},{7,5},{8,10},{9,11},{10,... | collective-permute-start | bytes 196616 | tf_op jit(solution)/shard_map/ppermute | solution.py:223
  16.9 6.3 %collective-permute-start.4 = (f32[128,128]{1,0:T(8,128)S(1)}, f32[128,128]{1,0:T(8,128)S(1)}, u32[]{:S(2)}, u32[]{:S(2)}) collective-permute-start(f32[128,128]{1,0:T(8,128)S(1)} %add.54), channel_id=1, source_target_pairs={{0,1},{1,0},{2,3},{3,2},{4,5},{5,4},{6,7},{7,6},{8,9},{9,8},{10,11... | collective-permute-start | bytes 196616 | tf_op jit(solution)/shard_map/ppermute | solution.py:223
  23.2 6.0 %collective-permute-start.9 = (f32[128,128]{1,0:T(8,128)S(1)}, f32[128,128]{1,0:T(8,128)S(1)}, u32[]{:S(2)}, u32[]{:S(2)}) collective-permute-start(f32[128,128]{1,0:T(8,128)S(1)} %add_add_fusion.1), channel_id=1, source_target_pairs={{0,24},{4,28},{8,16},{12,20},{16,8},{20,12},{24,0},{28,4},{1,25},{... | collective-permute-start | bytes 196616 | tf_op jit(solution)/shard_map/ppermute | solution.py:223
  25.7 5.5 %collective-permute-start.8 = (f32[128,128]{1,0:T(8,128)S(1)}, f32[128,128]{1,0:T(8,128)S(1)}, u32[]{:S(2)}, u32[]{:S(2)}) collective-permute-start(f32[128,128]{1,0:T(8,128)S(1)} %add_add_fusion.1), channel_id=1, source_target_pairs={{0,16},{4,20},{8,24},{12,28},{16,0},{20,4},{24,8},{28,12},{1,17},{... | collective-permute-start | bytes 196616 | tf_op jit(solution)/shard_map/ppermute | solution.py:223
  26.3 5.0 %collective-permute-start.7 = (f32[128,128]{1,0:T(8,128)S(1)}, f32[128,128]{1,0:T(8,128)S(1)}, u32[]{:S(2)}, u32[]{:S(2)}) collective-permute-start(f32[128,128]{1,0:T(8,128)S(1)} %add_add_fusion.1), channel_id=1, source_target_pairs={{0,8},{4,12},{8,0},{12,4},{16,24},{20,28},{24,16},{28,20},{1,9},{5... | collective-permute-start | bytes 196616 | tf_op jit(solution)/shard_map/ppermute | solution.py:223
  26.8 26.6 %collective-permute-start.12 = (f32[32,2048]{1,0:T(8,128)S(1)}, f32[32,2048]{1,0:T(8,128)S(1)}, u32[]{:S(2)}, u32[]{:S(2)}) collective-permute-start(f32[32,2048]{1,0:T(8,128)S(1)} %copy-done), channel_id=1, source_target_pairs={{0,3},{1,2},{2,1},{3,0},{4,7},{5,6},{6,5},{7,4},{8,11},{9,10},{10,... | collective-permute-start | bytes 786440 | tf_op jit(solution)/shard_map/ppermute | solution.py:223
  29.2 24.2 %collective-permute-start.11 = (f32[32,2048]{1,0:T(8,128)S(1)}, f32[32,2048]{1,0:T(8,128)S(1)}, u32[]{:S(2)}, u32[]{:S(2)}) collective-permute-start(f32[32,2048]{1,0:T(8,128)S(1)} %copy-done), channel_id=1, source_target_pairs={{0,2},{1,3},{2,0},{3,1},{4,6},{5,7},{6,4},{7,5},{8,10},{9,11},{10,... | collective-permute-start | bytes 786440 | tf_op jit(solution)/shard_map/ppermute | solution.py:223
  29.2 24.2 %collective-permute-start.10 = (f32[32,2048]{1,0:T(8,128)S(1)}, f32[32,2048]{1,0:T(8,128)S(1)}, u32[]{:S(2)}, u32[]{:S(2)}) collective-permute-start(f32[32,2048]{1,0:T(8,128)S(1)} %copy-done), channel_id=1, source_target_pairs={{0,1},{1,0},{2,3},{3,2},{4,5},{5,4},{6,7},{7,6},{8,9},{9,8},{10,11... | collective-permute-start | bytes 786440 | tf_op jit(solution)/shard_map/ppermute | solution.py:223

commit v5 on v4

--- a/solution.py
+++ b/solution.py
@@ -99,8 +99,18 @@
     return turned_by(c1, s1, w1, w1q), turned_by(c1, s1, t1, t1q), d2
 
 
+def unpacked(x):
+    cols = x.shape[1]
+    half, quarter = cols // 2, cols // 4
+    low = x[half:]
+    upper = jnp.concatenate([x[:half], low, pltpu.roll(low, 3 * quarter, 1)], axis=0)
+    row = lax.broadcasted_iota(jnp.int32, (cols, cols), 0) // quarter
+    lane = lax.broadcasted_iota(jnp.int32, (cols, cols), 1) // quarter
+    return jnp.where(lane >= row, upper, upper.T)
+
+
 def turn_kernel(n_steps, n_cells, gram_ref, plan_ref, place_ref, modes_ref, mean_ref, energy_ref, c_ref, q_ref, index_ref, sign_ref):
-    cols = gram_ref.shape[0]
+    cols = gram_ref.shape[1]
     pair = plan_ref.shape[1]
     half = pair // 2
     tiles = cols // LANES
@@ -111,7 +121,7 @@
     square_row = lax.broadcasted_iota(jnp.int32, (cols, cols), 0)
     square_lane = lax.broadcasted_iota(jnp.int32, (cols, cols), 1)
     own_pair = square_row // pair == square_lane // pair
-    c_ref[...] = gram_ref[...]
+    c_ref[...] = unpacked(gram_ref[...])
     q_ref[...] = (square_row == square_lane).astype(jnp.float32)
 
     own_lane = lax.broadcasted_iota(jnp.int32, (pair, LANES), 1)
@@ -196,7 +206,7 @@
 
 
 def turn_all(gram, plan, place, n_cells):
-    cols = gram.shape[0]
+    cols = gram.shape[1]
     n_steps, pair = plan.shape
     plan = jnp.concatenate([plan, jnp.arange(pair, dtype=jnp.int32)[None]], axis=0)
     return pl.pallas_call(
@@ -229,6 +239,13 @@
     return values[0]
 
 
+def packed(gram):
+    cols = gram.shape[0]
+    half, three = cols // 2, cols // 4 * 3
+    corner = jnp.concatenate([gram[three:, three:], jnp.zeros((cols - three, half - (cols - three)), gram.dtype)], axis=1)
+    return jnp.concatenate([gram[:half], jnp.concatenate([corner, gram[half:three, half:]], axis=1)], axis=0)
+
+
 def on_device(snapshots, plan):
     pair, cells = snapshots.shape
     n_blk, n_cell = lax.axis_size("blk"), lax.axis_size("cell")
@@ -243,6 +260,7 @@
     parts = [lax.dynamic_index_in_dim(parts, here ^ q, 0, keepdims=False) for q in range(n_blk)]
     whole = jnp.concatenate(parts, axis=0)
     gram = lax.dot_general(whole, whole, (((1,), (1,)), ((), ())), precision=lax.Precision.HIGHEST)
+    gram = packed(gram)
     gram = gram + sent(gram, "cell", 1)
     gram = tree_sum([gram] + [sent(gram, "blk", d) for d in range(1, n_blk)])
     gram, held = lax.optimization_barrier((gram, snapshots))
@@ -250,7 +268,7 @@
     gram = tree_sum([gram] + [sent(gram, "cell", d) for d in range(2, n_cell, 2)])
     modes, energy = turn_all(gram, plan, place, cells * n_cell)
     rotated = lax.dot_general(
-        modes, jnp.concatenate(blocks, axis=0), (((0,), (0,)), ((), ())), precision=lax.Precision.HIGHEST
+        modes, jnp.concatenate(blocks, axis=0), (((0,), (0,)), ((), ())), precision=lax.Precision.HIGH
     )
     return rotated * rotated, energy.reshape(pair)
 

time: 54.9 us -> 53.8 us (0.980)
  waiting for transfers between devices: 10.8 us -> 9.65 us
    ppermute x13, waiting for transfers between devices: 10.8 us -> 9.65 us  [sent(): lax.ppermute(value, axis, [(i, i ^ toggle) for i in range(lax.axis_size(a...]
  transfers between devices with their start and end apart: 13 -> 13, of which waited for: 5 -> 5; matrix products, arithmetic and copies ran while one was open for 0% -> 0% of each run, Pallas kernels for 40% -> 41%
where the time goes in v5:
time: 53.8 us; the launch traced here: 53.6 us
  Pallas kernels  22.2 us (41%)
  starting transfers between devices  18.1 us (34%)
  waiting for transfers between devices  9.65 us (18%)
  matrix products  1.56 us (3%)
  local copies, waits for them, and re-layouts  1.16 us (2%)
  between operations  0.74 us (1%)
    pallas_call x1, Pallas kernels, turn_all(): pl.pallas_call(functools.partial(turn_kernel, n_steps, n_cells), out_shap...  22.2 us
    ppermute x13, starting transfers between devices, sent(): lax.ppermute(value, axis, [(i, i ^ toggle) for i in range(lax.axis_size(a...  18.1 us
    ppermute x13, waiting for transfers between devices, sent(): lax.ppermute(value, axis, [(i, i ^ toggle) for i in range(lax.axis_size(a...  9.65 us
    dot_general x1, matrix products, on_device(): lax.dot_general(modes, jnp.concatenate(blocks, axis=0), (((0,), (0,)), ((...  1.18 us
  transfers between devices with their start and end apart: 13, of which 5 were waited for; matrix products, arithmetic and copies ran while one was open for 0% of the time, Pallas kernels for 41%

profile of v5, /device:TPU:0, one launch (start us, length us, event | category | flops | bytes accessed | tf_op | source)
XLA Modules:
  0.0 53.6 jit_solution(318213337635936383)
XLA Ops:
  0.7 1.0 %dynamic-slice_bitcast_fusion.4 = (f32[1,32,512]{2,1,0:T(8,128)S(1)}, f32[32,512]{1,0:T(8,128)S(1)}, f32[32,512]{1,0:T(8,128)S(1)}, f32[32,512]{1,0:T(8,128)S(1)}) fusion(f32[32,2048]{1,0:T(8,128)} %param.2, s32[]{:T(128)S(6)} %select_n.25, s32[]{:T(128)S(6)} %select_n.28, s32[]{:T(128)S(6)} %select_n.27, s32[]{:T(128)S(6)} %select_n.26), kind=kLoop, calls=%fused_computation.21 | loop fusion | bytes 524304 | tf_op jit(solution)/shard_map/stack | solution.py:259
  1.6 5.1 %collective-permute-start.2 = (f32[32,512]{1,0:T(8,128)S(1)}, f32[32,512]{1,0:T(8,128)S(1)}, u32[]{:S(2)}, u32[]{:S(2)}) collective-permute-start(f32[32,512]{1,0:T(8,128)S(1)} %get-tuple-element.15), channel_id=1, source_target_pairs={{0,3},{1,2},{2,1},{3,0},{4,7},{5,6},{6,5},{7,4},{8,11},{9,10},{10,... | collective-permute-start | bytes 196616 | tf_op jit(solution)/shard_map/ppermute | solution.py:233
  6.7 0.0 collective-permute-start.1
  6.7 0.6 %collective-permute-start = (f32[32,512]{1,0:T(8,128)S(1)}, f32[32,512]{1,0:T(8,128)S(1)}, u32[]{:S(2)}, u32[]{:S(2)}) collective-permute-start(f32[32,512]{1,0:T(8,128)S(1)} %get-tuple-element.17), channel_id=1, source_target_pairs={{0,1},{1,0},{2,3},{3,2},{4,5},{5,4},{6,7},{7,6},{8,9},{9,8},{10,11... | collective-permute-start | bytes 196616 | tf_op jit(solution)/shard_map/ppermute | solution.py:233
  7.4 1.9 %collective-permute-done.2 = f32[32,512]{1,0:T(8,128)S(1)} collective-permute-done((f32[32,512]{1,0:T(8,128)S(1)}, f32[32,512]{1,0:T(8,128)S(1)}, u32[]{:S(2)}, u32[]{:S(2)}) %collective-permute-start.2) | collective-permute-done | bytes 65568 | tf_op jit(solution)/shard_map/ppermute | solution.py:233
  9.3 3.0 %collective-permute-done.1 = f32[32,512]{1,0:T(8,128)S(1)} collective-permute-done((f32[32,512]{1,0:T(8,128)S(1)}, f32[32,512]{1,0:T(8,128)S(1)}, u32[]{:S(2)}, u32[]{:S(2)}) %collective-permute-start.1) | collective-permute-done | bytes 65568 | tf_op jit(solution)/shard_map/ppermute | solution.py:233
  12.3 0.0 collective-permute-done
  12.4 0.4 fusion.7
  12.8 0.1 slice.14
  12.9 0.1 slice.13
  12.9 0.0 copy-start
  13.0 0.1 maximum_maximum_fusion
  13.0 0.0 collective-permute-start.3
  13.1 1.2 %collective-permute-done.3 = f32[96,128]{1,0:T(8,128)S(1)} collective-permute-done((f32[96,128]{1,0:T(8,128)S(1)}, f32[96,128]{1,0:T(8,128)S(1)}, u32[]{:S(2)}, u32[]{:S(2)}) %collective-permute-start.3) | collective-permute-done | bytes 49184 | tf_op jit(solution)/shard_map/ppermute | solution.py:233
  14.3 0.1 fusion.18
  14.4 0.0 copy-start.1
  14.4 2.7 %collective-permute-start.6 = (f32[96,128]{1,0:T(8,128)S(1)}, f32[96,128]{1,0:T(8,128)S(1)}, u32[]{:S(2)}, u32[]{:S(2)}) collective-permute-start(f32[96,128]{1,0:T(8,128)S(1)} %fusion.18), channel_id=1, source_target_pairs={{0,3},{1,2},{2,1},{3,0},{4,7},{5,6},{6,5},{7,4},{8,11},{9,10},{10,... | collective-permute-start | bytes 147464 | tf_op jit(solution)/shard_map/ppermute | solution.py:233
  17.1 0.0 collective-permute-start.5
  17.1 1.7 %collective-permute-start.4 = (f32[96,128]{1,0:T(8,128)S(1)}, f32[96,128]{1,0:T(8,128)S(1)}, u32[]{:S(2)}, u32[]{:S(2)}) collective-permute-start(f32[96,128]{1,0:T(8,128)S(1)} %fusion.18), channel_id=1, source_target_pairs={{0,1},{1,0},{2,3},{3,2},{4,5},{5,4},{6,7},{7,6},{8,9},{9,8},{10,11... | collective-permute-start | bytes 147464 | tf_op jit(solution)/shard_map/ppermute | solution.py:233
  18.8 1.8 %collective-permute-done.6 = f32[96,128]{1,0:T(8,128)S(1)} collective-permute-done((f32[96,128]{1,0:T(8,128)S(1)}, f32[96,128]{1,0:T(8,128)S(1)}, u32[]{:S(2)}, u32[]{:S(2)}) %collective-permute-start.6) | collective-permute-done | bytes 49184 | tf_op jit(solution)/shard_map/ppermute | solution.py:233
  20.6 1.6 %collective-permute-done.5 = f32[96,128]{1,0:T(8,128)S(1)} collective-permute-done((f32[96,128]{1,0:T(8,128)S(1)}, f32[96,128]{1,0:T(8,128)S(1)}, u32[]{:S(2)}, u32[]{:S(2)}) %collective-permute-start.5) | collective-permute-done | bytes 49184 | tf_op jit(solution)/shard_map/ppermute | solution.py:233
  22.2 0.0 collective-permute-done.4
  22.2 2.5 %collective-permute-start.9 = (f32[96,128]{1,0:T(8,128)S(1)}, f32[96,128]{1,0:T(8,128)S(1)}, u32[]{:S(2)}, u32[]{:S(2)}) collective-permute-start(f32[96,128]{1,0:T(8,128)S(1)} %add_add_fusion.1), channel_id=1, source_target_pairs={{0,24},{4,28},{8,16},{12,20},{16,8},{20,12},{24,0},{28,4},{1,25},{... | collective-permute-start | bytes 147464 | tf_op jit(solution)/shard_map/ppermute | solution.py:233
  24.8 0.5 collective-permute-start.8
  25.3 0.5 collective-permute-start.7
  25.8 0.0 copy-done
  25.8 2.5 %collective-permute-start.12 = (f32[32,2048]{1,0:T(8,128)S(1)}, f32[32,2048]{1,0:T(8,128)S(1)}, u32[]{:S(2)}, u32[]{:S(2)}) collective-permute-start(f32[32,2048]{1,0:T(8,128)S(1)} %copy-done), channel_id=1, source_target_pairs={{0,3},{1,2},{2,1},{3,0},{4,7},{5,6},{6,5},{7,4},{8,11},{9,10},{10,... | collective-permute-start | bytes 786440 | tf_op jit(solution)/shard_map/ppermute | solution.py:233
  28.3 0.0 collective-permute-start.11
  28.3 0.0 collective-permute-done.9
  28.3 1.9 %collective-permute-start.10 = (f32[32,2048]{1,0:T(8,128)S(1)}, f32[32,2048]{1,0:T(8,128)S(1)}, u32[]{:S(2)}, u32[]{:S(2)}) collective-permute-start(f32[32,2048]{1,0:T(8,128)S(1)} %copy-done), channel_id=1, source_target_pairs={{0,1},{1,0},{2,3},{3,2},{4,5},{5,4},{6,7},{7,6},{8,9},{9,8},{10,11... | collective-permute-start | bytes 786440 | tf_op jit(solution)/shard_map/ppermute | solution.py:233
  30.2 0.0 copy-done.1
  30.2 0.0 collective-permute-done.8
  30.2 0.0 collective-permute-done.7
  30.3 22.2 %all_rounds.1 = (f32[128,32]{1,0:T(8,128)S(1)}, f32[1,32]{1,0:T(1,128)}) custom-call(f32[96,128]{1,0:T(8,128)S(1)} %add_add_fusion.gram_ref, s32[32,32]{1,0:T(8,128)S(1)} %pad_add_fusion.plan_ref, s32[1]{0:T(128)} %bitcast.8.place_ref), custom_call_target="tpu_custom_call" | custom-call | tf_op jit(solution)/shard_map/all_rounds/pallas_call | solution.py:212
  52.4 0.0 collective-permute-done.12
  52.4 0.0 collective-permute-done.11
  52.4 0.0 collective-permute-done.10
  52.4 1.2 %convolution_multiply_fusion = f32[32,2048]{1,0:T(8,128)} fusion(f32[128,32]{1,0:T(8,128)S(1)} %get-tuple-element.7, f32[32,2048]{1,0:T(8,128)S(1)} %collective-permute-done.12, f32[32,2048]{1,0:T(8,128)S(1)} %collective-permute-done.11, f32[32,2048]{1,0:T(8,128)S(1)} %collective-permute-done.10, f32[32,2048]{1,0:T(8,128)S(1)} %copy-done), kind=kOutput, calls=%fused_computation | convolution fusion | flops 51183616 | bytes 1327104 | tf_op jit(solution)/shard_map/dot_general | solution.py:270
  (8 shorter events, 0.1 us)
Async XLA Ops:
  1.6 7.7 %collective-permute-start.2 = (f32[32,512]{1,0:T(8,128)S(1)}, f32[32,512]{1,0:T(8,128)S(1)}, u32[]{:S(2)}, u32[]{:S(2)}) collective-permute-start(f32[32,512]{1,0:T(8,128)S(1)} %get-tuple-element.15), channel_id=1, source_target_pairs={{0,3},{1,2},{2,1},{3,0},{4,7},{5,6},{6,5},{7,4},{8,11},{9,10},{10,... | collective-permute-start | bytes 196616 | tf_op jit(solution)/shard_map/ppermute | solution.py:233
  6.7 5.6 %collective-permute-start.1 = (f32[32,512]{1,0:T(8,128)S(1)}, f32[32,512]{1,0:T(8,128)S(1)}, u32[]{:S(2)}, u32[]{:S(2)}) collective-permute-start(f32[32,512]{1,0:T(8,128)S(1)} %get-tuple-element.16), channel_id=1, source_target_pairs={{0,2},{1,3},{2,0},{3,1},{4,6},{5,7},{6,4},{7,5},{8,10},{9,11},{10,... | collective-permute-start | bytes 196616 | tf_op jit(solution)/shard_map/ppermute | solution.py:233
  6.7 5.6 %collective-permute-start = (f32[32,512]{1,0:T(8,128)S(1)}, f32[32,512]{1,0:T(8,128)S(1)}, u32[]{:S(2)}, u32[]{:S(2)}) collective-permute-start(f32[32,512]{1,0:T(8,128)S(1)} %get-tuple-element.17), channel_id=1, source_target_pairs={{0,1},{1,0},{2,3},{3,2},{4,5},{5,4},{6,7},{7,6},{8,9},{9,8},{10,11... | collective-permute-start | bytes 196616 | tf_op jit(solution)/shard_map/ppermute | solution.py:233
  12.9 12.9 %copy-start = (f32[32,2048]{1,0:T(8,128)S(1)}, f32[32,2048]{1,0:T(8,128)}, u32[]{:S(2)}) copy-start(f32[32,2048]{1,0:T(8,128)} %param.2) | copy-start | bytes 786436
  13.0 1.2 %collective-permute-start.3 = (f32[96,128]{1,0:T(8,128)S(1)}, f32[96,128]{1,0:T(8,128)S(1)}, u32[]{:S(2)}, u32[]{:S(2)}) collective-permute-start(f32[96,128]{1,0:T(8,128)S(1)} %maximum_maximum_fusion), channel_id=1, source_target_pairs={{0,4},{4,0},{8,12},{12,8},{16,20},{20,16},{24,28},{28,24},{1,5},{5... | collective-permute-start | bytes 147464 | tf_op jit(solution)/shard_map/ppermute | solution.py:233
  14.4 15.8 %copy-start.1 = (s32[31,32]{1,0:T(8,128)S(1)}, s32[31,32]{1,0:T(8,128)}, u32[]{:S(2)}) copy-start(s32[31,32]{1,0:T(8,128)} %param.3) | copy-start | bytes 11908
  14.4 6.2 %collective-permute-start.6 = (f32[96,128]{1,0:T(8,128)S(1)}, f32[96,128]{1,0:T(8,128)S(1)}, u32[]{:S(2)}, u32[]{:S(2)}) collective-permute-start(f32[96,128]{1,0:T(8,128)S(1)} %fusion.18), channel_id=1, source_target_pairs={{0,3},{1,2},{2,1},{3,0},{4,7},{5,6},{6,5},{7,4},{8,11},{9,10},{10,... | collective-permute-start | bytes 147464 | tf_op jit(solution)/shard_map/ppermute | solution.py:233
  17.1 5.1 %collective-permute-start.5 = (f32[96,128]{1,0:T(8,128)S(1)}, f32[96,128]{1,0:T(8,128)S(1)}, u32[]{:S(2)}, u32[]{:S(2)}) collective-permute-start(f32[96,128]{1,0:T(8,128)S(1)} %fusion.18), channel_id=1, source_target_pairs={{0,2},{1,3},{2,0},{3,1},{4,6},{5,7},{6,4},{7,5},{8,10},{9,11},{10,... | collective-permute-start | bytes 147464 | tf_op jit(solution)/shard_map/ppermute | solution.py:233
  17.1 5.1 %collective-permute-start.4 = (f32[96,128]{1,0:T(8,128)S(1)}, f32[96,128]{1,0:T(8,128)S(1)}, u32[]{:S(2)}, u32[]{:S(2)}) collective-permute-start(f32[96,128]{1,0:T(8,128)S(1)} %fusion.18), channel_id=1, source_target_pairs={{0,1},{1,0},{2,3},{3,2},{4,5},{5,4},{6,7},{7,6},{8,9},{9,8},{10,11... | collective-permute-start | bytes 147464 | tf_op jit(solution)/shard_map/ppermute | solution.py:233
  22.2 6.1 %collective-permute-start.9 = (f32[96,128]{1,0:T(8,128)S(1)}, f32[96,128]{1,0:T(8,128)S(1)}, u32[]{:S(2)}, u32[]{:S(2)}) collective-permute-start(f32[96,128]{1,0:T(8,128)S(1)} %add_add_fusion.1), channel_id=1, source_target_pairs={{0,24},{4,28},{8,16},{12,20},{16,8},{20,12},{24,0},{28,4},{1,25},{... | collective-permute-start | bytes 147464 | tf_op jit(solution)/shard_map/ppermute | solution.py:233
  24.8 5.5 %collective-permute-start.8 = (f32[96,128]{1,0:T(8,128)S(1)}, f32[96,128]{1,0:T(8,128)S(1)}, u32[]{:S(2)}, u32[]{:S(2)}) collective-permute-start(f32[96,128]{1,0:T(8,128)S(1)} %add_add_fusion.1), channel_id=1, source_target_pairs={{0,16},{4,20},{8,24},{12,28},{16,0},{20,4},{24,8},{28,12},{1,17},{... | collective-permute-start | bytes 147464 | tf_op jit(solution)/shard_map/ppermute | solution.py:233
  25.3 5.0 %collective-permute-start.7 = (f32[96,128]{1,0:T(8,128)S(1)}, f32[96,128]{1,0:T(8,128)S(1)}, u32[]{:S(2)}, u32[]{:S(2)}) collective-permute-start(f32[96,128]{1,0:T(8,128)S(1)} %add_add_fusion.1), channel_id=1, source_target_pairs={{0,8},{4,12},{8,0},{12,4},{16,24},{20,28},{24,16},{28,20},{1,9},{5... | collective-permute-start | bytes 147464 | tf_op jit(solution)/shard_map/ppermute | solution.py:233
  25.8 26.6 %collective-permute-start.12 = (f32[32,2048]{1,0:T(8,128)S(1)}, f32[32,2048]{1,0:T(8,128)S(1)}, u32[]{:S(2)}, u32[]{:S(2)}) collective-permute-start(f32[32,2048]{1,0:T(8,128)S(1)} %copy-done), channel_id=1, source_target_pairs={{0,3},{1,2},{2,1},{3,0},{4,7},{5,6},{6,5},{7,4},{8,11},{9,10},{10,... | collective-permute-start | bytes 786440 | tf_op jit(solution)/shard_map/ppermute | solution.py:233
  28.3 24.1 %collective-permute-start.11 = (f32[32,2048]{1,0:T(8,128)S(1)}, f32[32,2048]{1,0:T(8,128)S(1)}, u32[]{:S(2)}, u32[]{:S(2)}) collective-permute-start(f32[32,2048]{1,0:T(8,128)S(1)} %copy-done), channel_id=1, source_target_pairs={{0,2},{1,3},{2,0},{3,1},{4,6},{5,7},{6,4},{7,5},{8,10},{9,11},{10,... | collective-permute-start | bytes 786440 | tf_op jit(solution)/shard_map/ppermute | solution.py:233
  28.3 24.1 %collective-permute-start.10 = (f32[32,2048]{1,0:T(8,128)S(1)}, f32[32,2048]{1,0:T(8,128)S(1)}, u32[]{:S(2)}, u32[]{:S(2)}) collective-permute-start(f32[32,2048]{1,0:T(8,128)S(1)} %copy-done), channel_id=1, source_target_pairs={{0,1},{1,0},{2,3},{3,2},{4,5},{5,4},{6,7},{7,6},{8,9},{9,8},{10,11... | collective-permute-start | bytes 786440 | tf_op jit(solution)/shard_map/ppermute | solution.py:233

commit v6 on v5

v6 whole, which is shorter than its diff:
```python
import functools

import jax
import jax.numpy as jnp
from jax import lax
from jax.experimental import pallas as pl
from jax.experimental.pallas import tpu as pltpu
from jax.sharding import PartitionSpec as P

ROUNDS = 7
TINY_SQUARE = 2.0**-78
UP = 2.0**80
FLOOR = 2.0**-124
FLOOR_ROOT = 2.0**-62
LANES = 128


def split3(x):
    high = x.astype(jnp.bfloat16)
    rest = x - high.astype(jnp.float32)
    middle = rest.astype(jnp.bfloat16)
    low = (rest - middle.astype(jnp.float32)).astype(jnp.bfloat16)
    return high, middle, low


def dot_full(a, b, contract_a=1, contract_b=0):
    a0, a1, a2 = split3(a)
    b0, b1, b2 = split3(b)

    def one(x, y):
        return lax.dot_general(
            x, y, (((contract_a,), (contract_b,)), ((), ())), preferred_element_type=jnp.float32
        )

    small = one(a0, b2) + one(a2, b0) + one(a1, b1)
    return one(a0, b0) + ((one(a0, b1) + one(a1, b0)) + small)


def turning(twice_cross, own, other, sign):
    spread = (own - other) * sign
    up_cross, up_spread = twice_cross * UP, spread * UP
    square = spread * spread + twice_cross * twice_cross
    up_square = (up_spread * up_spread + FLOOR) + up_cross * up_cross
    is_small = square < TINY_SQUARE
    norm_square = jnp.where(is_small, up_square, square)
    size = jnp.maximum(jnp.abs(jnp.where(is_small, up_spread, spread)), FLOOR_ROOT)
    cross = jnp.where(is_small, up_cross, twice_cross) * sign
    half_norm = norm_square * jnp.where(is_small, (0.5 / UP) * sign, 0.5 * sign)
    cross_sign = jnp.where(twice_cross < 0, -sign, sign)
    in_order = spread >= 0
    inverse = lax.rsqrt(norm_square)
    large = size * inverse + 1.0
    double = (size + size) * inverse + 2.0
    small = cross * inverse
    u = jnp.where(in_order, large, jnp.abs(small))
    v = jnp.where(in_order, small, cross_sign * large)
    return u, v, lax.rsqrt(double), 0.5 * (own + other) + half_norm * inverse


def gather(x, index):
    return jnp.take_along_axis(x, jnp.broadcast_to(index, x.shape), axis=1)


def tall(x, like):
    return jnp.concatenate([x] * (like.shape[0] // x.shape[0]), axis=0)


def turned_by(c, s, x, y):
    return tall(c, x) * x + tall(s, x) * y


def product(x, y):
    return jnp.sum(x * y, axis=0, keepdims=True)


def last_step(state, places, sign):
    z, t, d = state
    (zi, ti, di), (zp, tp, dp) = [[gather(x, place) for x in (z, t, d)] for place in places]
    u, v, f, d = turning(product(zi, zp), di, dp, sign)
    return turned_by(u * f, v * f, ti, tp), d


def double_step(state, index_tile, sign_tile):
    z, zc, d = state
    p, q, pq = [index_tile[k : k + 1] for k in range(3)]
    sign, sign_q, sign_next = [sign_tile[k : k + 1] for k in range(3)]
    zp, zq, zpq = gather(z, p), gather(z, q), gather(z, pq)
    diagonals = jnp.take_along_axis(d, index_tile, axis=1)
    dp, dq, dpq = [jnp.broadcast_to(diagonals[k : k + 1], d.shape) for k in range(3)]
    zcq, zcp, zcpq = gather(zc, q), gather(zc, p), gather(zc, pq)
    u, v, f, d1 = turning(product(z, zp), d, dp, sign)
    uq, vq, fq, d1q = turning(product(zq, zpq), dq, dpq, sign_q)
    e00, e11 = product(z, zq), product(zp, zpq)
    e01, e10 = product(zc, zpq), product(zp, zcq)
    cross = (f * fq) * (((u * uq) * e00 + (v * vq) * e11) + ((u * vq) * e01 + (v * uq) * e10))
    u1, v1, f1, d2 = turning(cross, d1, d1q, sign_next)
    c, s, cq, sq = u * f, v * f, uq * fq, vq * fq
    c1, s1 = u1 * f1, v1 * f1
    z1, zc1 = turned_by(c, s, z, zcp), turned_by(c, s, zc, zp)
    zq1, zcq1 = turned_by(cq, sq, zq, zcpq), turned_by(cq, sq, zcq, zpq)
    return turned_by(c1, s1, z1, zcq1), turned_by(c1, s1, zc1, zq1), d2


def moved(x, pair):
    cols, half = x.shape[1], pair // 2
    place = lax.broadcasted_iota(jnp.int32, x.shape, 1)
    is_upper = place % pair < half
    from_own = (place < half) & is_upper
    shifted = ((place // pair == 1) & is_upper) | (place >= cols - half)
    right, left, by_half = pltpu.roll(x, pair, 1), pltpu.roll(x, cols - pair, 1), pltpu.roll(x, half, 1)
    return jnp.where(from_own, x, jnp.where(shifted, by_half, jnp.where(is_upper, right, left)))


def unpacked(x):
    cols = x.shape[1]
    half, quarter = cols // 2, cols // 4
    low = x[half:]
    upper = jnp.concatenate([x[:half], low, pltpu.roll(low, 3 * quarter, 1)], axis=0)
    row = lax.broadcasted_iota(jnp.int32, (cols, cols), 0) // quarter
    lane = lax.broadcasted_iota(jnp.int32, (cols, cols), 1) // quarter
    return jnp.where(lane >= row, upper, upper.T)


def sign_of(own, other):
    return jnp.where(own < other, 1.0, -1.0).astype(jnp.float32)


def table_kernel(plan_ref, index_ref, sign_ref, table_ref):
    pair = plan_ref.shape[1]
    doubles = pair // 2
    table = plan_ref[...]
    table_ref[...] = jnp.concatenate([table + pair * g for g in range(LANES // pair)], axis=1)
    first = table_ref[pl.ds(0, doubles, stride=2), :]
    second = table_ref[pl.ds(1, doubles, stride=2), :]
    own = lax.broadcasted_iota(jnp.int32, (doubles, LANES), 1)
    first_of_second = jnp.take_along_axis(first, second, axis=1)
    around = jnp.take_along_axis(second, first, axis=1)
    least = own
    reach = 1
    while reach < doubles:
        least = jnp.minimum(least, jnp.take_along_axis(least, around, axis=1))
        around = jnp.take_along_axis(around, around, axis=1)
        reach *= 2
    colour = sign_of(least, jnp.take_along_axis(least, first, axis=1))
    lower = sign_of(own, first)
    is_last = lax.broadcasted_iota(jnp.int32, (doubles, LANES), 0) == doubles - 1
    colour = jnp.where(is_last, lower, colour)
    signs = [lower, sign_of(second, first_of_second), sign_of(own, second), colour]
    for k in range(doubles):
        at = slice(k, k + 1)
        index_ref[k] = jnp.concatenate([first[at], second[at]] + [first_of_second[at]] * 6, axis=0)
        sign_ref[k] = jnp.concatenate([x[at] for x in signs] + [lower[at]] * 4, axis=0)


def turn_kernel(n_cells, gram_ref, index_ref, sign_ref, place_ref, modes_ref, mean_ref, energy_ref, c_ref, q_ref):
    cols = gram_ref.shape[1]
    doubles = index_ref.shape[0]
    pair = 2 * doubles
    tiles = cols // LANES
    square_row = lax.broadcasted_iota(jnp.int32, (cols, cols), 0)
    square_lane = lax.broadcasted_iota(jnp.int32, (cols, cols), 1)
    own_pair = square_row // pair == square_lane // pair
    is_diag = (square_row == square_lane % pair)[0:pair]
    start = jnp.where(is_diag, 2.0, 0.0)
    c_ref[...] = unpacked(gram_ref[...])
    q_ref[...] = (square_row == square_lane).astype(jnp.float32)

    arrivals = moved(lax.broadcasted_iota(jnp.int32, (8, cols), 1), pair)
    last = jnp.broadcast_to(index_ref[doubles - 1][0:1], (8, LANES))
    if tiles == 1:
        last_places = [arrivals, gather(last, arrivals)]
    else:
        last_places = [lax.broadcasted_iota(jnp.int32, (8, LANES), 1), last]
    last_places = [x[0:1] for x in last_places]
    last_sign = sign_of(*last_places)
    arrivals = arrivals[0:1]

    def colour_of(k):
        return sign_ref[k][3:4]

    def sweep():
        kept = jnp.where(own_pair, c_ref[...], 0.0)
        w = kept[0:pair]
        for p in range(1, cols // pair):
            w = w + kept[p * pair : (p + 1) * pair]
        d = jnp.broadcast_to(jnp.sum(jnp.where(is_diag, w, 0.0), axis=0, keepdims=True), (8, cols))
        turned, energies = [], []
        for tile in range(tiles):
            at = slice(tile * LANES, (tile + 1) * LANES)
            held = colour_of(0) > 0
            z, zc = jnp.where(held, w[:, at], start[:, at]), jnp.where(held, start[:, at], w[:, at])
            d_tile = d[:, at]
            for k in range(doubles - 1):
                z, zc, d_tile = double_step((z, zc, d_tile), index_ref[k], sign_ref[k])
                same = colour_of(k) * colour_of(k + 1) > 0
                z, zc = jnp.where(same, z, zc), jnp.where(same, zc, z)
            t = jnp.where(colour_of(doubles - 1) > 0, zc, z)
            t, d_tile = last_step((z, t, d_tile), last_places, last_sign)
            turned.append(t)
            energies.append(d_tile)
        if tiles == 1:
            t, energy_ref[...] = turned[0], energies[0]
        else:
            energy_ref[...] = moved(jnp.concatenate(energies, axis=1), pair)
            t = moved(jnp.concatenate(turned, axis=1), pair)
        whole = jnp.concatenate([0.5 * t] * (cols // pair), axis=0)
        return jnp.where(square_row // pair == arrivals // pair, whole, 0.0)

    def one_round(round_index, carry):
        whole = sweep()
        half_way = dot_full(c_ref[...], whole)
        c_ref[...] = dot_full(whole, half_way, 0, 0)
        q_ref[...] = dot_full(q_ref[...], whole)
        return carry

    lax.fori_loop(0, ROUNDS - 1, one_round, 0)
    q_ref[...] = dot_full(q_ref[...], sweep())
    place = place_ref[0]
    to_front = lax.rem(cols - place * pair, cols)
    mean_ref[...] = pltpu.roll(energy_ref[...], to_front, 1)[0:1, 0:pair] / n_cells
    for d in range(cols // pair):
        rows = q_ref[pl.ds(pl.multiple_of((place ^ d) * pair, pair), pair), :]
        modes_ref[d * pair : (d + 1) * pair] = pltpu.roll(rows, to_front, 1)[:, 0:pair]


def in_vmem(n):
    return [pl.BlockSpec(memory_space=pltpu.VMEM)] * n


def tables_of(plan):
    n_steps, pair = plan.shape
    plan = jnp.concatenate([plan, jnp.arange(pair, dtype=jnp.int32)[None]], axis=0)
    shape = ((n_steps + 1) // 2, 8, LANES)
    return pl.pallas_call(
        table_kernel,
        out_shape=(jax.ShapeDtypeStruct(shape, jnp.int32), jax.ShapeDtypeStruct(shape, jnp.float32)),
        in_specs=in_vmem(1),
        out_specs=in_vmem(2),
        scratch_shapes=[pltpu.VMEM((n_steps + 1, LANES), jnp.int32)],
        name="step_tables",
    )(plan)


def turn_all(gram, tables, place, n_cells):
    cols = gram.shape[1]
    pair = 2 * tables[0].shape[0]
    return pl.pallas_call(
        functools.partial(turn_kernel, n_cells),
        out_shape=(
            jax.ShapeDtypeStruct((cols, pair), jnp.float32),
            jax.ShapeDtypeStruct((1, pair), jnp.float32),
        ),
        in_specs=in_vmem(3) + [pl.BlockSpec(memory_space=pltpu.SMEM)],
        out_specs=in_vmem(2),
        scratch_shapes=[
            pltpu.VMEM((8, cols), jnp.float32),
            pltpu.VMEM((cols, cols), jnp.float32),
            pltpu.VMEM((cols, cols), jnp.float32),
        ],
        compiler_params=pltpu.CompilerParams(vmem_limit_bytes=48 * 1024 * 1024),
        name="all_rounds",
    )(gram, *tables, place)


def sent(value, axis, toggle):
    return lax.ppermute(value, axis, [(i, i ^ toggle) for i in range(lax.axis_size(axis))])


def tree_sum(values):
    while len(values) > 1:
        values = [a + b for a, b in zip(values[::2], values[1::2])]
    return values[0]


def packed(gram):
    cols = gram.shape[0]
    half, three = cols // 2, cols // 4 * 3
    corner = jnp.concatenate([gram[three:, three:], jnp.zeros((cols - three, half - (cols - three)), gram.dtype)], axis=1)
    return jnp.concatenate([gram[:half], jnp.concatenate([corner, gram[half:three, half:]], axis=1)], axis=0)


def on_device(snapshots, plan):
    pair, cells = snapshots.shape
    n_blk, n_cell = lax.axis_size("blk"), lax.axis_size("cell")
    here = lax.axis_index("blk")
    place = here.astype(jnp.int32)[None]
    part = cells // n_blk

    def part_for(d):
        return lax.dynamic_slice_in_dim(snapshots, (here ^ d) * part, part, 1)

    parts = jnp.stack([part_for(0)] + [sent(part_for(d), "blk", d) for d in range(1, n_blk)])
    parts = [lax.dynamic_index_in_dim(parts, here ^ q, 0, keepdims=False) for q in range(n_blk)]
    tables, parts = lax.optimization_barrier((tables_of(plan), parts))
    whole = jnp.concatenate(parts, axis=0)
    gram = lax.dot_general(whole, whole, (((1,), (1,)), ((), ())), precision=lax.Precision.HIGHEST)
    gram = packed(gram)
    gram = gram + sent(gram, "cell", 1)
    gram = tree_sum([gram] + [sent(gram, "blk", d) for d in range(1, n_blk)])
    gram, held = lax.optimization_barrier((gram, snapshots))
    blocks = [snapshots] + [sent(held, "blk", d) for d in range(1, n_blk)]
    gram = tree_sum([gram] + [sent(gram, "cell", d) for d in range(2, n_cell, 2)])
    modes, energy = turn_all(gram, tables, place, cells * n_cell)
    rotated = lax.dot_general(
        modes, jnp.concatenate(blocks, axis=0), (((0,), (0,)), ((), ())), precision=lax.Precision.HIGH
    )
    return rotated * rotated, energy.reshape(pair)


def solution(mesh):
    return jax.shard_map(
        on_device,
        mesh=mesh,
        in_specs=(P("blk", "cell"), P()),
        out_specs=(P("blk", "cell"), P("blk")),
        check_vma=False,
    )
```

time: 53.8 us -> 50.8 us (0.944)
  waiting for transfers between devices: 9.65 us -> 7.21 us
  Pallas kernels: 22.2 us -> 20.9 us
  other arithmetic: 0.21 us -> 0.81 us
    ppermute x13, waiting for transfers between devices: 9.65 us -> 7.21 us  [sent(): lax.ppermute(value, axis, [(i, i ^ toggle) for i in range(lax.axis_size(a...]
    pallas_call x1 -> x2, Pallas kernels: 22.2 us -> 20.9 us  [the longest x1 19.1 us: turn_all(): pl.pallas_call(functools.partial(turn_kernel, n_cells), out_shape=(jax.Sh...]
    concatenate x1, other arithmetic: 0.01 us -> 0.6 us  [tables_of(): jnp.concatenate([plan, jnp.arange(pair, dtype=jnp.int32)[None]], axis=0)]
  transfers between devices with their start and end apart: 13 -> 13, of which waited for: 5 -> 4; matrix products, arithmetic and copies ran while one was open for 0% -> 1% of each run, Pallas kernels for 41% -> 41%
where the time goes in v6:
time: 50.8 us; the launch traced here: 50.5 us
  Pallas kernels  20.9 us (41%)
  starting transfers between devices  18.1 us (36%)
  waiting for transfers between devices  7.21 us (14%)
  matrix products  1.56 us (3%)
  local copies, waits for them, and re-layouts  1.17 us (2%)
  other arithmetic  0.81 us (2%)
  between operations  0.76 us (1%)
    pallas_call x1, Pallas kernels, turn_all(): pl.pallas_call(functools.partial(turn_kernel, n_cells), out_shape=(jax.Sh...  19.1 us
    ppermute x13, starting transfers between devices, sent(): lax.ppermute(value, axis, [(i, i ^ toggle) for i in range(lax.axis_size(a...  18.1 us
    ppermute x13, waiting for transfers between devices, sent(): lax.ppermute(value, axis, [(i, i ^ toggle) for i in range(lax.axis_size(a...  7.21 us
    pallas_call x1, Pallas kernels, tables_of(): pl.pallas_call(table_kernel, out_shape=(jax.ShapeDtypeStruct(shape, jnp.i...  1.85 us
    dot_general x1, matrix products, on_device(): lax.dot_general(modes, jnp.concatenate(blocks, axis=0), (((0,), (0,)), ((...  1.18 us
  transfers between devices with their start and end apart: 13, of which 4 were waited for; matrix products, arithmetic and copies ran while one was open for 1% of the time, Pallas kernels for 41%

profile of v6, /device:TPU:0, one launch (start us, length us, event | category | flops | bytes accessed | tf_op | source)
XLA Modules:
  0.0 50.5 jit_solution(5350697563179696853)
XLA Ops:
  0.7 1.0 %dynamic-slice_bitcast_fusion.4 = (f32[1,32,512]{2,1,0:T(8,128)S(1)}, f32[32,512]{1,0:T(8,128)S(1)}, f32[32,512]{1,0:T(8,128)S(1)}, f32[32,512]{1,0:T(8,128)S(1)}) fusion(f32[32,2048]{1,0:T(8,128)} %param.2, s32[]{:T(128)S(6)} %select_n.25, s32[]{:T(128)S(6)} %select_n.28, s32[]{:T(128)S(6)} %select_n.27, s32[]{:T(128)S(6)} %select_n.26), kind=kLoop, calls=%fused_computation.21 | loop fusion | bytes 524304 | tf_op jit(solution)/shard_map/stack | solution.py:292
  1.6 0.0 copy-start.3
  1.6 5.1 %collective-permute-start.2 = (f32[32,512]{1,0:T(8,128)S(1)}, f32[32,512]{1,0:T(8,128)S(1)}, u32[]{:S(2)}, u32[]{:S(2)}) collective-permute-start(f32[32,512]{1,0:T(8,128)S(1)} %get-tuple-element.31), channel_id=1, source_target_pairs={{0,3},{1,2},{2,1},{3,0},{4,7},{5,6},{6,5},{7,4},{8,11},{9,10},{10,... | collective-permute-start | bytes 196616 | tf_op jit(solution)/shard_map/ppermute | solution.py:266
  6.8 0.0 collective-permute-start.1
  6.8 0.6 %collective-permute-start = (f32[32,512]{1,0:T(8,128)S(1)}, f32[32,512]{1,0:T(8,128)S(1)}, u32[]{:S(2)}, u32[]{:S(2)}) collective-permute-start(f32[32,512]{1,0:T(8,128)S(1)} %get-tuple-element.33), channel_id=1, source_target_pairs={{0,1},{1,0},{2,3},{3,2},{4,5},{5,4},{6,7},{7,6},{8,9},{9,8},{10,11... | collective-permute-start | bytes 196616 | tf_op jit(solution)/shard_map/ppermute | solution.py:266
  7.4 0.0 copy-done.3
  7.4 0.6 %pad_add_fusion.plan_ref = s32[32,32]{1,0:T(8,128)} fusion(s32[1,32]{1,0:T(1,128)S(1)} %iota.4, s32[31,32]{1,0:T(8,128)S(1)} %copy-done.3), kind=kLoop, calls=%fused_computation.25 | loop fusion | flops 1024 | bytes 8192 | tf_op jit(solution)/shard_map/concatenate | solution.py:232
  8.0 1.9 %step_tables.1 = (s32[16,8,128]{2,1,0:T(8,128)}, f32[16,8,128]{2,1,0:T(8,128)}) custom-call(s32[32,32]{1,0:T(8,128)} %pad_add_fusion.plan_ref), custom_call_target="tpu_custom_call" | custom-call | tf_op jit(solution)/shard_map/step_tables/pallas_call | solution.py:234
  9.9 0.0 collective-permute-done.2
  9.9 2.5 %collective-permute-done.1 = f32[32,512]{1,0:T(8,128)S(1)} collective-permute-done((f32[32,512]{1,0:T(8,128)S(1)}, f32[32,512]{1,0:T(8,128)S(1)}, u32[]{:S(2)}, u32[]{:S(2)}) %collective-permute-start.1) | collective-permute-done | bytes 65568 | tf_op jit(solution)/shard_map/ppermute | solution.py:266
  12.4 0.0 collective-permute-done
  12.4 0.4 fusion.7
  12.8 0.1 slice.14
  12.9 0.1 slice.13
  13.0 0.0 copy-start.2
  13.0 0.1 maximum_maximum_fusion
  13.0 0.0 collective-permute-start.3
  13.1 1.2 %collective-permute-done.3 = f32[96,128]{1,0:T(8,128)S(1)} collective-permute-done((f32[96,128]{1,0:T(8,128)S(1)}, f32[96,128]{1,0:T(8,128)S(1)}, u32[]{:S(2)}, u32[]{:S(2)}) %collective-permute-start.3) | collective-permute-done | bytes 49184 | tf_op jit(solution)/shard_map/ppermute | solution.py:266
  14.3 0.1 fusion.18
  14.4 2.7 %collective-permute-start.6 = (f32[96,128]{1,0:T(8,128)S(1)}, f32[96,128]{1,0:T(8,128)S(1)}, u32[]{:S(2)}, u32[]{:S(2)}) collective-permute-start(f32[96,128]{1,0:T(8,128)S(1)} %fusion.18), channel_id=1, source_target_pairs={{0,3},{1,2},{2,1},{3,0},{4,7},{5,6},{6,5},{7,4},{8,11},{9,10},{10,... | collective-permute-start | bytes 147464 | tf_op jit(solution)/shard_map/ppermute | solution.py:266
  17.1 0.0 collective-permute-start.5
  17.1 1.7 %collective-permute-start.4 = (f32[96,128]{1,0:T(8,128)S(1)}, f32[96,128]{1,0:T(8,128)S(1)}, u32[]{:S(2)}, u32[]{:S(2)}) collective-permute-start(f32[96,128]{1,0:T(8,128)S(1)} %fusion.18), channel_id=1, source_target_pairs={{0,1},{1,0},{2,3},{3,2},{4,5},{5,4},{6,7},{7,6},{8,9},{9,8},{10,11... | collective-permute-start | bytes 147464 | tf_op jit(solution)/shard_map/ppermute | solution.py:266
  18.8 1.8 %collective-permute-done.6 = f32[96,128]{1,0:T(8,128)S(1)} collective-permute-done((f32[96,128]{1,0:T(8,128)S(1)}, f32[96,128]{1,0:T(8,128)S(1)}, u32[]{:S(2)}, u32[]{:S(2)}) %collective-permute-start.6) | collective-permute-done | bytes 49184 | tf_op jit(solution)/shard_map/ppermute | solution.py:266
  20.6 1.6 %collective-permute-done.5 = f32[96,128]{1,0:T(8,128)S(1)} collective-permute-done((f32[96,128]{1,0:T(8,128)S(1)}, f32[96,128]{1,0:T(8,128)S(1)}, u32[]{:S(2)}, u32[]{:S(2)}) %collective-permute-start.5) | collective-permute-done | bytes 49184 | tf_op jit(solution)/shard_map/ppermute | solution.py:266
  22.2 0.0 collective-permute-done.4
  22.2 0.0 copy-start
  22.2 0.0 copy-start.1
  22.3 2.5 %collective-permute-start.9 = (f32[96,128]{1,0:T(8,128)S(1)}, f32[96,128]{1,0:T(8,128)S(1)}, u32[]{:S(2)}, u32[]{:S(2)}) collective-permute-start(f32[96,128]{1,0:T(8,128)S(1)} %add_add_fusion.1), channel_id=1, source_target_pairs={{0,24},{4,28},{8,16},{12,20},{16,8},{20,12},{24,0},{28,4},{1,25},{... | collective-permute-start | bytes 147464 | tf_op jit(solution)/shard_map/ppermute | solution.py:266
  24.8 0.5 %collective-permute-start.8 = (f32[96,128]{1,0:T(8,128)S(1)}, f32[96,128]{1,0:T(8,128)S(1)}, u32[]{:S(2)}, u32[]{:S(2)}) collective-permute-start(f32[96,128]{1,0:T(8,128)S(1)} %add_add_fusion.1), channel_id=1, source_target_pairs={{0,16},{4,20},{8,24},{12,28},{16,0},{20,4},{24,8},{28,12},{1,17},{... | collective-permute-start | bytes 147464 | tf_op jit(solution)/shard_map/ppermute | solution.py:266
  25.3 0.5 %collective-permute-start.7 = (f32[96,128]{1,0:T(8,128)S(1)}, f32[96,128]{1,0:T(8,128)S(1)}, u32[]{:S(2)}, u32[]{:S(2)}) collective-permute-start(f32[96,128]{1,0:T(8,128)S(1)} %add_add_fusion.1), channel_id=1, source_target_pairs={{0,8},{4,12},{8,0},{12,4},{16,24},{20,28},{24,16},{28,20},{1,9},{5... | collective-permute-start | bytes 147464 | tf_op jit(solution)/shard_map/ppermute | solution.py:266
  25.8 0.0 copy-done.2
  25.8 2.5 %collective-permute-start.12 = (f32[32,2048]{1,0:T(8,128)S(1)}, f32[32,2048]{1,0:T(8,128)S(1)}, u32[]{:S(2)}, u32[]{:S(2)}) collective-permute-start(f32[32,2048]{1,0:T(8,128)S(1)} %copy-done.2), channel_id=1, source_target_pairs={{0,3},{1,2},{2,1},{3,0},{4,7},{5,6},{6,5},{7,4},{8,11},{9,10},{10,... | collective-permute-start | bytes 786440 | tf_op jit(solution)/shard_map/ppermute | solution.py:266
  28.3 0.0 collective-permute-start.11
  28.3 0.0 collective-permute-done.9
  28.3 1.9 %collective-permute-start.10 = (f32[32,2048]{1,0:T(8,128)S(1)}, f32[32,2048]{1,0:T(8,128)S(1)}, u32[]{:S(2)}, u32[]{:S(2)}) collective-permute-start(f32[32,2048]{1,0:T(8,128)S(1)} %copy-done.2), channel_id=1, source_target_pairs={{0,1},{1,0},{2,3},{3,2},{4,5},{5,4},{6,7},{7,6},{8,9},{9,8},{10,11... | collective-permute-start | bytes 786440 | tf_op jit(solution)/shard_map/ppermute | solution.py:266
  30.2 0.0 collective-permute-done.8
  30.2 0.0 collective-permute-done.7
  30.2 0.0 copy-done
  30.2 0.0 copy-done.1
  30.3 19.1 %all_rounds.1 = (f32[128,32]{1,0:T(8,128)S(1)}, f32[1,32]{1,0:T(1,128)}) custom-call(f32[96,128]{1,0:T(8,128)S(1)} %add_add_fusion.gram_ref, s32[16,8,128]{2,1,0:T(8,128)S(1)} %copy-done, f32[16,8,128]{2,1,0:T(8,128)S(1)} %copy-done.1, s32[1]{0:T(128)} %bitcast.8.place_ref), custom_call_target="tpu_custom_call" | custom-call | tf_op jit(solution)/shard_map/all_rounds/pallas_call | solution.py:247
  49.3 0.0 collective-permute-done.12
  49.3 0.0 collective-permute-done.11
  49.3 0.0 collective-permute-done.10
  49.3 1.2 %convolution_multiply_fusion = f32[32,2048]{1,0:T(8,128)} fusion(f32[128,32]{1,0:T(8,128)S(1)} %get-tuple-element.23, f32[32,2048]{1,0:T(8,128)S(1)} %collective-permute-done.12, f32[32,2048]{1,0:T(8,128)S(1)} %collective-permute-done.11, f32[32,2048]{1,0:T(8,128)S(1)} %collective-permute-done.10, f32[32,2048]{1,0:T(8,128)S(1)} %copy-done.2), kind=kOutput, calls=%fused_computation | convolution fusion | flops 51183616 | bytes 1327104 | tf_op jit(solution)/shard_map/dot_general | solution.py:304
  (7 shorter events, 0.1 us)
Async XLA Ops:
  1.6 5.8 %copy-start.3 = (s32[31,32]{1,0:T(8,128)S(1)}, s32[31,32]{1,0:T(8,128)}, u32[]{:S(2)}) copy-start(s32[31,32]{1,0:T(8,128)} %param.3) | copy-start | bytes 11908
  1.6 8.2 %collective-permute-start.2 = (f32[32,512]{1,0:T(8,128)S(1)}, f32[32,512]{1,0:T(8,128)S(1)}, u32[]{:S(2)}, u32[]{:S(2)}) collective-permute-start(f32[32,512]{1,0:T(8,128)S(1)} %get-tuple-element.31), channel_id=1, source_target_pairs={{0,3},{1,2},{2,1},{3,0},{4,7},{5,6},{6,5},{7,4},{8,11},{9,10},{10,... | collective-permute-start | bytes 196616 | tf_op jit(solution)/shard_map/ppermute | solution.py:266
  6.8 5.6 %collective-permute-start.1 = (f32[32,512]{1,0:T(8,128)S(1)}, f32[32,512]{1,0:T(8,128)S(1)}, u32[]{:S(2)}, u32[]{:S(2)}) collective-permute-start(f32[32,512]{1,0:T(8,128)S(1)} %get-tuple-element.32), channel_id=1, source_target_pairs={{0,2},{1,3},{2,0},{3,1},{4,6},{5,7},{6,4},{7,5},{8,10},{9,11},{10,... | collective-permute-start | bytes 196616 | tf_op jit(solution)/shard_map/ppermute | solution.py:266
  6.8 5.6 %collective-permute-start = (f32[32,512]{1,0:T(8,128)S(1)}, f32[32,512]{1,0:T(8,128)S(1)}, u32[]{:S(2)}, u32[]{:S(2)}) collective-permute-start(f32[32,512]{1,0:T(8,128)S(1)} %get-tuple-element.33), channel_id=1, source_target_pairs={{0,1},{1,0},{2,3},{3,2},{4,5},{5,4},{6,7},{7,6},{8,9},{9,8},{10,11... | collective-permute-start | bytes 196616 | tf_op jit(solution)/shard_map/ppermute | solution.py:266
  13.0 12.9 %copy-start.2 = (f32[32,2048]{1,0:T(8,128)S(1)}, f32[32,2048]{1,0:T(8,128)}, u32[]{:S(2)}) copy-start(f32[32,2048]{1,0:T(8,128)} %param.2) | copy-start | bytes 786436
  13.0 1.2 %collective-permute-start.3 = (f32[96,128]{1,0:T(8,128)S(1)}, f32[96,128]{1,0:T(8,128)S(1)}, u32[]{:S(2)}, u32[]{:S(2)}) collective-permute-start(f32[96,128]{1,0:T(8,128)S(1)} %maximum_maximum_fusion), channel_id=1, source_target_pairs={{0,4},{4,0},{8,12},{12,8},{16,20},{20,16},{24,28},{28,24},{1,5},{5... | collective-permute-start | bytes 147464 | tf_op jit(solution)/shard_map/ppermute | solution.py:266
  14.4 6.2 %collective-permute-start.6 = (f32[96,128]{1,0:T(8,128)S(1)}, f32[96,128]{1,0:T(8,128)S(1)}, u32[]{:S(2)}, u32[]{:S(2)}) collective-permute-start(f32[96,128]{1,0:T(8,128)S(1)} %fusion.18), channel_id=1, source_target_pairs={{0,3},{1,2},{2,1},{3,0},{4,7},{5,6},{6,5},{7,4},{8,11},{9,10},{10,... | collective-permute-start | bytes 147464 | tf_op jit(solution)/shard_map/ppermute | solution.py:266
  17.1 5.1 %collective-permute-start.5 = (f32[96,128]{1,0:T(8,128)S(1)}, f32[96,128]{1,0:T(8,128)S(1)}, u32[]{:S(2)}, u32[]{:S(2)}) collective-permute-start(f32[96,128]{1,0:T(8,128)S(1)} %fusion.18), channel_id=1, source_target_pairs={{0,2},{1,3},{2,0},{3,1},{4,6},{5,7},{6,4},{7,5},{8,10},{9,11},{10,... | collective-permute-start | bytes 147464 | tf_op jit(solution)/shard_map/ppermute | solution.py:266
  17.1 5.1 %collective-permute-start.4 = (f32[96,128]{1,0:T(8,128)S(1)}, f32[96,128]{1,0:T(8,128)S(1)}, u32[]{:S(2)}, u32[]{:S(2)}) collective-permute-start(f32[96,128]{1,0:T(8,128)S(1)} %fusion.18), channel_id=1, source_target_pairs={{0,1},{1,0},{2,3},{3,2},{4,5},{5,4},{6,7},{7,6},{8,9},{9,8},{10,11... | collective-permute-start | bytes 147464 | tf_op jit(solution)/shard_map/ppermute | solution.py:266
  22.2 8.0 %copy-start = (s32[16,8,128]{2,1,0:T(8,128)S(1)}, s32[16,8,128]{2,1,0:T(8,128)}, u32[]{:S(2)}) copy-start(s32[16,8,128]{2,1,0:T(8,128)} %get-tuple-element.21.index_ref) | copy-start | bytes 196612
  22.2 8.0 %copy-start.1 = (f32[16,8,128]{2,1,0:T(8,128)S(1)}, f32[16,8,128]{2,1,0:T(8,128)}, u32[]{:S(2)}) copy-start(f32[16,8,128]{2,1,0:T(8,128)} %get-tuple-element.22.sign_ref) | copy-start | bytes 196612
  22.3 6.1 %collective-permute-start.9 = (f32[96,128]{1,0:T(8,128)S(1)}, f32[96,128]{1,0:T(8,128)S(1)}, u32[]{:S(2)}, u32[]{:S(2)}) collective-permute-start(f32[96,128]{1,0:T(8,128)S(1)} %add_add_fusion.1), channel_id=1, source_target_pairs={{0,24},{4,28},{8,16},{12,20},{16,8},{20,12},{24,0},{28,4},{1,25},{... | collective-permute-start | bytes 147464 | tf_op jit(solution)/shard_map/ppermute | solution.py:266
  24.8 5.4 %collective-permute-start.8 = (f32[96,128]{1,0:T(8,128)S(1)}, f32[96,128]{1,0:T(8,128)S(1)}, u32[]{:S(2)}, u32[]{:S(2)}) collective-permute-start(f32[96,128]{1,0:T(8,128)S(1)} %add_add_fusion.1), channel_id=1, source_target_pairs={{0,16},{4,20},{8,24},{12,28},{16,0},{20,4},{24,8},{28,12},{1,17},{... | collective-permute-start | bytes 147464 | tf_op jit(solution)/shard_map/ppermute | solution.py:266
  25.3 4.9 %collective-permute-start.7 = (f32[96,128]{1,0:T(8,128)S(1)}, f32[96,128]{1,0:T(8,128)S(1)}, u32[]{:S(2)}, u32[]{:S(2)}) collective-permute-start(f32[96,128]{1,0:T(8,128)S(1)} %add_add_fusion.1), channel_id=1, source_target_pairs={{0,8},{4,12},{8,0},{12,4},{16,24},{20,28},{24,16},{28,20},{1,9},{5... | collective-permute-start | bytes 147464 | tf_op jit(solution)/shard_map/ppermute | solution.py:266
  25.8 23.5 %collective-permute-start.12 = (f32[32,2048]{1,0:T(8,128)S(1)}, f32[32,2048]{1,0:T(8,128)S(1)}, u32[]{:S(2)}, u32[]{:S(2)}) collective-permute-start(f32[32,2048]{1,0:T(8,128)S(1)} %copy-done.2), channel_id=1, source_target_pairs={{0,3},{1,2},{2,1},{3,0},{4,7},{5,6},{6,5},{7,4},{8,11},{9,10},{10,... | collective-permute-start | bytes 786440 | tf_op jit(solution)/shard_map/ppermute | solution.py:266
  28.3 21.0 %collective-permute-start.11 = (f32[32,2048]{1,0:T(8,128)S(1)}, f32[32,2048]{1,0:T(8,128)S(1)}, u32[]{:S(2)}, u32[]{:S(2)}) collective-permute-start(f32[32,2048]{1,0:T(8,128)S(1)} %copy-done.2), channel_id=1, source_target_pairs={{0,2},{1,3},{2,0},{3,1},{4,6},{5,7},{6,4},{7,5},{8,10},{9,11},{10,... | collective-permute-start | bytes 786440 | tf_op jit(solution)/shard_map/ppermute | solution.py:266
  28.3 21.0 %collective-permute-start.10 = (f32[32,2048]{1,0:T(8,128)S(1)}, f32[32,2048]{1,0:T(8,128)S(1)}, u32[]{:S(2)}, u32[]{:S(2)}) collective-permute-start(f32[32,2048]{1,0:T(8,128)S(1)} %copy-done.2), channel_id=1, source_target_pairs={{0,1},{1,0},{2,3},{3,2},{4,5},{5,4},{6,7},{7,6},{8,9},{9,8},{10,11... | collective-permute-start | bytes 786440 | tf_op jit(solution)/shard_map/ppermute | solution.py:266

commit v7 on v6

--- a/solution.py
+++ b/solution.py
@@ -80,7 +80,7 @@
     return turned_by(u * f, v * f, ti, tp), d
 
 
-def double_step(state, index_tile, sign_tile):
+def double_step(state, index_tile, sign_tile, same):
     z, zc, d = state
     p, q, pq = [index_tile[k : k + 1] for k in range(3)]
     sign, sign_q, sign_next = [sign_tile[k : k + 1] for k in range(3)]
@@ -95,10 +95,12 @@
     cross = (f * fq) * (((u * uq) * e00 + (v * vq) * e11) + ((u * vq) * e01 + (v * uq) * e10))
     u1, v1, f1, d2 = turning(cross, d1, d1q, sign_next)
     c, s, cq, sq = u * f, v * f, uq * fq, vq * fq
-    c1, s1 = u1 * f1, v1 * f1
     z1, zc1 = turned_by(c, s, z, zcp), turned_by(c, s, zc, zp)
     zq1, zcq1 = turned_by(cq, sq, zq, zcpq), turned_by(cq, sq, zcq, zpq)
-    return turned_by(c1, s1, z1, zcq1), turned_by(c1, s1, zc1, zq1), d2
+    own, other = jnp.where(same, z1, zc1), jnp.where(same, zcq1, zq1)
+    own_c, other_c = jnp.where(same, zc1, z1), jnp.where(same, zq1, zcq1)
+    f1 = tall(f1, z)
+    return f1 * turned_by(u1, v1, own, other), f1 * turned_by(u1, v1, own_c, other_c), d2
 
 
 def moved(x, pair):
@@ -191,9 +193,8 @@
             z, zc = jnp.where(held, w[:, at], start[:, at]), jnp.where(held, start[:, at], w[:, at])
             d_tile = d[:, at]
             for k in range(doubles - 1):
-                z, zc, d_tile = double_step((z, zc, d_tile), index_ref[k], sign_ref[k])
                 same = colour_of(k) * colour_of(k + 1) > 0
-                z, zc = jnp.where(same, z, zc), jnp.where(same, zc, z)
+                z, zc, d_tile = double_step((z, zc, d_tile), index_ref[k], sign_ref[k], same)
             t = jnp.where(colour_of(doubles - 1) > 0, zc, z)
             t, d_tile = last_step((z, t, d_tile), last_places, last_sign)
             turned.append(t)

time: 50.8 us -> 50.8 us (level)
  transfers between devices with their start and end apart: 13 -> 13, of which waited for: 4 -> 5; matrix products, arithmetic and copies ran while one was open for 1% -> 1% of each run, Pallas kernels for 41% -> 41%
where the time goes in v7:
time: 50.8 us; the launch traced here: 50.5 us
  Pallas kernels  20.6 us (41%)
  starting transfers between devices  18.1 us (36%)
  waiting for transfers between devices  7.52 us (15%)
  matrix products  1.56 us (3%)
  local copies, waits for them, and re-layouts  1.17 us (2%)
  other arithmetic  0.81 us (2%)
  between operations  0.76 us (1%)
    pallas_call x1, Pallas kernels, turn_all(): pl.pallas_call(functools.partial(turn_kernel, n_cells), out_shape=(jax.Sh...  18.8 us
    ppermute x13, starting transfers between devices, sent(): lax.ppermute(value, axis, [(i, i ^ toggle) for i in range(lax.axis_size(a...  18.1 us
    ppermute x13, waiting for transfers between devices, sent(): lax.ppermute(value, axis, [(i, i ^ toggle) for i in range(lax.axis_size(a...  7.52 us
    pallas_call x1, Pallas kernels, tables_of(): pl.pallas_call(table_kernel, out_shape=(jax.ShapeDtypeStruct(shape, jnp.i...  1.85 us
    dot_general x1, matrix products, on_device(): lax.dot_general(modes, jnp.concatenate(blocks, axis=0), (((0,), (0,)), ((...  1.18 us
  transfers between devices with their start and end apart: 13, of which 5 were waited for; matrix products, arithmetic and copies ran while one was open for 1% of the time, Pallas kernels for 41%

profile of v7, /device:TPU:0, one launch (start us, length us, event | category | flops | bytes accessed | tf_op | source)
XLA Modules:
  0.0 50.5 jit_solution(18062542748772313283)
XLA Ops:
  0.7 1.0 %dynamic-slice_bitcast_fusion.4 = (f32[1,32,512]{2,1,0:T(8,128)S(1)}, f32[32,512]{1,0:T(8,128)S(1)}, f32[32,512]{1,0:T(8,128)S(1)}, f32[32,512]{1,0:T(8,128)S(1)}) fusion(f32[32,2048]{1,0:T(8,128)} %param.2, s32[]{:T(128)S(6)} %select_n.25, s32[]{:T(128)S(6)} %select_n.28, s32[]{:T(128)S(6)} %select_n.27, s32[]{:T(128)S(6)} %select_n.26), kind=kLoop, calls=%fused_computation.21 | loop fusion | bytes 524304 | tf_op jit(solution)/shard_map/stack | solution.py:293
  1.6 0.0 copy-start.3
  1.6 5.1 %collective-permute-start.2 = (f32[32,512]{1,0:T(8,128)S(1)}, f32[32,512]{1,0:T(8,128)S(1)}, u32[]{:S(2)}, u32[]{:S(2)}) collective-permute-start(f32[32,512]{1,0:T(8,128)S(1)} %get-tuple-element.31), channel_id=1, source_target_pairs={{0,3},{1,2},{2,1},{3,0},{4,7},{5,6},{6,5},{7,4},{8,11},{9,10},{10,... | collective-permute-start | bytes 196616 | tf_op jit(solution)/shard_map/ppermute | solution.py:267
  6.8 0.0 collective-permute-start.1
  6.8 0.6 %collective-permute-start = (f32[32,512]{1,0:T(8,128)S(1)}, f32[32,512]{1,0:T(8,128)S(1)}, u32[]{:S(2)}, u32[]{:S(2)}) collective-permute-start(f32[32,512]{1,0:T(8,128)S(1)} %get-tuple-element.33), channel_id=1, source_target_pairs={{0,1},{1,0},{2,3},{3,2},{4,5},{5,4},{6,7},{7,6},{8,9},{9,8},{10,11... | collective-permute-start | bytes 196616 | tf_op jit(solution)/shard_map/ppermute | solution.py:267
  7.4 0.0 copy-done.3
  7.4 0.6 %pad_add_fusion.plan_ref = s32[32,32]{1,0:T(8,128)} fusion(s32[1,32]{1,0:T(1,128)S(1)} %iota.4, s32[31,32]{1,0:T(8,128)S(1)} %copy-done.3), kind=kLoop, calls=%fused_computation.25 | loop fusion | flops 1024 | bytes 8192 | tf_op jit(solution)/shard_map/concatenate | solution.py:233
  8.0 1.9 %step_tables.1 = (s32[16,8,128]{2,1,0:T(8,128)}, f32[16,8,128]{2,1,0:T(8,128)}) custom-call(s32[32,32]{1,0:T(8,128)} %pad_add_fusion.plan_ref), custom_call_target="tpu_custom_call" | custom-call | tf_op jit(solution)/shard_map/step_tables/pallas_call | solution.py:235
  9.9 0.0 collective-permute-done.2
  9.9 2.5 %collective-permute-done.1 = f32[32,512]{1,0:T(8,128)S(1)} collective-permute-done((f32[32,512]{1,0:T(8,128)S(1)}, f32[32,512]{1,0:T(8,128)S(1)}, u32[]{:S(2)}, u32[]{:S(2)}) %collective-permute-start.1) | collective-permute-done | bytes 65568 | tf_op jit(solution)/shard_map/ppermute | solution.py:267
  12.4 0.0 collective-permute-done
  12.4 0.4 fusion.7
  12.8 0.1 slice.14
  12.9 0.1 slice.13
  13.0 0.0 copy-start.2
  13.0 0.1 maximum_maximum_fusion
  13.0 0.0 collective-permute-start.3
  13.1 1.2 %collective-permute-done.3 = f32[96,128]{1,0:T(8,128)S(1)} collective-permute-done((f32[96,128]{1,0:T(8,128)S(1)}, f32[96,128]{1,0:T(8,128)S(1)}, u32[]{:S(2)}, u32[]{:S(2)}) %collective-permute-start.3) | collective-permute-done | bytes 49184 | tf_op jit(solution)/shard_map/ppermute | solution.py:267
  14.3 0.1 fusion.18
  14.4 2.7 %collective-permute-start.6 = (f32[96,128]{1,0:T(8,128)S(1)}, f32[96,128]{1,0:T(8,128)S(1)}, u32[]{:S(2)}, u32[]{:S(2)}) collective-permute-start(f32[96,128]{1,0:T(8,128)S(1)} %fusion.18), channel_id=1, source_target_pairs={{0,3},{1,2},{2,1},{3,0},{4,7},{5,6},{6,5},{7,4},{8,11},{9,10},{10,... | collective-permute-start | bytes 147464 | tf_op jit(solution)/shard_map/ppermute | solution.py:267
  17.1 0.0 collective-permute-start.5
  17.1 1.7 %collective-permute-start.4 = (f32[96,128]{1,0:T(8,128)S(1)}, f32[96,128]{1,0:T(8,128)S(1)}, u32[]{:S(2)}, u32[]{:S(2)}) collective-permute-start(f32[96,128]{1,0:T(8,128)S(1)} %fusion.18), channel_id=1, source_target_pairs={{0,1},{1,0},{2,3},{3,2},{4,5},{5,4},{6,7},{7,6},{8,9},{9,8},{10,11... | collective-permute-start | bytes 147464 | tf_op jit(solution)/shard_map/ppermute | solution.py:267
  18.8 1.8 %collective-permute-done.6 = f32[96,128]{1,0:T(8,128)S(1)} collective-permute-done((f32[96,128]{1,0:T(8,128)S(1)}, f32[96,128]{1,0:T(8,128)S(1)}, u32[]{:S(2)}, u32[]{:S(2)}) %collective-permute-start.6) | collective-permute-done | bytes 49184 | tf_op jit(solution)/shard_map/ppermute | solution.py:267
  20.6 1.6 %collective-permute-done.5 = f32[96,128]{1,0:T(8,128)S(1)} collective-permute-done((f32[96,128]{1,0:T(8,128)S(1)}, f32[96,128]{1,0:T(8,128)S(1)}, u32[]{:S(2)}, u32[]{:S(2)}) %collective-permute-start.5) | collective-permute-done | bytes 49184 | tf_op jit(solution)/shard_map/ppermute | solution.py:267
  22.2 0.0 collective-permute-done.4
  22.2 0.0 copy-start
  22.2 0.0 copy-start.1
  22.3 2.5 %collective-permute-start.9 = (f32[96,128]{1,0:T(8,128)S(1)}, f32[96,128]{1,0:T(8,128)S(1)}, u32[]{:S(2)}, u32[]{:S(2)}) collective-permute-start(f32[96,128]{1,0:T(8,128)S(1)} %add_add_fusion.1), channel_id=1, source_target_pairs={{0,24},{4,28},{8,16},{12,20},{16,8},{20,12},{24,0},{28,4},{1,25},{... | collective-permute-start | bytes 147464 | tf_op jit(solution)/shard_map/ppermute | solution.py:267
  24.8 0.5 %collective-permute-start.8 = (f32[96,128]{1,0:T(8,128)S(1)}, f32[96,128]{1,0:T(8,128)S(1)}, u32[]{:S(2)}, u32[]{:S(2)}) collective-permute-start(f32[96,128]{1,0:T(8,128)S(1)} %add_add_fusion.1), channel_id=1, source_target_pairs={{0,16},{4,20},{8,24},{12,28},{16,0},{20,4},{24,8},{28,12},{1,17},{... | collective-permute-start | bytes 147464 | tf_op jit(solution)/shard_map/ppermute | solution.py:267
  25.3 0.5 %collective-permute-start.7 = (f32[96,128]{1,0:T(8,128)S(1)}, f32[96,128]{1,0:T(8,128)S(1)}, u32[]{:S(2)}, u32[]{:S(2)}) collective-permute-start(f32[96,128]{1,0:T(8,128)S(1)} %add_add_fusion.1), channel_id=1, source_target_pairs={{0,8},{4,12},{8,0},{12,4},{16,24},{20,28},{24,16},{28,20},{1,9},{5... | collective-permute-start | bytes 147464 | tf_op jit(solution)/shard_map/ppermute | solution.py:267
  25.8 0.0 copy-done.2
  25.8 2.5 %collective-permute-start.12 = (f32[32,2048]{1,0:T(8,128)S(1)}, f32[32,2048]{1,0:T(8,128)S(1)}, u32[]{:S(2)}, u32[]{:S(2)}) collective-permute-start(f32[32,2048]{1,0:T(8,128)S(1)} %copy-done.2), channel_id=1, source_target_pairs={{0,3},{1,2},{2,1},{3,0},{4,7},{5,6},{6,5},{7,4},{8,11},{9,10},{10,... | collective-permute-start | bytes 786440 | tf_op jit(solution)/shard_map/ppermute | solution.py:267
  28.3 0.0 collective-permute-start.11
  28.3 0.0 collective-permute-done.9
  28.3 1.9 %collective-permute-start.10 = (f32[32,2048]{1,0:T(8,128)S(1)}, f32[32,2048]{1,0:T(8,128)S(1)}, u32[]{:S(2)}, u32[]{:S(2)}) collective-permute-start(f32[32,2048]{1,0:T(8,128)S(1)} %copy-done.2), channel_id=1, source_target_pairs={{0,1},{1,0},{2,3},{3,2},{4,5},{5,4},{6,7},{7,6},{8,9},{9,8},{10,11... | collective-permute-start | bytes 786440 | tf_op jit(solution)/shard_map/ppermute | solution.py:267
  30.2 0.0 collective-permute-done.8
  30.2 0.0 collective-permute-done.7
  30.2 0.0 copy-done
  30.2 0.0 copy-done.1
  30.3 18.8 %all_rounds.1 = (f32[128,32]{1,0:T(8,128)S(1)}, f32[1,32]{1,0:T(1,128)}) custom-call(f32[96,128]{1,0:T(8,128)S(1)} %add_add_fusion.gram_ref, s32[16,8,128]{2,1,0:T(8,128)S(1)} %copy-done, f32[16,8,128]{2,1,0:T(8,128)S(1)} %copy-done.1, s32[1]{0:T(128)} %bitcast.8.place_ref), custom_call_target="tpu_custom_call" | custom-call | tf_op jit(solution)/shard_map/all_rounds/pallas_call | solution.py:248
  49.0 0.0 collective-permute-done.12
  49.0 0.3 collective-permute-done.11
  49.3 0.0 collective-permute-done.10
  49.3 1.2 %convolution_multiply_fusion = f32[32,2048]{1,0:T(8,128)} fusion(f32[128,32]{1,0:T(8,128)S(1)} %get-tuple-element.23, f32[32,2048]{1,0:T(8,128)S(1)} %collective-permute-done.12, f32[32,2048]{1,0:T(8,128)S(1)} %collective-permute-done.11, f32[32,2048]{1,0:T(8,128)S(1)} %collective-permute-done.10, f32[32,2048]{1,0:T(8,128)S(1)} %copy-done.2), kind=kOutput, calls=%fused_computation | convolution fusion | flops 51183616 | bytes 1327104 | tf_op jit(solution)/shard_map/dot_general | solution.py:305
  (7 shorter events, 0.1 us)
Async XLA Ops:
  1.6 5.8 %copy-start.3 = (s32[31,32]{1,0:T(8,128)S(1)}, s32[31,32]{1,0:T(8,128)}, u32[]{:S(2)}) copy-start(s32[31,32]{1,0:T(8,128)} %param.3) | copy-start | bytes 11908
  1.6 8.2 %collective-permute-start.2 = (f32[32,512]{1,0:T(8,128)S(1)}, f32[32,512]{1,0:T(8,128)S(1)}, u32[]{:S(2)}, u32[]{:S(2)}) collective-permute-start(f32[32,512]{1,0:T(8,128)S(1)} %get-tuple-element.31), channel_id=1, source_target_pairs={{0,3},{1,2},{2,1},{3,0},{4,7},{5,6},{6,5},{7,4},{8,11},{9,10},{10,... | collective-permute-start | bytes 196616 | tf_op jit(solution)/shard_map/ppermute | solution.py:267
  6.8 5.6 %collective-permute-start.1 = (f32[32,512]{1,0:T(8,128)S(1)}, f32[32,512]{1,0:T(8,128)S(1)}, u32[]{:S(2)}, u32[]{:S(2)}) collective-permute-start(f32[32,512]{1,0:T(8,128)S(1)} %get-tuple-element.32), channel_id=1, source_target_pairs={{0,2},{1,3},{2,0},{3,1},{4,6},{5,7},{6,4},{7,5},{8,10},{9,11},{10,... | collective-permute-start | bytes 196616 | tf_op jit(solution)/shard_map/ppermute | solution.py:267
  6.8 5.6 %collective-permute-start = (f32[32,512]{1,0:T(8,128)S(1)}, f32[32,512]{1,0:T(8,128)S(1)}, u32[]{:S(2)}, u32[]{:S(2)}) collective-permute-start(f32[32,512]{1,0:T(8,128)S(1)} %get-tuple-element.33), channel_id=1, source_target_pairs={{0,1},{1,0},{2,3},{3,2},{4,5},{5,4},{6,7},{7,6},{8,9},{9,8},{10,11... | collective-permute-start | bytes 196616 | tf_op jit(solution)/shard_map/ppermute | solution.py:267
  13.0 12.9 %copy-start.2 = (f32[32,2048]{1,0:T(8,128)S(1)}, f32[32,2048]{1,0:T(8,128)}, u32[]{:S(2)}) copy-start(f32[32,2048]{1,0:T(8,128)} %param.2) | copy-start | bytes 786436
  13.0 1.2 %collective-permute-start.3 = (f32[96,128]{1,0:T(8,128)S(1)}, f32[96,128]{1,0:T(8,128)S(1)}, u32[]{:S(2)}, u32[]{:S(2)}) collective-permute-start(f32[96,128]{1,0:T(8,128)S(1)} %maximum_maximum_fusion), channel_id=1, source_target_pairs={{0,4},{4,0},{8,12},{12,8},{16,20},{20,16},{24,28},{28,24},{1,5},{5... | collective-permute-start | bytes 147464 | tf_op jit(solution)/shard_map/ppermute | solution.py:267
  14.4 6.2 %collective-permute-start.6 = (f32[96,128]{1,0:T(8,128)S(1)}, f32[96,128]{1,0:T(8,128)S(1)}, u32[]{:S(2)}, u32[]{:S(2)}) collective-permute-start(f32[96,128]{1,0:T(8,128)S(1)} %fusion.18), channel_id=1, source_target_pairs={{0,3},{1,2},{2,1},{3,0},{4,7},{5,6},{6,5},{7,4},{8,11},{9,10},{10,... | collective-permute-start | bytes 147464 | tf_op jit(solution)/shard_map/ppermute | solution.py:267
  17.1 5.1 %collective-permute-start.5 = (f32[96,128]{1,0:T(8,128)S(1)}, f32[96,128]{1,0:T(8,128)S(1)}, u32[]{:S(2)}, u32[]{:S(2)}) collective-permute-start(f32[96,128]{1,0:T(8,128)S(1)} %fusion.18), channel_id=1, source_target_pairs={{0,2},{1,3},{2,0},{3,1},{4,6},{5,7},{6,4},{7,5},{8,10},{9,11},{10,... | collective-permute-start | bytes 147464 | tf_op jit(solution)/shard_map/ppermute | solution.py:267
  17.1 5.1 %collective-permute-start.4 = (f32[96,128]{1,0:T(8,128)S(1)}, f32[96,128]{1,0:T(8,128)S(1)}, u32[]{:S(2)}, u32[]{:S(2)}) collective-permute-start(f32[96,128]{1,0:T(8,128)S(1)} %fusion.18), channel_id=1, source_target_pairs={{0,1},{1,0},{2,3},{3,2},{4,5},{5,4},{6,7},{7,6},{8,9},{9,8},{10,11... | collective-permute-start | bytes 147464 | tf_op jit(solution)/shard_map/ppermute | solution.py:267
  22.2 8.0 %copy-start = (s32[16,8,128]{2,1,0:T(8,128)S(1)}, s32[16,8,128]{2,1,0:T(8,128)}, u32[]{:S(2)}) copy-start(s32[16,8,128]{2,1,0:T(8,128)} %get-tuple-element.21.index_ref) | copy-start | bytes 196612
  22.2 8.0 %copy-start.1 = (f32[16,8,128]{2,1,0:T(8,128)S(1)}, f32[16,8,128]{2,1,0:T(8,128)}, u32[]{:S(2)}) copy-start(f32[16,8,128]{2,1,0:T(8,128)} %get-tuple-element.22.sign_ref) | copy-start | bytes 196612
  22.3 6.1 %collective-permute-start.9 = (f32[96,128]{1,0:T(8,128)S(1)}, f32[96,128]{1,0:T(8,128)S(1)}, u32[]{:S(2)}, u32[]{:S(2)}) collective-permute-start(f32[96,128]{1,0:T(8,128)S(1)} %add_add_fusion.1), channel_id=1, source_target_pairs={{0,24},{4,28},{8,16},{12,20},{16,8},{20,12},{24,0},{28,4},{1,25},{... | collective-permute-start | bytes 147464 | tf_op jit(solution)/shard_map/ppermute | solution.py:267
  24.8 5.4 %collective-permute-start.8 = (f32[96,128]{1,0:T(8,128)S(1)}, f32[96,128]{1,0:T(8,128)S(1)}, u32[]{:S(2)}, u32[]{:S(2)}) collective-permute-start(f32[96,128]{1,0:T(8,128)S(1)} %add_add_fusion.1), channel_id=1, source_target_pairs={{0,16},{4,20},{8,24},{12,28},{16,0},{20,4},{24,8},{28,12},{1,17},{... | collective-permute-start | bytes 147464 | tf_op jit(solution)/shard_map/ppermute | solution.py:267
  25.3 4.9 %collective-permute-start.7 = (f32[96,128]{1,0:T(8,128)S(1)}, f32[96,128]{1,0:T(8,128)S(1)}, u32[]{:S(2)}, u32[]{:S(2)}) collective-permute-start(f32[96,128]{1,0:T(8,128)S(1)} %add_add_fusion.1), channel_id=1, source_target_pairs={{0,8},{4,12},{8,0},{12,4},{16,24},{20,28},{24,16},{28,20},{1,9},{5... | collective-permute-start | bytes 147464 | tf_op jit(solution)/shard_map/ppermute | solution.py:267
  25.8 23.2 %collective-permute-start.12 = (f32[32,2048]{1,0:T(8,128)S(1)}, f32[32,2048]{1,0:T(8,128)S(1)}, u32[]{:S(2)}, u32[]{:S(2)}) collective-permute-start(f32[32,2048]{1,0:T(8,128)S(1)} %copy-done.2), channel_id=1, source_target_pairs={{0,3},{1,2},{2,1},{3,0},{4,7},{5,6},{6,5},{7,4},{8,11},{9,10},{10,... | collective-permute-start | bytes 786440 | tf_op jit(solution)/shard_map/ppermute | solution.py:267
  28.3 21.0 %collective-permute-start.11 = (f32[32,2048]{1,0:T(8,128)S(1)}, f32[32,2048]{1,0:T(8,128)S(1)}, u32[]{:S(2)}, u32[]{:S(2)}) collective-permute-start(f32[32,2048]{1,0:T(8,128)S(1)} %copy-done.2), channel_id=1, source_target_pairs={{0,2},{1,3},{2,0},{3,1},{4,6},{5,7},{6,4},{7,5},{8,10},{9,11},{10,... | collective-permute-start | bytes 786440 | tf_op jit(solution)/shard_map/ppermute | solution.py:267
  28.3 21.0 %collective-permute-start.10 = (f32[32,2048]{1,0:T(8,128)S(1)}, f32[32,2048]{1,0:T(8,128)S(1)}, u32[]{:S(2)}, u32[]{:S(2)}) collective-permute-start(f32[32,2048]{1,0:T(8,128)S(1)} %copy-done.2), channel_id=1, source_target_pairs={{0,1},{1,0},{2,3},{3,2},{4,5},{5,4},{6,7},{7,6},{8,9},{9,8},{10,11... | collective-permute-start | bytes 786440 | tf_op jit(solution)/shard_map/ppermute | solution.py:267

commit v8 on v7

--- a/solution.py
+++ b/solution.py
@@ -36,25 +36,34 @@
     return one(a0, b0) + ((one(a0, b1) + one(a1, b0)) + small)
 
 
-def turning(twice_cross, own, other, sign):
+def turning(twice_cross, own, other, sign, square_stretch=None, shrink=None):
     spread = (own - other) * sign
     up_cross, up_spread = twice_cross * UP, spread * UP
-    square = spread * spread + twice_cross * twice_cross
-    up_square = (up_spread * up_spread + FLOOR) + up_cross * up_cross
+    if shrink is None:
+        spread_square, up_spread_square = spread * spread, up_spread * up_spread + FLOOR
+    else:
+        spread_square = (spread * spread) * square_stretch
+        up_spread_square = (up_spread * up_spread) * square_stretch + FLOOR
+    square = spread_square + twice_cross * twice_cross
+    up_square = up_spread_square + up_cross * up_cross
     is_small = square < TINY_SQUARE
     norm_square = jnp.where(is_small, up_square, square)
-    size = jnp.maximum(jnp.abs(jnp.where(is_small, up_spread, spread)), FLOOR_ROOT)
+    size = jnp.abs(jnp.where(is_small, up_spread, spread))
+    half_norm = norm_square * jnp.where(is_small, (0.5 / UP) * sign, 0.5 * sign)
+    if shrink is not None:
+        size = size * (square_stretch * shrink)
+        half_norm = half_norm * shrink
+    size = jnp.maximum(size, FLOOR_ROOT)
     cross = jnp.where(is_small, up_cross, twice_cross) * sign
-    half_norm = norm_square * jnp.where(is_small, (0.5 / UP) * sign, 0.5 * sign)
     cross_sign = jnp.where(twice_cross < 0, -sign, sign)
     in_order = spread >= 0
     inverse = lax.rsqrt(norm_square)
     large = size * inverse + 1.0
-    double = (size + size) * inverse + 2.0
+    square_uv = (size + size) * inverse + 2.0
     small = cross * inverse
     u = jnp.where(in_order, large, jnp.abs(small))
     v = jnp.where(in_order, small, cross_sign * large)
-    return u, v, lax.rsqrt(double), 0.5 * (own + other) + half_norm * inverse
+    return u, v, lax.rsqrt(square_uv), 0.5 * (own + other) + half_norm * inverse, square_uv
 
 
 def gather(x, index):
@@ -74,33 +83,33 @@
 
 
 def last_step(state, places, sign):
-    z, t, d = state
-    (zi, ti, di), (zp, tp, dp) = [[gather(x, place) for x in (z, t, d)] for place in places]
-    u, v, f, d = turning(product(zi, zp), di, dp, sign)
-    return turned_by(u * f, v * f, ti, tp), d
+    z, t, d, g = state
+    (zi, ti, di, gi), (zp, tp, dp, gp) = [[gather(x, place) for x in state] for place in places]
+    u, v, f, d, _ = turning((gi * gp) * product(zi, zp), di, dp, sign)
+    return turned_by(u * f * gi, v * f * gp, ti, tp), d
 
 
 def double_step(state, index_tile, sign_tile, same):
-    z, zc, d = state
+    z, zc, d, g = state
     p, q, pq = [index_tile[k : k + 1] for k in range(3)]
     sign, sign_q, sign_next = [sign_tile[k : k + 1] for k in range(3)]
     zp, zq, zpq = gather(z, p), gather(z, q), gather(z, pq)
-    diagonals = jnp.take_along_axis(d, index_tile, axis=1)
-    dp, dq, dpq = [jnp.broadcast_to(diagonals[k : k + 1], d.shape) for k in range(3)]
+    rows = lax.broadcasted_iota(jnp.int32, d.shape, 0)
+    both = jnp.take_along_axis(jnp.where(rows < 4, d, g), index_tile, axis=1)
+    dp, dq, dpq, _, gp, gq, gpq = [jnp.broadcast_to(both[k : k + 1], d.shape) for k in range(7)]
     zcq, zcp, zcpq = gather(zc, q), gather(zc, p), gather(zc, pq)
-    u, v, f, d1 = turning(product(z, zp), d, dp, sign)
-    uq, vq, fq, d1q = turning(product(zq, zpq), dq, dpq, sign_q)
-    e00, e11 = product(z, zq), product(zp, zpq)
-    e01, e10 = product(zc, zpq), product(zp, zcq)
-    cross = (f * fq) * (((u * uq) * e00 + (v * vq) * e11) + ((u * vq) * e01 + (v * uq) * e10))
-    u1, v1, f1, d2 = turning(cross, d1, d1q, sign_next)
-    c, s, cq, sq = u * f, v * f, uq * fq, vq * fq
+    u, v, f, d1, n = turning((g * gp) * product(z, zp), d, dp, sign)
+    uq, vq, fq, d1q, nq = turning((gq * gpq) * product(zq, zpq), dq, dpq, sign_q)
+    e00, e11 = (g * gq) * product(z, zq), (gp * gpq) * product(zp, zpq)
+    e01, e10 = (g * gpq) * product(zc, zpq), (gp * gq) * product(zp, zcq)
+    cross = ((u * uq) * e00 + (v * vq) * e11) + ((u * vq) * e01 + (v * uq) * e10)
+    u1, v1, f1, d2, _ = turning(cross, d1, d1q, sign_next, n * nq, f * fq)
+    c, s, cq, sq = u * (f * g), v * (f * gp), uq * (fq * gq), vq * (fq * gpq)
     z1, zc1 = turned_by(c, s, z, zcp), turned_by(c, s, zc, zp)
     zq1, zcq1 = turned_by(cq, sq, zq, zcpq), turned_by(cq, sq, zcq, zpq)
     own, other = jnp.where(same, z1, zc1), jnp.where(same, zcq1, zq1)
     own_c, other_c = jnp.where(same, zc1, z1), jnp.where(same, zq1, zcq1)
-    f1 = tall(f1, z)
-    return f1 * turned_by(u1, v1, own, other), f1 * turned_by(u1, v1, own_c, other_c), d2
+    return turned_by(u1, v1, own, other), turned_by(u1, v1, own_c, other_c), d2, f1
 
 
 def moved(x, pair):
@@ -150,7 +159,7 @@
     signs = [lower, sign_of(second, first_of_second), sign_of(own, second), colour]
     for k in range(doubles):
         at = slice(k, k + 1)
-        index_ref[k] = jnp.concatenate([first[at], second[at]] + [first_of_second[at]] * 6, axis=0)
+        index_ref[k] = jnp.concatenate([first[at], second[at], first_of_second[at], own[at]] * 2, axis=0)
         sign_ref[k] = jnp.concatenate([x[at] for x in signs] + [lower[at]] * 4, axis=0)
 
 
@@ -191,12 +200,12 @@
             at = slice(tile * LANES, (tile + 1) * LANES)
             held = colour_of(0) > 0
             z, zc = jnp.where(held, w[:, at], start[:, at]), jnp.where(held, start[:, at], w[:, at])
-            d_tile = d[:, at]
+            d_tile, g = d[:, at], jnp.ones((8, LANES), jnp.float32)
             for k in range(doubles - 1):
                 same = colour_of(k) * colour_of(k + 1) > 0
-                z, zc, d_tile = double_step((z, zc, d_tile), index_ref[k], sign_ref[k], same)
+                z, zc, d_tile, g = double_step((z, zc, d_tile, g), index_ref[k], sign_ref[k], same)
             t = jnp.where(colour_of(doubles - 1) > 0, zc, z)
-            t, d_tile = last_step((z, t, d_tile), last_places, last_sign)
+            t, d_tile = last_step((z, t, d_tile, g), last_places, last_sign)
             turned.append(t)
             energies.append(d_tile)
         if tiles == 1:

time: 50.8 us -> 50.8 us (level)
  transfers between devices with their start and end apart: 13 -> 13, of which waited for: 5 -> 5; matrix products, arithmetic and copies ran while one was open for 1% -> 1% of each run, Pallas kernels for 41% -> 40%
where the time goes in v8:
time: 50.8 us; the launch traced here: 50.5 us
  Pallas kernels  20.2 us (40%)
  starting transfers between devices  18.1 us (36%)
  waiting for transfers between devices  7.96 us (16%)
  matrix products  1.56 us (3%)
  local copies, waits for them, and re-layouts  1.17 us (2%)
  other arithmetic  0.81 us (2%)
  between operations  0.76 us (1%)
    pallas_call x1, Pallas kernels, turn_all(): pl.pallas_call(functools.partial(turn_kernel, n_cells), out_shape=(jax.Sh...  18.3 us
    ppermute x13, starting transfers between devices, sent(): lax.ppermute(value, axis, [(i, i ^ toggle) for i in range(lax.axis_size(a...  18.1 us
    ppermute x13, waiting for transfers between devices, sent(): lax.ppermute(value, axis, [(i, i ^ toggle) for i in range(lax.axis_size(a...  7.96 us
    pallas_call x1, Pallas kernels, tables_of(): pl.pallas_call(table_kernel, out_shape=(jax.ShapeDtypeStruct(shape, jnp.i...  1.85 us
    dot_general x1, matrix products, on_device(): lax.dot_general(modes, jnp.concatenate(blocks, axis=0), (((0,), (0,)), ((...  1.18 us
  transfers between devices with their start and end apart: 13, of which 5 were waited for; matrix products, arithmetic and copies ran while one was open for 1% of the time, Pallas kernels for 40%

profile of v8, /device:TPU:0, one launch (start us, length us, event | category | flops | bytes accessed | tf_op | source)
XLA Modules:
  0.0 50.5 jit_solution(17607481155067832442)
XLA Ops:
  0.7 1.0 %dynamic-slice_bitcast_fusion.4 = (f32[1,32,512]{2,1,0:T(8,128)S(1)}, f32[32,512]{1,0:T(8,128)S(1)}, f32[32,512]{1,0:T(8,128)S(1)}, f32[32,512]{1,0:T(8,128)S(1)}) fusion(f32[32,2048]{1,0:T(8,128)} %param.2, s32[]{:T(128)S(6)} %select_n.25, s32[]{:T(128)S(6)} %select_n.28, s32[]{:T(128)S(6)} %select_n.27, s32[]{:T(128)S(6)} %select_n.26), kind=kLoop, calls=%fused_computation.21 | loop fusion | bytes 524304 | tf_op jit(solution)/shard_map/stack | solution.py:302
  1.6 0.0 copy-start.3
  1.6 5.1 %collective-permute-start.2 = (f32[32,512]{1,0:T(8,128)S(1)}, f32[32,512]{1,0:T(8,128)S(1)}, u32[]{:S(2)}, u32[]{:S(2)}) collective-permute-start(f32[32,512]{1,0:T(8,128)S(1)} %get-tuple-element.31), channel_id=1, source_target_pairs={{0,3},{1,2},{2,1},{3,0},{4,7},{5,6},{6,5},{7,4},{8,11},{9,10},{10,... | collective-permute-start | bytes 196616 | tf_op jit(solution)/shard_map/ppermute | solution.py:276
  6.8 0.0 collective-permute-start.1
  6.8 0.6 %collective-permute-start = (f32[32,512]{1,0:T(8,128)S(1)}, f32[32,512]{1,0:T(8,128)S(1)}, u32[]{:S(2)}, u32[]{:S(2)}) collective-permute-start(f32[32,512]{1,0:T(8,128)S(1)} %get-tuple-element.33), channel_id=1, source_target_pairs={{0,1},{1,0},{2,3},{3,2},{4,5},{5,4},{6,7},{7,6},{8,9},{9,8},{10,11... | collective-permute-start | bytes 196616 | tf_op jit(solution)/shard_map/ppermute | solution.py:276
  7.4 0.0 copy-done.3
  7.4 0.6 %pad_add_fusion.plan_ref = s32[32,32]{1,0:T(8,128)} fusion(s32[1,32]{1,0:T(1,128)S(1)} %iota.4, s32[31,32]{1,0:T(8,128)S(1)} %copy-done.3), kind=kLoop, calls=%fused_computation.25 | loop fusion | flops 1024 | bytes 8192 | tf_op jit(solution)/shard_map/concatenate | solution.py:242
  8.0 1.9 %step_tables.1 = (s32[16,8,128]{2,1,0:T(8,128)}, f32[16,8,128]{2,1,0:T(8,128)}) custom-call(s32[32,32]{1,0:T(8,128)} %pad_add_fusion.plan_ref), custom_call_target="tpu_custom_call" | custom-call | tf_op jit(solution)/shard_map/step_tables/pallas_call | solution.py:244
  9.9 0.0 collective-permute-done.2
  9.9 2.5 %collective-permute-done.1 = f32[32,512]{1,0:T(8,128)S(1)} collective-permute-done((f32[32,512]{1,0:T(8,128)S(1)}, f32[32,512]{1,0:T(8,128)S(1)}, u32[]{:S(2)}, u32[]{:S(2)}) %collective-permute-start.1) | collective-permute-done | bytes 65568 | tf_op jit(solution)/shard_map/ppermute | solution.py:276
  12.4 0.0 collective-permute-done
  12.4 0.4 fusion.7
  12.8 0.1 slice.14
  12.9 0.1 slice.13
  13.0 0.0 copy-start.2
  13.0 0.1 maximum_maximum_fusion
  13.0 0.0 collective-permute-start.3
  13.1 1.2 %collective-permute-done.3 = f32[96,128]{1,0:T(8,128)S(1)} collective-permute-done((f32[96,128]{1,0:T(8,128)S(1)}, f32[96,128]{1,0:T(8,128)S(1)}, u32[]{:S(2)}, u32[]{:S(2)}) %collective-permute-start.3) | collective-permute-done | bytes 49184 | tf_op jit(solution)/shard_map/ppermute | solution.py:276
  14.3 0.1 fusion.18
  14.4 2.7 %collective-permute-start.6 = (f32[96,128]{1,0:T(8,128)S(1)}, f32[96,128]{1,0:T(8,128)S(1)}, u32[]{:S(2)}, u32[]{:S(2)}) collective-permute-start(f32[96,128]{1,0:T(8,128)S(1)} %fusion.18), channel_id=1, source_target_pairs={{0,3},{1,2},{2,1},{3,0},{4,7},{5,6},{6,5},{7,4},{8,11},{9,10},{10,... | collective-permute-start | bytes 147464 | tf_op jit(solution)/shard_map/ppermute | solution.py:276
  17.1 0.0 collective-permute-start.5
  17.1 1.7 %collective-permute-start.4 = (f32[96,128]{1,0:T(8,128)S(1)}, f32[96,128]{1,0:T(8,128)S(1)}, u32[]{:S(2)}, u32[]{:S(2)}) collective-permute-start(f32[96,128]{1,0:T(8,128)S(1)} %fusion.18), channel_id=1, source_target_pairs={{0,1},{1,0},{2,3},{3,2},{4,5},{5,4},{6,7},{7,6},{8,9},{9,8},{10,11... | collective-permute-start | bytes 147464 | tf_op jit(solution)/shard_map/ppermute | solution.py:276
  18.8 1.8 %collective-permute-done.6 = f32[96,128]{1,0:T(8,128)S(1)} collective-permute-done((f32[96,128]{1,0:T(8,128)S(1)}, f32[96,128]{1,0:T(8,128)S(1)}, u32[]{:S(2)}, u32[]{:S(2)}) %collective-permute-start.6) | collective-permute-done | bytes 49184 | tf_op jit(solution)/shard_map/ppermute | solution.py:276
  20.6 1.6 %collective-permute-done.5 = f32[96,128]{1,0:T(8,128)S(1)} collective-permute-done((f32[96,128]{1,0:T(8,128)S(1)}, f32[96,128]{1,0:T(8,128)S(1)}, u32[]{:S(2)}, u32[]{:S(2)}) %collective-permute-start.5) | collective-permute-done | bytes 49184 | tf_op jit(solution)/shard_map/ppermute | solution.py:276
  22.2 0.0 collective-permute-done.4
  22.2 0.0 copy-start
  22.2 0.0 copy-start.1
  22.3 2.5 %collective-permute-start.9 = (f32[96,128]{1,0:T(8,128)S(1)}, f32[96,128]{1,0:T(8,128)S(1)}, u32[]{:S(2)}, u32[]{:S(2)}) collective-permute-start(f32[96,128]{1,0:T(8,128)S(1)} %add_add_fusion.1), channel_id=1, source_target_pairs={{0,24},{4,28},{8,16},{12,20},{16,8},{20,12},{24,0},{28,4},{1,25},{... | collective-permute-start | bytes 147464 | tf_op jit(solution)/shard_map/ppermute | solution.py:276
  24.8 0.5 %collective-permute-start.8 = (f32[96,128]{1,0:T(8,128)S(1)}, f32[96,128]{1,0:T(8,128)S(1)}, u32[]{:S(2)}, u32[]{:S(2)}) collective-permute-start(f32[96,128]{1,0:T(8,128)S(1)} %add_add_fusion.1), channel_id=1, source_target_pairs={{0,16},{4,20},{8,24},{12,28},{16,0},{20,4},{24,8},{28,12},{1,17},{... | collective-permute-start | bytes 147464 | tf_op jit(solution)/shard_map/ppermute | solution.py:276
  25.3 0.5 %collective-permute-start.7 = (f32[96,128]{1,0:T(8,128)S(1)}, f32[96,128]{1,0:T(8,128)S(1)}, u32[]{:S(2)}, u32[]{:S(2)}) collective-permute-start(f32[96,128]{1,0:T(8,128)S(1)} %add_add_fusion.1), channel_id=1, source_target_pairs={{0,8},{4,12},{8,0},{12,4},{16,24},{20,28},{24,16},{28,20},{1,9},{5... | collective-permute-start | bytes 147464 | tf_op jit(solution)/shard_map/ppermute | solution.py:276
  25.8 0.0 copy-done.2
  25.8 2.5 %collective-permute-start.12 = (f32[32,2048]{1,0:T(8,128)S(1)}, f32[32,2048]{1,0:T(8,128)S(1)}, u32[]{:S(2)}, u32[]{:S(2)}) collective-permute-start(f32[32,2048]{1,0:T(8,128)S(1)} %copy-done.2), channel_id=1, source_target_pairs={{0,3},{1,2},{2,1},{3,0},{4,7},{5,6},{6,5},{7,4},{8,11},{9,10},{10,... | collective-permute-start | bytes 786440 | tf_op jit(solution)/shard_map/ppermute | solution.py:276
  28.3 0.0 collective-permute-start.11
  28.3 0.0 collective-permute-done.9
  28.3 1.9 %collective-permute-start.10 = (f32[32,2048]{1,0:T(8,128)S(1)}, f32[32,2048]{1,0:T(8,128)S(1)}, u32[]{:S(2)}, u32[]{:S(2)}) collective-permute-start(f32[32,2048]{1,0:T(8,128)S(1)} %copy-done.2), channel_id=1, source_target_pairs={{0,1},{1,0},{2,3},{3,2},{4,5},{5,4},{6,7},{7,6},{8,9},{9,8},{10,11... | collective-permute-start | bytes 786440 | tf_op jit(solution)/shard_map/ppermute | solution.py:276
  30.2 0.0 collective-permute-done.8
  30.2 0.0 collective-permute-done.7
  30.2 0.0 copy-done
  30.2 0.0 copy-done.1
  30.3 18.3 %all_rounds.1 = (f32[128,32]{1,0:T(8,128)S(1)}, f32[1,32]{1,0:T(1,128)}) custom-call(f32[96,128]{1,0:T(8,128)S(1)} %add_add_fusion.gram_ref, s32[16,8,128]{2,1,0:T(8,128)S(1)} %copy-done, f32[16,8,128]{2,1,0:T(8,128)S(1)} %copy-done.1, s32[1]{0:T(128)} %bitcast.8.place_ref), custom_call_target="tpu_custom_call" | custom-call | tf_op jit(solution)/shard_map/all_rounds/pallas_call | solution.py:257
  48.6 0.0 collective-permute-done.12
  48.6 0.8 %collective-permute-done.11 = f32[32,2048]{1,0:T(8,128)S(1)} collective-permute-done((f32[32,2048]{1,0:T(8,128)S(1)}, f32[32,2048]{1,0:T(8,128)S(1)}, u32[]{:S(2)}, u32[]{:S(2)}) %collective-permute-start.11) | collective-permute-done | bytes 262176 | tf_op jit(solution)/shard_map/ppermute | solution.py:276
  49.3 0.0 collective-permute-done.10
  49.3 1.2 %convolution_multiply_fusion = f32[32,2048]{1,0:T(8,128)} fusion(f32[128,32]{1,0:T(8,128)S(1)} %get-tuple-element.23, f32[32,2048]{1,0:T(8,128)S(1)} %collective-permute-done.12, f32[32,2048]{1,0:T(8,128)S(1)} %collective-permute-done.11, f32[32,2048]{1,0:T(8,128)S(1)} %collective-permute-done.10, f32[32,2048]{1,0:T(8,128)S(1)} %copy-done.2), kind=kOutput, calls=%fused_computation | convolution fusion | flops 51183616 | bytes 1327104 | tf_op jit(solution)/shard_map/dot_general | solution.py:314
  (7 shorter events, 0.1 us)
Async XLA Ops:
  1.6 5.8 %copy-start.3 = (s32[31,32]{1,0:T(8,128)S(1)}, s32[31,32]{1,0:T(8,128)}, u32[]{:S(2)}) copy-start(s32[31,32]{1,0:T(8,128)} %param.3) | copy-start | bytes 11908
  1.6 8.2 %collective-permute-start.2 = (f32[32,512]{1,0:T(8,128)S(1)}, f32[32,512]{1,0:T(8,128)S(1)}, u32[]{:S(2)}, u32[]{:S(2)}) collective-permute-start(f32[32,512]{1,0:T(8,128)S(1)} %get-tuple-element.31), channel_id=1, source_target_pairs={{0,3},{1,2},{2,1},{3,0},{4,7},{5,6},{6,5},{7,4},{8,11},{9,10},{10,... | collective-permute-start | bytes 196616 | tf_op jit(solution)/shard_map/ppermute | solution.py:276
  6.8 5.6 %collective-permute-start.1 = (f32[32,512]{1,0:T(8,128)S(1)}, f32[32,512]{1,0:T(8,128)S(1)}, u32[]{:S(2)}, u32[]{:S(2)}) collective-permute-start(f32[32,512]{1,0:T(8,128)S(1)} %get-tuple-element.32), channel_id=1, source_target_pairs={{0,2},{1,3},{2,0},{3,1},{4,6},{5,7},{6,4},{7,5},{8,10},{9,11},{10,... | collective-permute-start | bytes 196616 | tf_op jit(solution)/shard_map/ppermute | solution.py:276
  6.8 5.6 %collective-permute-start = (f32[32,512]{1,0:T(8,128)S(1)}, f32[32,512]{1,0:T(8,128)S(1)}, u32[]{:S(2)}, u32[]{:S(2)}) collective-permute-start(f32[32,512]{1,0:T(8,128)S(1)} %get-tuple-element.33), channel_id=1, source_target_pairs={{0,1},{1,0},{2,3},{3,2},{4,5},{5,4},{6,7},{7,6},{8,9},{9,8},{10,11... | collective-permute-start | bytes 196616 | tf_op jit(solution)/shard_map/ppermute | solution.py:276
  13.0 12.9 %copy-start.2 = (f32[32,2048]{1,0:T(8,128)S(1)}, f32[32,2048]{1,0:T(8,128)}, u32[]{:S(2)}) copy-start(f32[32,2048]{1,0:T(8,128)} %param.2) | copy-start | bytes 786436
  13.0 1.2 %collective-permute-start.3 = (f32[96,128]{1,0:T(8,128)S(1)}, f32[96,128]{1,0:T(8,128)S(1)}, u32[]{:S(2)}, u32[]{:S(2)}) collective-permute-start(f32[96,128]{1,0:T(8,128)S(1)} %maximum_maximum_fusion), channel_id=1, source_target_pairs={{0,4},{4,0},{8,12},{12,8},{16,20},{20,16},{24,28},{28,24},{1,5},{5... | collective-permute-start | bytes 147464 | tf_op jit(solution)/shard_map/ppermute | solution.py:276
  14.4 6.2 %collective-permute-start.6 = (f32[96,128]{1,0:T(8,128)S(1)}, f32[96,128]{1,0:T(8,128)S(1)}, u32[]{:S(2)}, u32[]{:S(2)}) collective-permute-start(f32[96,128]{1,0:T(8,128)S(1)} %fusion.18), channel_id=1, source_target_pairs={{0,3},{1,2},{2,1},{3,0},{4,7},{5,6},{6,5},{7,4},{8,11},{9,10},{10,... | collective-permute-start | bytes 147464 | tf_op jit(solution)/shard_map/ppermute | solution.py:276
  17.1 5.1 %collective-permute-start.5 = (f32[96,128]{1,0:T(8,128)S(1)}, f32[96,128]{1,0:T(8,128)S(1)}, u32[]{:S(2)}, u32[]{:S(2)}) collective-permute-start(f32[96,128]{1,0:T(8,128)S(1)} %fusion.18), channel_id=1, source_target_pairs={{0,2},{1,3},{2,0},{3,1},{4,6},{5,7},{6,4},{7,5},{8,10},{9,11},{10,... | collective-permute-start | bytes 147464 | tf_op jit(solution)/shard_map/ppermute | solution.py:276
  17.1 5.1 %collective-permute-start.4 = (f32[96,128]{1,0:T(8,128)S(1)}, f32[96,128]{1,0:T(8,128)S(1)}, u32[]{:S(2)}, u32[]{:S(2)}) collective-permute-start(f32[96,128]{1,0:T(8,128)S(1)} %fusion.18), channel_id=1, source_target_pairs={{0,1},{1,0},{2,3},{3,2},{4,5},{5,4},{6,7},{7,6},{8,9},{9,8},{10,11... | collective-permute-start | bytes 147464 | tf_op jit(solution)/shard_map/ppermute | solution.py:276
  22.2 8.0 %copy-start = (s32[16,8,128]{2,1,0:T(8,128)S(1)}, s32[16,8,128]{2,1,0:T(8,128)}, u32[]{:S(2)}) copy-start(s32[16,8,128]{2,1,0:T(8,128)} %get-tuple-element.21.index_ref) | copy-start | bytes 196612
  22.2 8.0 %copy-start.1 = (f32[16,8,128]{2,1,0:T(8,128)S(1)}, f32[16,8,128]{2,1,0:T(8,128)}, u32[]{:S(2)}) copy-start(f32[16,8,128]{2,1,0:T(8,128)} %get-tuple-element.22.sign_ref) | copy-start | bytes 196612
  22.3 6.1 %collective-permute-start.9 = (f32[96,128]{1,0:T(8,128)S(1)}, f32[96,128]{1,0:T(8,128)S(1)}, u32[]{:S(2)}, u32[]{:S(2)}) collective-permute-start(f32[96,128]{1,0:T(8,128)S(1)} %add_add_fusion.1), channel_id=1, source_target_pairs={{0,24},{4,28},{8,16},{12,20},{16,8},{20,12},{24,0},{28,4},{1,25},{... | collective-permute-start | bytes 147464 | tf_op jit(solution)/shard_map/ppermute | solution.py:276
  24.8 5.4 %collective-permute-start.8 = (f32[96,128]{1,0:T(8,128)S(1)}, f32[96,128]{1,0:T(8,128)S(1)}, u32[]{:S(2)}, u32[]{:S(2)}) collective-permute-start(f32[96,128]{1,0:T(8,128)S(1)} %add_add_fusion.1), channel_id=1, source_target_pairs={{0,16},{4,20},{8,24},{12,28},{16,0},{20,4},{24,8},{28,12},{1,17},{... | collective-permute-start | bytes 147464 | tf_op jit(solution)/shard_map/ppermute | solution.py:276
  25.3 4.9 %collective-permute-start.7 = (f32[96,128]{1,0:T(8,128)S(1)}, f32[96,128]{1,0:T(8,128)S(1)}, u32[]{:S(2)}, u32[]{:S(2)}) collective-permute-start(f32[96,128]{1,0:T(8,128)S(1)} %add_add_fusion.1), channel_id=1, source_target_pairs={{0,8},{4,12},{8,0},{12,4},{16,24},{20,28},{24,16},{28,20},{1,9},{5... | collective-permute-start | bytes 147464 | tf_op jit(solution)/shard_map/ppermute | solution.py:276
  25.8 22.8 %collective-permute-start.12 = (f32[32,2048]{1,0:T(8,128)S(1)}, f32[32,2048]{1,0:T(8,128)S(1)}, u32[]{:S(2)}, u32[]{:S(2)}) collective-permute-start(f32[32,2048]{1,0:T(8,128)S(1)} %copy-done.2), channel_id=1, source_target_pairs={{0,3},{1,2},{2,1},{3,0},{4,7},{5,6},{6,5},{7,4},{8,11},{9,10},{10,... | collective-permute-start | bytes 786440 | tf_op jit(solution)/shard_map/ppermute | solution.py:276
  28.3 21.0 %collective-permute-start.11 = (f32[32,2048]{1,0:T(8,128)S(1)}, f32[32,2048]{1,0:T(8,128)S(1)}, u32[]{:S(2)}, u32[]{:S(2)}) collective-permute-start(f32[32,2048]{1,0:T(8,128)S(1)} %copy-done.2), channel_id=1, source_target_pairs={{0,2},{1,3},{2,0},{3,1},{4,6},{5,7},{6,4},{7,5},{8,10},{9,11},{10,... | collective-permute-start | bytes 786440 | tf_op jit(solution)/shard_map/ppermute | solution.py:276
  28.3 21.0 %collective-permute-start.10 = (f32[32,2048]{1,0:T(8,128)S(1)}, f32[32,2048]{1,0:T(8,128)S(1)}, u32[]{:S(2)}, u32[]{:S(2)}) collective-permute-start(f32[32,2048]{1,0:T(8,128)S(1)} %copy-done.2), channel_id=1, source_target_pairs={{0,1},{1,0},{2,3},{3,2},{4,5},{5,4},{6,7},{7,6},{8,9},{9,8},{10,11... | collective-permute-start | bytes 786440 | tf_op jit(solution)/shard_map/ppermute | solution.py:276

commit v9 on v8

--- a/solution.py
+++ b/solution.py
@@ -296,25 +296,36 @@
     place = here.astype(jnp.int32)[None]
     part = cells // n_blk
 
+    def run_of(x, first, count):
+        twice = jnp.concatenate([x, x], axis=1)
+        return lax.dynamic_slice_in_dim(twice, lax.rem(first, n_blk) * part, count * part, 1)
+
     def part_for(d):
         return lax.dynamic_slice_in_dim(snapshots, (here ^ d) * part, part, 1)
 
-    parts = jnp.stack([part_for(0)] + [sent(part_for(d), "blk", d) for d in range(1, n_blk)])
+    arrived = [part_for(0)] + [sent(part_for(d), "blk", d) for d in range(1, n_blk)]
+    tables, source = lax.optimization_barrier((tables_of(plan), snapshots))
+    rest = [run_of(source, (here ^ d) + 1, n_blk - 1) for d in range(1, n_blk)]
+    own = run_of(source, here, n_blk)
+    parts = jnp.stack(arrived)
     parts = [lax.dynamic_index_in_dim(parts, here ^ q, 0, keepdims=False) for q in range(n_blk)]
-    tables, parts = lax.optimization_barrier((tables_of(plan), parts))
+    tables, rest, own, parts = lax.optimization_barrier((tables, rest, own, parts))
     whole = jnp.concatenate(parts, axis=0)
     gram = lax.dot_general(whole, whole, (((1,), (1,)), ((), ())), precision=lax.Precision.HIGHEST)
     gram = packed(gram)
     gram = gram + sent(gram, "cell", 1)
+    gram, rest = lax.optimization_barrier((gram, rest))
+    others = [sent(rest[0], "blk", 1)]
     gram = tree_sum([gram] + [sent(gram, "blk", d) for d in range(1, n_blk)])
-    gram, held = lax.optimization_barrier((gram, snapshots))
-    blocks = [snapshots] + [sent(held, "blk", d) for d in range(1, n_blk)]
+    gram, rest = lax.optimization_barrier((gram, rest))
+    others += [sent(rest[d - 1], "blk", d) for d in range(len(others) + 1, n_blk)]
+    blocks = [own] + [jnp.concatenate(x, axis=1) for x in zip(arrived[1:], others)]
     gram = tree_sum([gram] + [sent(gram, "cell", d) for d in range(2, n_cell, 2)])
     modes, energy = turn_all(gram, tables, place, cells * n_cell)
     rotated = lax.dot_general(
         modes, jnp.concatenate(blocks, axis=0), (((0,), (0,)), ((), ())), precision=lax.Precision.HIGH
     )
-    return rotated * rotated, energy.reshape(pair)
+    return run_of(rotated * rotated, n_blk - here, n_blk), energy.reshape(pair)
 
 
 def solution(mesh):

time: 50.8 us -> 49.5 us (0.974)
  starting transfers between devices: 18.1 us -> 16.3 us
  local copies, waits for them, and re-layouts: 1.17 us -> 2.03 us
  other arithmetic: 0.81 us -> 1.57 us
  matrix products: 1.56 us -> 0.83 us
  waiting for transfers between devices: 7.96 us -> 7.41 us
    ppermute x13, starting transfers between devices: 18.1 us -> 16.3 us  [sent(): lax.ppermute(value, axis, [(i, i ^ toggle) for i in range(lax.axis_size(a...]
    concatenate x0 -> x1, other arithmetic: none -> 0.76 us  [run_of(): twice = jnp.concatenate([x, x], axis=1)]
    dot_general x1, matrix products: 1.18 us -> 0.45 us  [on_device(): lax.dot_general(modes, jnp.concatenate(blocks, axis=0), (((0,), (0,)), ((...]
    unnamed x8 -> x9, local copies, waits for them, and re-layouts: 0.02 us -> 0.74 us
    ppermute x13, waiting for transfers between devices: 7.96 us -> 7.41 us  [sent(): lax.ppermute(value, axis, [(i, i ^ toggle) for i in range(lax.axis_size(a...]
  transfers between devices with their start and end apart: 13 -> 13, of which waited for: 5 -> 6; matrix products, arithmetic and copies ran while one was open for 1% -> 1% of each run, Pallas kernels for 40% -> 41%
where the time goes in v9:
time: 49.5 us; the launch traced here: 49.2 us
  Pallas kernels  20.2 us (41%)
  starting transfers between devices  16.3 us (33%)
  waiting for transfers between devices  7.41 us (15%)
  local copies, waits for them, and re-layouts  2.03 us (4%)
  other arithmetic  1.57 us (3%)
  matrix products  0.83 us (2%)
  between operations  0.83 us (2%)
    pallas_call x1, Pallas kernels, turn_all(): pl.pallas_call(functools.partial(turn_kernel, n_cells), out_shape=(jax.Sh...  18.3 us
    ppermute x13, starting transfers between devices, sent(): lax.ppermute(value, axis, [(i, i ^ toggle) for i in range(lax.axis_size(a...  16.3 us
    ppermute x13, waiting for transfers between devices, sent(): lax.ppermute(value, axis, [(i, i ^ toggle) for i in range(lax.axis_size(a...  7.41 us
    pallas_call x1, Pallas kernels, tables_of(): pl.pallas_call(table_kernel, out_shape=(jax.ShapeDtypeStruct(shape, jnp.i...  1.86 us
    another operation x1, local copies, waits for them, and re-layouts, on_device(): parts = jnp.stack(arrived)  1 us
  transfers between devices with their start and end apart: 13, of which 6 were waited for; matrix products, arithmetic and copies ran while one was open for 1% of the time, Pallas kernels for 41%

profile of v9, /device:TPU:0, one launch (start us, length us, event | category | flops | bytes accessed | tf_op | source)
XLA Modules:
  0.0 49.2 jit_solution(5520871292293428257)
XLA Ops:
  0.7 0.0 copy-start.2
  0.7 1.0 %dynamic-slice_bitcast_fusion.4 = (f32[1,32,512]{2,1,0:T(8,128)S(1)}, f32[32,512]{1,0:T(8,128)S(1)}, f32[32,512]{1,0:T(8,128)S(1)}, f32[32,512]{1,0:T(8,128)S(1)}) fusion(f32[32,2048]{1,0:T(8,128)} %param.2, s32[]{:T(128)S(6)} %select_n.44, s32[]{:T(128)S(6)} %select_n.45, s32[]{:T(128)S(6)} %select_n.47, s32[]{:T(128)S(6)} %select_n.46), kind=kLoop, calls=%fused_computation.30 | loop fusion | bytes 524304 | tf_op jit(solution)/shard_map/stack | solution.py:310
  1.7 5.1 %collective-permute-start.2 = (f32[32,512]{1,0:T(8,128)S(1)}, f32[32,512]{1,0:T(8,128)S(1)}, u32[]{:S(2)}, u32[]{:S(2)}) collective-permute-start(f32[32,512]{1,0:T(8,128)S(1)} %get-tuple-element.59), channel_id=1, source_target_pairs={{0,3},{1,2},{2,1},{3,0},{4,7},{5,6},{6,5},{7,4},{8,11},{9,10},{10,... | collective-permute-start | bytes 196616 | tf_op jit(solution)/shard_map/ppermute | solution.py:276
  6.8 0.0 collective-permute-start.1
  6.8 0.6 %collective-permute-start = (f32[32,512]{1,0:T(8,128)S(1)}, f32[32,512]{1,0:T(8,128)S(1)}, u32[]{:S(2)}, u32[]{:S(2)}) collective-permute-start(f32[32,512]{1,0:T(8,128)S(1)} %get-tuple-element.58), channel_id=1, source_target_pairs={{0,1},{1,0},{2,3},{3,2},{4,5},{5,4},{6,7},{7,6},{8,9},{9,8},{10,11... | collective-permute-start | bytes 196616 | tf_op jit(solution)/shard_map/ppermute | solution.py:276
  7.4 0.0 copy-start.3
  7.4 0.7 %copy-done.3 = s32[31,32]{1,0:T(8,128)S(1)} copy-done((s32[31,32]{1,0:T(8,128)S(1)}, s32[31,32]{1,0:T(8,128)}, u32[]{:S(2)}) %copy-start.3) | copy-done | bytes 3992
  8.2 0.6 %pad_add_fusion.plan_ref = s32[32,32]{1,0:T(8,128)} fusion(s32[1,32]{1,0:T(1,128)S(1)} %iota.4, s32[31,32]{1,0:T(8,128)S(1)} %copy-done.3), kind=kLoop, calls=%fused_computation.34 | loop fusion | flops 1024 | bytes 8192 | tf_op jit(solution)/shard_map/concatenate | solution.py:242
  8.8 1.9 %step_tables.1 = (s32[16,8,128]{2,1,0:T(8,128)}, f32[16,8,128]{2,1,0:T(8,128)}) custom-call(s32[32,32]{1,0:T(8,128)} %pad_add_fusion.plan_ref), custom_call_target="tpu_custom_call" | custom-call | tf_op jit(solution)/shard_map/step_tables/pallas_call | solution.py:244
  10.6 0.0 copy-done.2
  10.8 0.0 collective-permute-done.2
  10.8 1.6 %collective-permute-done.1 = f32[32,512]{1,0:T(8,128)S(1)} collective-permute-done((f32[32,512]{1,0:T(8,128)S(1)}, f32[32,512]{1,0:T(8,128)S(1)}, u32[]{:S(2)}, u32[]{:S(2)}) %collective-permute-start.1) | collective-permute-done | bytes 65568 | tf_op jit(solution)/shard_map/ppermute | solution.py:276
  12.4 0.0 collective-permute-done
  12.5 0.4 fusion.14
  12.8 0.1 slice.14
  12.9 0.1 slice.13
  13.0 0.1 maximum_maximum_fusion
  13.1 0.0 collective-permute-start.3
  13.1 1.2 %collective-permute-done.3 = f32[96,128]{1,0:T(8,128)S(1)} collective-permute-done((f32[96,128]{1,0:T(8,128)S(1)}, f32[96,128]{1,0:T(8,128)S(1)}, u32[]{:S(2)}, u32[]{:S(2)}) %collective-permute-start.3) | collective-permute-done | bytes 49184 | tf_op jit(solution)/shard_map/ppermute | solution.py:276
  14.3 0.1 fusion.25
  14.4 1.6 %collective-permute-start.5 = (f32[96,128]{1,0:T(8,128)S(1)}, f32[96,128]{1,0:T(8,128)S(1)}, u32[]{:S(2)}, u32[]{:S(2)}) collective-permute-start(f32[96,128]{1,0:T(8,128)S(1)} %fusion.25), channel_id=1, source_target_pairs={{0,2},{1,3},{2,0},{3,1},{4,6},{5,7},{6,4},{7,5},{8,10},{9,11},{10,... | collective-permute-start | bytes 147464 | tf_op jit(solution)/shard_map/ppermute | solution.py:276
  16.0 1.9 %collective-permute-start.6 = (f32[96,128]{1,0:T(8,128)S(1)}, f32[96,128]{1,0:T(8,128)S(1)}, u32[]{:S(2)}, u32[]{:S(2)}) collective-permute-start(f32[96,128]{1,0:T(8,128)S(1)} %fusion.25), channel_id=1, source_target_pairs={{0,3},{1,2},{2,1},{3,0},{4,7},{5,6},{6,5},{7,4},{8,11},{9,10},{10,... | collective-permute-start | bytes 147464 | tf_op jit(solution)/shard_map/ppermute | solution.py:276
  17.8 0.0 collective-permute-start.4
  17.9 3.1 %collective-permute-done.5 = f32[96,128]{1,0:T(8,128)S(1)} collective-permute-done((f32[96,128]{1,0:T(8,128)S(1)}, f32[96,128]{1,0:T(8,128)S(1)}, u32[]{:S(2)}, u32[]{:S(2)}) %collective-permute-start.5) | collective-permute-done | bytes 49184 | tf_op jit(solution)/shard_map/ppermute | solution.py:276
  21.0 1.1 %collective-permute-done.6 = f32[96,128]{1,0:T(8,128)S(1)} collective-permute-done((f32[96,128]{1,0:T(8,128)S(1)}, f32[96,128]{1,0:T(8,128)S(1)}, u32[]{:S(2)}, u32[]{:S(2)}) %collective-permute-start.6) | collective-permute-done | bytes 49184 | tf_op jit(solution)/shard_map/ppermute | solution.py:276
  22.0 0.4 collective-permute-done.4
  22.5 1.6 %collective-permute-start.8 = (f32[96,128]{1,0:T(8,128)S(1)}, f32[96,128]{1,0:T(8,128)S(1)}, u32[]{:S(2)}, u32[]{:S(2)}) collective-permute-start(f32[96,128]{1,0:T(8,128)S(1)} %add_add_fusion.1), channel_id=1, source_target_pairs={{0,16},{4,20},{8,24},{12,28},{16,0},{20,4},{24,8},{28,12},{1,17},{... | collective-permute-start | bytes 147464 | tf_op jit(solution)/shard_map/ppermute | solution.py:276
  24.1 1.4 %collective-permute-start.9 = (f32[96,128]{1,0:T(8,128)S(1)}, f32[96,128]{1,0:T(8,128)S(1)}, u32[]{:S(2)}, u32[]{:S(2)}) collective-permute-start(f32[96,128]{1,0:T(8,128)S(1)} %add_add_fusion.1), channel_id=1, source_target_pairs={{0,24},{4,28},{8,16},{12,20},{16,8},{20,12},{24,0},{28,4},{1,25},{... | collective-permute-start | bytes 147464 | tf_op jit(solution)/shard_map/ppermute | solution.py:276
  25.5 0.5 %collective-permute-start.7 = (f32[96,128]{1,0:T(8,128)S(1)}, f32[96,128]{1,0:T(8,128)S(1)}, u32[]{:S(2)}, u32[]{:S(2)}) collective-permute-start(f32[96,128]{1,0:T(8,128)S(1)} %add_add_fusion.1), channel_id=1, source_target_pairs={{0,8},{4,12},{8,0},{12,4},{16,24},{20,28},{24,16},{28,20},{1,9},{5... | collective-permute-start | bytes 147464 | tf_op jit(solution)/shard_map/ppermute | solution.py:276
  26.0 0.0 copy-start
  26.0 0.0 copy-start.1
  26.0 0.4 collective-permute-start.10
  26.4 2.5 %collective-permute-start.12 = (f32[32,1536]{1,0:T(8,128)S(1)}, f32[32,1536]{1,0:T(8,128)S(1)}, u32[]{:S(2)}, u32[]{:S(2)}) collective-permute-start(f32[32,1536]{1,0:T(8,128)S(1)} %get-tuple-element.48), channel_id=1, source_target_pairs={{0,3},{1,2},{2,1},{3,0},{4,7},{5,6},{6,5},{7,4},{8,11},{9,10},{10,... | collective-permute-start | bytes 589832 | tf_op jit(solution)/shard_map/ppermute | solution.py:276
  28.9 0.0 collective-permute-done.8
  28.9 0.6 %collective-permute-start.11 = (f32[32,1536]{1,0:T(8,128)S(1)}, f32[32,1536]{1,0:T(8,128)S(1)}, u32[]{:S(2)}, u32[]{:S(2)}) collective-permute-start(f32[32,1536]{1,0:T(8,128)S(1)} %get-tuple-element.47), channel_id=1, source_target_pairs={{0,2},{1,3},{2,0},{3,1},{4,6},{5,7},{6,4},{7,5},{8,10},{9,11},{10,... | collective-permute-start | bytes 589832 | tf_op jit(solution)/shard_map/ppermute | solution.py:276
  29.5 0.0 collective-permute-done.9
  29.5 0.1 collective-permute-done.7
  29.6 0.0 copy-done
  29.6 0.0 copy-done.1
  29.6 18.3 %all_rounds.1 = (f32[128,32]{1,0:T(8,128)S(1)}, f32[1,32]{1,0:T(1,128)}) custom-call(f32[96,128]{1,0:T(8,128)S(1)} %add_add_fusion.gram_ref, s32[16,8,128]{2,1,0:T(8,128)S(1)} %copy-done, f32[16,8,128]{2,1,0:T(8,128)S(1)} %copy-done.1, s32[1]{0:T(128)} %bitcast.8.place_ref), custom_call_target="tpu_custom_call" | custom-call | tf_op jit(solution)/shard_map/all_rounds/pallas_call | solution.py:257
  47.9 0.0 collective-permute-done.10
  47.9 0.0 collective-permute-done.12
  47.9 0.0 collective-permute-done.11
  47.9 0.4 convolution_multiply_fusion
  48.4 0.8 %fusion.13 = f32[32,2048]{1,0:T(8,128)} fusion(s32[]{:T(128)S(6)} %select_n.52, f32[32,2048]{1,0:T(8,128)S(1)} %convolution_multiply_fusion), kind=kLoop, calls=%fused_computation.16 | loop fusion | flops 65536 | bytes 524292 | tf_op jit(solution)/shard_map/concatenate | solution.py:300
  (11 shorter events, 0.2 us)
Async XLA Ops:
  0.7 10.0 %copy-start.2 = (f32[32,2048]{1,0:T(8,128)S(1)}, f32[32,2048]{1,0:T(8,128)}, u32[]{:S(2)}) copy-start(f32[32,2048]{1,0:T(8,128)} %param.2) | copy-start | bytes 786436
  1.7 9.1 %collective-permute-start.2 = (f32[32,512]{1,0:T(8,128)S(1)}, f32[32,512]{1,0:T(8,128)S(1)}, u32[]{:S(2)}, u32[]{:S(2)}) collective-permute-start(f32[32,512]{1,0:T(8,128)S(1)} %get-tuple-element.59), channel_id=1, source_target_pairs={{0,3},{1,2},{2,1},{3,0},{4,7},{5,6},{6,5},{7,4},{8,11},{9,10},{10,... | collective-permute-start | bytes 196616 | tf_op jit(solution)/shard_map/ppermute | solution.py:276
  6.8 5.6 %collective-permute-start.1 = (f32[32,512]{1,0:T(8,128)S(1)}, f32[32,512]{1,0:T(8,128)S(1)}, u32[]{:S(2)}, u32[]{:S(2)}) collective-permute-start(f32[32,512]{1,0:T(8,128)S(1)} %get-tuple-element.60), channel_id=1, source_target_pairs={{0,2},{1,3},{2,0},{3,1},{4,6},{5,7},{6,4},{7,5},{8,10},{9,11},{10,... | collective-permute-start | bytes 196616 | tf_op jit(solution)/shard_map/ppermute | solution.py:276
  6.8 5.6 %collective-permute-start = (f32[32,512]{1,0:T(8,128)S(1)}, f32[32,512]{1,0:T(8,128)S(1)}, u32[]{:S(2)}, u32[]{:S(2)}) collective-permute-start(f32[32,512]{1,0:T(8,128)S(1)} %get-tuple-element.58), channel_id=1, source_target_pairs={{0,1},{1,0},{2,3},{3,2},{4,5},{5,4},{6,7},{7,6},{8,9},{9,8},{10,11... | collective-permute-start | bytes 196616 | tf_op jit(solution)/shard_map/ppermute | solution.py:276
  7.4 0.7 %copy-start.3 = (s32[31,32]{1,0:T(8,128)S(1)}, s32[31,32]{1,0:T(8,128)}, u32[]{:S(2)}) copy-start(s32[31,32]{1,0:T(8,128)} %param.3) | copy-start | bytes 11908
  13.1 1.2 %collective-permute-start.3 = (f32[96,128]{1,0:T(8,128)S(1)}, f32[96,128]{1,0:T(8,128)S(1)}, u32[]{:S(2)}, u32[]{:S(2)}) collective-permute-start(f32[96,128]{1,0:T(8,128)S(1)} %maximum_maximum_fusion), channel_id=1, source_target_pairs={{0,4},{4,0},{8,12},{12,8},{16,20},{20,16},{24,28},{28,24},{1,5},{5... | collective-permute-start | bytes 147464 | tf_op jit(solution)/shard_map/ppermute | solution.py:276
  14.4 6.6 %collective-permute-start.5 = (f32[96,128]{1,0:T(8,128)S(1)}, f32[96,128]{1,0:T(8,128)S(1)}, u32[]{:S(2)}, u32[]{:S(2)}) collective-permute-start(f32[96,128]{1,0:T(8,128)S(1)} %fusion.25), channel_id=1, source_target_pairs={{0,2},{1,3},{2,0},{3,1},{4,6},{5,7},{6,4},{7,5},{8,10},{9,11},{10,... | collective-permute-start | bytes 147464 | tf_op jit(solution)/shard_map/ppermute | solution.py:276
  16.0 6.0 %collective-permute-start.6 = (f32[96,128]{1,0:T(8,128)S(1)}, f32[96,128]{1,0:T(8,128)S(1)}, u32[]{:S(2)}, u32[]{:S(2)}) collective-permute-start(f32[96,128]{1,0:T(8,128)S(1)} %fusion.25), channel_id=1, source_target_pairs={{0,3},{1,2},{2,1},{3,0},{4,7},{5,6},{6,5},{7,4},{8,11},{9,10},{10,... | collective-permute-start | bytes 147464 | tf_op jit(solution)/shard_map/ppermute | solution.py:276
  17.8 4.6 %collective-permute-start.4 = (f32[96,128]{1,0:T(8,128)S(1)}, f32[96,128]{1,0:T(8,128)S(1)}, u32[]{:S(2)}, u32[]{:S(2)}) collective-permute-start(f32[96,128]{1,0:T(8,128)S(1)} %fusion.25), channel_id=1, source_target_pairs={{0,1},{1,0},{2,3},{3,2},{4,5},{5,4},{6,7},{7,6},{8,9},{9,8},{10,11... | collective-permute-start | bytes 147464 | tf_op jit(solution)/shard_map/ppermute | solution.py:276
  22.5 6.4 %collective-permute-start.8 = (f32[96,128]{1,0:T(8,128)S(1)}, f32[96,128]{1,0:T(8,128)S(1)}, u32[]{:S(2)}, u32[]{:S(2)}) collective-permute-start(f32[96,128]{1,0:T(8,128)S(1)} %add_add_fusion.1), channel_id=1, source_target_pairs={{0,16},{4,20},{8,24},{12,28},{16,0},{20,4},{24,8},{28,12},{1,17},{... | collective-permute-start | bytes 147464 | tf_op jit(solution)/shard_map/ppermute | solution.py:276
  24.1 5.5 %collective-permute-start.9 = (f32[96,128]{1,0:T(8,128)S(1)}, f32[96,128]{1,0:T(8,128)S(1)}, u32[]{:S(2)}, u32[]{:S(2)}) collective-permute-start(f32[96,128]{1,0:T(8,128)S(1)} %add_add_fusion.1), channel_id=1, source_target_pairs={{0,24},{4,28},{8,16},{12,20},{16,8},{20,12},{24,0},{28,4},{1,25},{... | collective-permute-start | bytes 147464 | tf_op jit(solution)/shard_map/ppermute | solution.py:276
  25.5 4.1 %collective-permute-start.7 = (f32[96,128]{1,0:T(8,128)S(1)}, f32[96,128]{1,0:T(8,128)S(1)}, u32[]{:S(2)}, u32[]{:S(2)}) collective-permute-start(f32[96,128]{1,0:T(8,128)S(1)} %add_add_fusion.1), channel_id=1, source_target_pairs={{0,8},{4,12},{8,0},{12,4},{16,24},{20,28},{24,16},{28,20},{1,9},{5... | collective-permute-start | bytes 147464 | tf_op jit(solution)/shard_map/ppermute | solution.py:276
  26.0 3.6 %copy-start = (s32[16,8,128]{2,1,0:T(8,128)S(1)}, s32[16,8,128]{2,1,0:T(8,128)}, u32[]{:S(2)}) copy-start(s32[16,8,128]{2,1,0:T(8,128)} %get-tuple-element.43.index_ref) | copy-start | bytes 196612
  26.0 3.6 %copy-start.1 = (f32[16,8,128]{2,1,0:T(8,128)S(1)}, f32[16,8,128]{2,1,0:T(8,128)}, u32[]{:S(2)}) copy-start(f32[16,8,128]{2,1,0:T(8,128)} %get-tuple-element.44.sign_ref) | copy-start | bytes 196612
  26.0 21.9 %collective-permute-start.10 = (f32[32,1536]{1,0:T(8,128)S(1)}, f32[32,1536]{1,0:T(8,128)S(1)}, u32[]{:S(2)}, u32[]{:S(2)}) collective-permute-start(f32[32,1536]{1,0:T(8,128)S(1)} %get-tuple-element.39), channel_id=1, source_target_pairs={{0,1},{1,0},{2,3},{3,2},{4,5},{5,4},{6,7},{7,6},{8,9},{9,8},{10,11... | collective-permute-start | bytes 589832 | tf_op jit(solution)/shard_map/ppermute | solution.py:276
  26.4 21.5 %collective-permute-start.12 = (f32[32,1536]{1,0:T(8,128)S(1)}, f32[32,1536]{1,0:T(8,128)S(1)}, u32[]{:S(2)}, u32[]{:S(2)}) collective-permute-start(f32[32,1536]{1,0:T(8,128)S(1)} %get-tuple-element.48), channel_id=1, source_target_pairs={{0,3},{1,2},{2,1},{3,0},{4,7},{5,6},{6,5},{7,4},{8,11},{9,10},{10,... | collective-permute-start | bytes 589832 | tf_op jit(solution)/shard_map/ppermute | solution.py:276
  28.9 19.0 %collective-permute-start.11 = (f32[32,1536]{1,0:T(8,128)S(1)}, f32[32,1536]{1,0:T(8,128)S(1)}, u32[]{:S(2)}, u32[]{:S(2)}) collective-permute-start(f32[32,1536]{1,0:T(8,128)S(1)} %get-tuple-element.47), channel_id=1, source_target_pairs={{0,2},{1,3},{2,0},{3,1},{4,6},{5,7},{6,4},{7,5},{8,10},{9,11},{10,... | collective-permute-start | bytes 589832 | tf_op jit(solution)/shard_map/ppermute | solution.py:276
